TPU v7x, 128 devices: a whole 4x4x4 slice. The times are simulated.
128 devices in a mesh: row: 8 (over z, core), leaf: 16 (over y, x).
Axes of the slice: x: 4, y: 4, z: 4, core: 2. Of those that a mesh axis runs over, the one named last changes fastest.
Arguments:
- leaf_update: float32 [16384, 256], P(('leaf', 'row')), may hold values from -6 to 6
- rhs: float32 [3, 16384, 256], P(None, ('leaf', 'row')), may hold values from -6 to 6
- inv_top: bfloat16 [2, 16384, 16, 8, 128], P(None, 'leaf', None, 'row'), may hold values from -0.03125 to 0.03125
- inv_mid: bfloat16 [2, 16384, 8, 8, 128], P(None, 'leaf', None, 'row'), may hold values from -0.046875 to 0.046875
- inv_low: bfloat16 [2, 16384, 4, 8, 128], P(None, 'leaf', None, 'row'), may hold values from -0.0625 to 0.0625
- couple_mid: bfloat16 [2, 16384, 8, 8, 128], P(None, 'leaf', None, 'row'), may hold values from -0.046875 to 0.046875
- couple_low: bfloat16 [2, 16384, 4, 8, 128], P(None, 'leaf', None, 'row'), may hold values from -0.0625 to 0.0625
- block_map: int32 [3, 128], P(None, ('leaf', 'row')), may hold values from 0 to 127, as said below
Outputs:
- solution: float32 [3, 16384, 256], P(None, ('leaf', 'row'))
- leaf_solution: float32 [16384, 256], P(('leaf', 'row'))
Inputs may be any that keep to these rules, and one draw needn't show every extreme that they name: Device d of the group of a front holds rows d * 128 to (d + 1) * 128 - 1 of the front's separator part and the same rows of its update part, with d = p * 8 + r for group position p (leaf index modulo the group size) and row index r. block_map[k] is one to one within each parent, and a block held at row index r and group position p of a child lands on a parent block held at row index r and group position p or p + (group size of the parent) / 2. At level 0 every parent block receives one block.
All inputs are finite; a program needn't handle non-finite values.
Results may differ from a plain program's by a relative error of at most 0.012.
Values may be sent and summed in bfloat16 or wider, within the bound.
No kernel may reach another device: no remote copies, remote signals or barrier semaphores. Data moves between devices by JAX's collectives and lax.ppermute only.
A program may use at most 128 MiB of HBM per device.

v0:
```python
import functools

import jax
import jax.numpy as jnp
from jax import lax
from jax.experimental import pallas as pl
from jax.experimental.pallas import tpu as pltpu
from jax.sharding import PartitionSpec as P

BF = jnp.bfloat16
F32 = jnp.float32
B = 128
C = 256
STEPS = (1, 3, 2)
X, Y, Z, CORE, ROW, T0, T1, T2 = range(8)
SMALL = 8 << 20


def swap(value, axis, mask):
    count = lax.axis_size(axis)
    return lax.ppermute(value, axis, [(i, i ^ mask) for i in range(count)])


def small(body, outs, scal, *ins):
    return pl.pallas_call(
        body,
        out_shape=[jax.ShapeDtypeStruct(*o) for o in outs],
        in_specs=[pl.BlockSpec(memory_space=pltpu.SMEM)]
        + [pl.BlockSpec(memory_space=pltpu.VMEM)] * len(ins),
        out_specs=[pl.BlockSpec(memory_space=pltpu.VMEM)] * len(outs),
        compiler_params=pltpu.CompilerParams(vmem_limit_bytes=SMALL),
        cost_estimate=pl.CostEstimate(flops=1 << 18, bytes_accessed=1 << 19, transcendentals=0),
    )(scal, *ins)


def relay_body(groups, real_ref, imag_ref, out_ref):
    span = C // groups
    shift = span.bit_length() - 1
    target = lax.broadcasted_iota(jnp.int32, (C, C), 0)
    source = lax.broadcasted_iota(jnp.int32, (C, C), 1)
    place = (source == (target & span - 1) * groups + (target >> shift)).astype(BF)

    @pl.loop(0, B * groups // C)
    def _(chunk):
        rows = pl.ds(pl.multiple_of(chunk * C, C), C)
        both = jnp.concatenate([real_ref[rows, :], imag_ref[rows, :]], axis=1)
        moved = jnp.dot(place, both, preferred_element_type=F32).astype(BF)
        for p in range(groups):
            out_ref[pl.ds(pl.multiple_of(chunk * span, span), span), p * C : (p + 1) * C] = moved[
                p * span : (p + 1) * span
            ]


def relay(weights):
    _, rows, groups, _, width = weights.shape
    flat = weights.reshape(2 * rows * groups, width)
    tiles = rows // B
    return pl.pallas_call(
        functools.partial(relay_body, groups),
        grid=(tiles,),
        out_shape=jax.ShapeDtypeStruct((rows, groups * C), BF),
        in_specs=[
            pl.BlockSpec((B * groups, B), lambda t: (t, 0)),
            pl.BlockSpec((B * groups, B), lambda t: (t + tiles, 0)),
        ],
        out_specs=pl.BlockSpec((B, groups * C), lambda t: (t, 0)),
        compiler_params=pltpu.CompilerParams(vmem_limit_bytes=2 * SMALL),
        cost_estimate=pl.CostEstimate(
            flops=4 * rows * groups * C * B, bytes_accessed=8 * rows * groups * B, transcendentals=0
        ),
    )(flat, flat)


def call(body, outs, scal, ins, scratch, flops):
    limit = 2 * ins[0].size + (12 << 20)
    return pl.pallas_call(
        body,
        out_shape=[jax.ShapeDtypeStruct(*o) for o in outs],
        in_specs=[pl.BlockSpec(memory_space=pltpu.SMEM)]
        + [pl.BlockSpec(memory_space=pltpu.VMEM)] * len(ins),
        out_specs=[pl.BlockSpec(memory_space=pltpu.VMEM)] * len(outs),
        scratch_shapes=scratch,
        compiler_params=pltpu.CompilerParams(vmem_limit_bytes=limit),
        cost_estimate=pl.CostEstimate(flops=flops, bytes_accessed=1 << 20, transcendentals=0),
    )(scal, *ins)


def forward(weights, scal, ins, gather, extras=()):
    rows, depth = weights.shape
    count = len(ins)

    def body(s, w_ref, *refs):
        in_refs, out_refs, vec = refs[:count], refs[count:-1], refs[-1]
        for index, block in gather(s, in_refs, out_refs[2:]):
            start = pl.multiple_of(index * C, C)
            block = block.astype(F32)
            vec[pl.ds(start, B), :] = block.astype(BF)
            vec[pl.ds(start + B, B), :] = jnp.concatenate(
                [-block[:, B:], block[:, :B]], axis=1
            ).astype(BF)
        swapped = s[CORE] == 1

        @pl.loop(0, 4)
        def _(k):
            start = pl.multiple_of((s[Z] ^ k) * C, C)
            prod = jnp.dot(w_ref[pl.ds(start, C), :], vec[...], preferred_element_type=F32)
            upper, lower = prod[:B], prod[B:]
            out_refs[0][k] = jnp.where(swapped, lower, upper)
            out_refs[1][k] = jnp.where(swapped, upper, lower).astype(BF)

    outs = [((4, B, C), F32), ((4, B, C), BF)] + list(extras)
    return call(
        body, outs, scal, [weights, *ins], [pltpu.VMEM((depth, C), BF)], 2 * rows * depth * C
    )


def transposed(weights, scal, pieces, paired=None, only=None):
    rows, depth = weights.shape
    tiles = depth // (4 * C)
    ins = list(pieces.values()) + ([] if paired is None else [paired])
    keys = list(pieces)
    count = len(ins)
    mask = tiles - 1
    used = count + (4 if only is None else 1)

    def body(s, w_ref, *refs):
        in_refs, out_refs, scratch = refs[:count], refs[count:used], refs[used:]
        vec = scratch[0]
        for (zz, j), ref in zip(keys, in_refs):
            slot = 2 * (s[Z] ^ zz) + (s[CORE] ^ j)
            vec[:, pl.ds(pl.multiple_of(slot * B, B), B)] = ref[...]

        def block(position):
            part = jnp.dot(
                vec[...],
                w_ref[:, pl.ds(pl.multiple_of(position * C, C), C)],
                preferred_element_type=F32,
            )
            return jnp.concatenate(
                [part[:B, :B] - part[B:, B:], part[B:, :B] + part[:B, B:]], axis=0
            )

        if only is not None:

            @pl.loop(0, 4)
            def _(plane):
                j = (plane & 1) * 2 + (plane >> 1)
                value = block((s[Y] ^ j) * 4 + (s[X] ^ only))
                out_refs[0][plane] = value.astype(out_refs[0].dtype)

            return
        acc = scratch[1]

        @pl.loop(0, 4 * tiles)
        def _(step):
            k, j = step & 3, step >> 2
            acc[k, j] = block(((s[Y] & mask) ^ j) * 4 + (s[X] ^ k))

        for k in range(4):
            kind = out_refs[k].dtype
            out_refs[k][:tiles] = acc[k].astype(kind)
            if paired is not None:
                out_refs[k][1] = acc[k ^ 2, 0].astype(kind)
        if paired is not None:
            out_refs[2][2] = in_refs[-1][...]

    scratch_shapes = [pltpu.VMEM((C, rows), BF)]
    if only is not None:
        outs = [((4, C, B), BF if only else F32)]
    else:
        scratch_shapes.append(pltpu.VMEM((4, tiles, C, B), F32))
        planes = [1, 1, 1, 1] if paired is None else [2, 2, 3, 2]
        outs = [((tiles * planes[k], C, B), BF if k else F32) for k in range(4)]
    return call(
        body, outs, scal, [weights, *ins], scratch_shapes, 2 * rows * depth * C
    )


def same(goal, slot):
    return (goal == slot.astype(F32)).astype(F32)


def shards(leaf_update, rhs, inv_top, inv_mid, inv_low, couple_mid, couple_low, block_map):
    leaf = lax.axis_index("leaf")
    row = lax.axis_index("row")
    scal = jnp.concatenate(
        [jnp.stack([leaf & 3, leaf >> 2, row >> 1, row & 1, row]).astype(jnp.int32), block_map[:, 0]]
    )

    def reduce_row(own, other):
        other = swap(other, "row", 1)
        parts = {k: own[k] + other[k].astype(F32) for k in range(4)}
        total = parts[0]
        for k in STEPS:
            total = total + swap(parts[k].astype(BF), "row", 2 * k).astype(F32)
        return total

    def gather_row(own):
        pieces = {(0, 0): own}
        for k in STEPS:
            pieces[(k, 0)] = swap(own, "row", 2 * k)
        for k in (0,) + STEPS:
            pieces[(k, 1)] = swap(pieces[(k, 0)], "row", 1)
        return pieces

    def gather_x(value):
        return [value] + [swap(value, "leaf", k) for k in (1, 2, 3)]

    def send(map_ref, leaf_ref, rhs_ref, low_ref, leaf_vmem, rhs_vmem, sems):
        first = pltpu.make_async_copy(leaf_ref, leaf_vmem, sems.at[0])
        second = pltpu.make_async_copy(rhs_ref.at[2], rhs_vmem, sems.at[1])
        first.start()
        second.start()
        low_ref[2 * B :] = jnp.full((16, C), map_ref[2, 0].astype(F32), F32).astype(BF)
        first.wait()
        low_ref[:B] = leaf_vmem[...].astype(BF)
        second.wait()
        low_ref[B : 2 * B] = rhs_vmem[...].astype(BF)

    low = pl.pallas_call(
        send,
        out_shape=jax.ShapeDtypeStruct((2 * B + 16, C), BF),
        in_specs=[
            pl.BlockSpec(memory_space=pltpu.SMEM),
            pl.BlockSpec(memory_space=pl.ANY),
            pl.BlockSpec(memory_space=pl.ANY),
        ],
        out_specs=pl.BlockSpec(memory_space=pltpu.VMEM),
        scratch_shapes=[
            pltpu.VMEM((B, C), F32),
            pltpu.VMEM((B, C), F32),
            pltpu.SemaphoreType.DMA((2,)),
        ],
        compiler_params=pltpu.CompilerParams(vmem_limit_bytes=SMALL),
    )(block_map, leaf_update, rhs)
    got = gather_x(low)
    w_low, b_low, w_mid, b_mid, w_top = [
        relay(w) for w in (inv_low, couple_low, inv_mid, couple_mid, inv_top)
    ]

    def gather_low(s, refs, extra):
        goal = [r[2 * B : 2 * B + 16, :].astype(F32)[:1] for r in refs[:4]]
        child = [r[:B, :].astype(F32) for r in refs[:4]]
        slot = (s[X] + 4) * 8 + s[ROW]
        update = same(goal[0], slot) * child[0] + same(goal[2], slot) * child[2]
        extra[0][...] = update
        message = extra[1]
        rhs_ref = refs[4]
        message[:B] = rhs_ref[1].astype(BF)
        message[B : 2 * B] = rhs_ref[0].astype(BF)
        message[2 * B : 2 * B + 16] = jnp.full((16, C), s[T1].astype(F32), F32).astype(BF)
        message[2 * B + 16 : 2 * B + 32] = jnp.full((16, C), s[T0].astype(F32), F32).astype(BF)
        extra[2][:B] = rhs_ref[0].astype(BF)
        extra[2][B:] = jnp.full((16, C), s[T0].astype(F32), F32).astype(BF)
        for k in range(4):
            slot = (s[X] ^ k) * 8 + s[ROW]
            yield s[X] ^ k, (
                refs[k][B : 2 * B, :].astype(F32)
                + same(goal[k], slot) * child[k]
                + same(goal[k ^ 2], slot) * child[k ^ 2]
            )

    own, others, update, to_y1, to_y3 = forward(
        w_low,
        scal,
        [*got, rhs],
        gather_low,
        extras=[((B, C), F32), ((2 * B + 32, C), BF), ((B + 16, C), BF)],
    )
    from_y1 = swap(to_y1, "leaf", 4)
    from_y3 = swap(to_y3, "leaf", 12)
    from_y2 = swap(to_y3, "leaf", 8)
    y_low = reduce_row(own, others)

    def gather_plain(s, refs, extra):
        for k in range(4):
            yield s[X] ^ k, refs[k][...]

    own, others = forward(b_low, scal, gather_x(y_low.astype(BF)), gather_plain)
    children = update - reduce_row(own, others)

    theirs = swap(children.astype(BF), "leaf", 4)

    def extend_mid(s, own_ref, other_ref, rhs_ref, y1_ref, pair_ref, up_ref):
        position = (s[Y] & 1) * 4 + s[X]
        goal_own = jnp.full((1, C), s[T1].astype(F32), F32)
        goal_other = y1_ref[2 * B : 2 * B + 16, :].astype(F32)[:1]

        def landed(slot):
            return same(goal_own, slot) * own_ref[...] + same(goal_other, slot) * other_ref[
                ...
            ].astype(F32)

        slot = position * 8 + s[ROW]
        pair_ref[0] = (rhs_ref[1] + landed(slot)).astype(BF)
        up_ref[...] = landed(slot + 64)
        slot = (position ^ 4) * 8 + s[ROW]
        pair_ref[1] = (y1_ref[:B, :].astype(F32) + landed(slot)).astype(BF)

    pair, update = small(
        extend_mid, [((2, B, C), BF), ((B, C), F32)], scal, children, theirs, rhs, from_y1
    )

    def gather_mid(s, refs, extra):
        for k in range(4):
            for j in range(2):
                yield ((s[Y] & 1) ^ j) * 4 + (s[X] ^ k), refs[k][j]

    own, others = forward(w_mid, scal, gather_x(pair), gather_mid)
    y_mid = reduce_row(own, others)
    half = y_mid.astype(BF)

    def join(s, a_ref, b_ref, out_ref):
        out_ref[0] = a_ref[...]
        out_ref[1] = b_ref[...]

    (pair,) = small(join, [((2, B, C), BF)], scal, half, swap(half, "leaf", 4))
    own, others = forward(b_mid, scal, gather_x(pair), gather_mid)
    children = update - reduce_row(own, others)
    half = children.astype(BF)

    def flip(s, low_ref, mid_ref, low_out, mid_out):
        low_out[...] = low_ref[...].T
        mid_out[...] = mid_ref[...].T

    turned_low, turned_mid = small(flip, [((C, B), F32)] * 2, scal, y_low, y_mid)

    moved = [swap(half, "leaf", 4 * k) for k in STEPS]

    def extend_top(s, own_ref, m1, m3, m2, rhs_ref, y1_ref, y3_ref, y2_ref, out_ref):
        child = [own_ref[...], m1[...].astype(F32), m2[...].astype(F32), m3[...].astype(F32)]
        base = [rhs_ref[0], y1_ref[B : 2 * B, :], y2_ref[:B, :], y3_ref[:B, :]]
        goal = [
            jnp.full((1, C), s[T0].astype(F32), F32),
            y1_ref[2 * B + 16 : 2 * B + 32, :].astype(F32)[:1],
            y2_ref[B : B + 16, :].astype(F32)[:1],
            y3_ref[B : B + 16, :].astype(F32)[:1],
        ]
        for k in range(4):
            slot = ((s[Y] ^ k) * 4 + s[X]) * 8 + s[ROW]
            out_ref[k] = (
                base[k].astype(F32)
                + same(goal[k], slot) * child[k]
                + same(goal[k ^ 2], slot) * child[k ^ 2]
            ).astype(BF)

    (column,) = small(
        extend_top, [((4, B, C), BF)], scal, children, *moved, rhs, from_y1, from_y3, from_y2
    )

    def gather_top(s, refs, extra):
        for k in range(4):
            for j in range(4):
                yield (s[Y] ^ j) * 4 + (s[X] ^ k), refs[k][j]

    own, others = forward(w_top, scal, gather_x(column), gather_top)

    def turn(s, total_ref, out_ref):
        out_ref[...] = total_ref[...].T.astype(BF)

    (half,) = small(turn, [((C, B), BF)], scal, reduce_row(own, others))
    pieces = gather_row(half)
    got = [swap(transposed(w_top, scal, pieces, only=k)[0], "leaf", k) for k in (2, 1, 3)]
    (own,) = transposed(w_top, scal, pieces, only=0)

    def total(planes):
        return own[planes] + sum(g[planes].astype(F32) for g in got)

    pair, cross = total(slice(0, 2)), total(slice(2, 4)).astype(BF)
    from_1, from_3 = swap(cross, "leaf", 4).astype(F32), swap(cross, "leaf", 12).astype(F32)
    from_2 = swap(pair.astype(BF), "leaf", 8).astype(F32)
    x_top = pair[0] + from_2[1] + from_1[0] + from_3[1]
    x_other = pair[1] + from_2[0] + from_1[1] + from_3[0]
    down_mid = jnp.where(block_map[0, 0] == leaf * 8 + row, x_top, x_other)
    half = down_mid.astype(BF)

    down_half = half
    parts = transposed(b_mid, scal, gather_row(half))
    got = [swap(parts[k], "leaf", k) for k in STEPS]
    full, cross = [parts[0][j] + sum(g[j].astype(F32) for g in got) for j in range(2)]
    coupled = full + swap(cross.astype(BF), "leaf", 4).astype(F32)
    half = (turned_mid - coupled).astype(BF)
    parts = transposed(w_mid, scal, gather_row(half))
    got = [swap(parts[k], "leaf", k) for k in STEPS]

    def pair_mid(s, own_ref, a, b, c, down_ref, full_ref, out_ref):
        for j in range(2):
            total = own_ref[j] + a[j].astype(F32) + b[j].astype(F32) + c[j].astype(F32)
            full_ref[j] = total
            out_ref[1 - j] = total.astype(BF)
        out_ref[2] = down_ref[...]

    full, sent = small(
        pair_mid, [((2, C, B), F32), ((3, C, B), BF)], scal, parts[0], *got, down_half
    )

    def choose(s, target, base, blocks):
        down = None
        goal = jnp.full((1, B), target.astype(F32), F32)
        for slot, block in zip(base, blocks):
            term = block * same(goal, slot)
            down = term if down is None else down + term
        return down

    def end_mid(s, full_ref, got_ref, down_ref, x_ref, out_ref, half_ref):
        own = full_ref[0] + got_ref[0].astype(F32)
        other = full_ref[1] + got_ref[1].astype(F32)
        x_ref[...] = own
        position = (s[Y] & 1) * 4 + s[X]
        slot, far = position * 8 + s[ROW], (position ^ 4) * 8 + s[ROW]
        down = choose(
            s,
            s[T1],
            (slot, slot + 64, far, far + 64),
            (own, down_ref[...], other, got_ref[2].astype(F32)),
        )
        out_ref[...] = down
        half_ref[...] = down.astype(BF)

    x_mid, down_low, half = small(
        end_mid,
        [((C, B), F32), ((C, B), F32), ((C, B), BF)],
        scal,
        full,
        swap(sent, "leaf", 4),
        down_mid,
    )

    down_half = half
    parts = transposed(b_low, scal, gather_row(half))
    got = [swap(parts[k], "leaf", k) for k in STEPS]

    coupled = parts[0][0] + sum(g[0].astype(F32) for g in got)
    half = (turned_low - coupled).astype(BF)
    parts = transposed(w_low, scal, gather_row(half), down_half)
    got = [swap(parts[k], "leaf", k) for k in STEPS]

    def end_low(s, own_ref, a, b, c, down_ref, top_ref, mid_ref, sol_ref, leaf_ref):
        own, other = [
            own_ref[j] + a[j].astype(F32) + b[j].astype(F32) + c[j].astype(F32) for j in range(2)
        ]
        sol_ref[0] = top_ref[...].T
        sol_ref[1] = mid_ref[...].T
        sol_ref[2] = own.T
        slot, far = s[X] * 8 + s[ROW], (s[X] ^ 2) * 8 + s[ROW]
        leaf_ref[...] = choose(
            s,
            s[T2],
            (slot, slot + 32, far, far + 32),
            (own, down_ref[...], other, c[2].astype(F32)),
        ).T

    solved, leaf_solution = small(
        end_low,
        [((3, B, C), F32), ((B, C), F32)],
        scal,
        parts[0],
        *got,
        down_low,
        x_top,
        x_mid,
    )
    return (solved, leaf_solution)


def solution(mesh):
    return jax.shard_map(
        shards,
        mesh=mesh,
        in_specs=(
            P(("leaf", "row"), None),
            P(None, ("leaf", "row"), None),
            P(None, "leaf", None, "row", None),
            P(None, "leaf", None, "row", None),
            P(None, "leaf", None, "row", None),
            P(None, "leaf", None, "row", None),
            P(None, "leaf", None, "row", None),
            P(None, ("leaf", "row")),
        ),
        out_specs=(P(None, ("leaf", "row"), None), P(("leaf", "row"), None)),
        check_vma=False,
    )
```

profile of v0, /device:TPU:0, one launch (start us, length us, event | category | flops | bytes accessed | tf_op | source)
XLA Modules:
  0.0 286.2 jit_solution(11373028914771912851)
XLA Ops:
  4.2 2.9 %collective-permute-start.2 = (bf16[272,256]{1,0:T(8,128)(2,1)S(1)}, bf16[272,256]{1,0:T(8,128)(2,1)S(1)}, u32[]{:S(2)}, u32[]{:S(2)}) collective-permute-start(bf16[272,256]{1,0:T(8,128)(2,1)S(1)} %shard_map.96.refs_0_), channel_id=1, source_target_pairs={{0,3},{1,2},{2,1},{3,0},{4,7},{5,6},{6,5},{7,4},{8,11},{9,10},{10,... | collective-permute-start | bytes 417800 | tf_op jit(solution)/shard_map/ppermute | solution.py:21
  10.7 3.5 %shard_map.95.w_ref = bf16[1024,1024]{1,0:T(8,128)(2,1)S(1)} custom-call(bf16[8192,128]{1,0:T(8,128)(2,1)S(1)} %bitcast.109, bf16[8192,128]{1,0:T(8,128)(2,1)S(1)} %bitcast.110), custom_call_target="tpu_custom_call" | custom-call | flops 536870912 | bytes 4194304 | tf_op jit(solution)/shard_map/pallas_call | solution.py:58
  15.3 2.0 shard_map.97
  18.9 2.0 collective-permute-start.4
  20.9 3.6 %collective-permute-start.6 = (bf16[128,256]{1,0:T(8,128)(2,1)S(1)}, bf16[128,256]{1,0:T(8,128)(2,1)S(1)}, u32[]{:S(2)}, u32[]{:S(2)}) collective-permute-start(bf16[128,256]{1,0:T(8,128)(2,1)S(1)} %get-tuple-element.105), channel_id=1, source_target_pairs={{0,64},{16,80},{32,96},{48,112},{64,0},{80,16},{96,32},{112,48},{1... | collective-permute-start | bytes 196616 | tf_op jit(solution)/shard_map/ppermute | solution.py:21
  24.5 3.5 %collective-permute-done.6 = bf16[128,256]{1,0:T(8,128)(2,1)S(1)} collective-permute-done((bf16[128,256]{1,0:T(8,128)(2,1)S(1)}, bf16[128,256]{1,0:T(8,128)(2,1)S(1)}, u32[]{:S(2)}, u32[]{:S(2)}) %collective-permute-start.6) | collective-permute-done | bytes 65568 | tf_op jit(solution)/shard_map/ppermute | solution.py:21
  28.0 2.0 collective-permute-done.5
  30.0 2.2 collective-permute-start.9
  34.2 3.5 %shard_map.99.w_ref = bf16[1024,1024]{1,0:T(8,128)(2,1)S(1)} custom-call(bf16[8192,128]{1,0:T(8,128)(2,1)S(1)} %bitcast.111, bf16[8192,128]{1,0:T(8,128)(2,1)S(1)} %bitcast.112), custom_call_target="tpu_custom_call" | custom-call | flops 536870912 | bytes 4194304 | tf_op jit(solution)/shard_map/pallas_call | solution.py:58
  38.0 1.8 shard_map.100
  43.3 2.9 %collective-permute-start.12 = (bf16[128,256]{1,0:T(8,128)(2,1)S(1)}, bf16[128,256]{1,0:T(8,128)(2,1)S(1)}, u32[]{:S(2)}, u32[]{:S(2)}) collective-permute-start(bf16[128,256]{1,0:T(8,128)(2,1)S(1)} %get-tuple-element.103), channel_id=1, source_target_pairs={{0,96},{16,112},{32,64},{48,80},{64,32},{80,48},{96,0},{112,16},{1... | collective-permute-start | bytes 196616 | tf_op jit(solution)/shard_map/ppermute | solution.py:21
  53.8 1.9 collective-permute-start.18
  58.0 6.6 %shard_map.98.w_ref = bf16[1024,2048]{1,0:T(8,128)(2,1)S(1)} custom-call(bf16[16384,128]{1,0:T(8,128)(2,1)S(1)} %bitcast.105, bf16[16384,128]{1,0:T(8,128)(2,1)S(1)} %bitcast.106), custom_call_target="tpu_custom_call" | custom-call | flops 1073741824 | bytes 8388608 | tf_op jit(solution)/shard_map/pallas_call | solution.py:58
  64.6 2.4 shard_map.102
  67.0 2.0 copy-done
  71.3 3.8 %collective-permute-start.22 = (bf16[128,256]{1,0:T(8,128)(2,1)S(1)}, bf16[128,256]{1,0:T(8,128)(2,1)S(1)}, u32[]{:S(2)}, u32[]{:S(2)}) collective-permute-start(bf16[128,256]{1,0:T(8,128)(2,1)S(1)} %get-tuple-element.99), channel_id=1, source_target_pairs={{0,64},{16,80},{32,96},{48,112},{64,0},{80,16},{96,32},{112,48},{1... | collective-permute-start | bytes 196616 | tf_op jit(solution)/shard_map/ppermute | solution.py:21
  75.4 3.2 %collective-permute-done.22 = bf16[128,256]{1,0:T(8,128)(2,1)S(1)} collective-permute-done((bf16[128,256]{1,0:T(8,128)(2,1)S(1)}, bf16[128,256]{1,0:T(8,128)(2,1)S(1)}, u32[]{:S(2)}, u32[]{:S(2)}) %collective-permute-start.22) | collective-permute-done | bytes 65568 | tf_op jit(solution)/shard_map/ppermute | solution.py:21
  78.6 2.0 collective-permute-done.21
  82.3 2.7 collective-permute-done.23.b_ref
  85.5 1.9 collective-permute-start.26
  89.7 6.6 %shard_map.104.w_ref = bf16[1024,2048]{1,0:T(8,128)(2,1)S(1)} custom-call(bf16[16384,128]{1,0:T(8,128)(2,1)S(1)} %bitcast.107, bf16[16384,128]{1,0:T(8,128)(2,1)S(1)} %bitcast.108), custom_call_target="tpu_custom_call" | custom-call | flops 1073741824 | bytes 8388608 | tf_op jit(solution)/shard_map/pallas_call | solution.py:58
  96.4 2.4 shard_map.107
  102.3 2.9 %collective-permute-start.29 = (bf16[128,256]{1,0:T(8,128)(2,1)S(1)}, bf16[128,256]{1,0:T(8,128)(2,1)S(1)}, u32[]{:S(2)}, u32[]{:S(2)}) collective-permute-start(bf16[128,256]{1,0:T(8,128)(2,1)S(1)} %get-tuple-element.97), channel_id=1, source_target_pairs={{0,96},{16,112},{32,64},{48,80},{64,32},{80,48},{96,0},{112,16},{1... | collective-permute-start | bytes 196616 | tf_op jit(solution)/shard_map/ppermute | solution.py:21
  105.2 3.2 %collective-permute-start.35 = (bf16[144,256]{1,0:T(8,128)(2,1)S(1)}, bf16[144,256]{1,0:T(8,128)(2,1)S(1)}, u32[]{:S(2)}, u32[]{:S(2)}) collective-permute-start(bf16[144,256]{1,0:T(8,128)(2,1)S(1)} %get-tuple-element.54), channel_id=1, source_target_pairs={{0,8},{1,9},{2,10},{3,11},{4,12},{5,13},{6,14},{7,15},{8,0},{9,1},... | collective-permute-start | bytes 221192 | tf_op jit(solution)/shard_map/ppermute | solution.py:21
  109.5 2.0 collective-permute-start.33
  117.7 1.9 collective-permute-start.38
  121.8 12.8 %shard_map.105.w_ref = bf16[1024,4096]{1,0:T(8,128)(2,1)S(1)} custom-call(bf16[32768,128]{1,0:T(8,128)(2,1)S(1)} %bitcast.103, bf16[32768,128]{1,0:T(8,128)(2,1)S(1)} %bitcast.104), custom_call_target="tpu_custom_call" | custom-call | flops 2147483648 | bytes 16777216 | tf_op jit(solution)/shard_map/pallas_call | solution.py:58
  134.7 3.6 %shard_map.109 = (f32[4,128,256]{2,1,0:T(8,128)S(1)}, bf16[4,128,256]{2,1,0:T(8,128)(2,1)S(1)}) custom-call(s32[8]{0:T(128)S(1)} %concatenate.3.s, bf16[1024,4096]{1,0:T(8,128)(2,1)S(1)} %shard_map.105.w_ref, bf16[4,128,256]{2,1,0:T(8,128)(2,1)S(1)} %shard_map.108.refs_0_, bf16[4,128,256]{2,1,0:T(8,128)(2,1)S(1)} %collective-permute-done.36.refs_1_, ...), custom_call_target="tpu_custom_call" | custom-call | flops 2147483648 | bytes 1048576 | tf_op jit(solution)/shard_map/pallas_call | solution.py:76
  140.4 3.9 %collective-permute-start.42 = (bf16[128,256]{1,0:T(8,128)(2,1)S(1)}, bf16[128,256]{1,0:T(8,128)(2,1)S(1)}, u32[]{:S(2)}, u32[]{:S(2)}) collective-permute-start(bf16[128,256]{1,0:T(8,128)(2,1)S(1)} %get-tuple-element.93), channel_id=1, source_target_pairs={{0,64},{16,80},{32,96},{48,112},{64,0},{80,16},{96,32},{112,48},{1... | collective-permute-start | bytes 196616 | tf_op jit(solution)/shard_map/ppermute | solution.py:21
  144.8 3.0 %collective-permute-done.42 = bf16[128,256]{1,0:T(8,128)(2,1)S(1)} collective-permute-done((bf16[128,256]{1,0:T(8,128)(2,1)S(1)}, bf16[128,256]{1,0:T(8,128)(2,1)S(1)}, u32[]{:S(2)}, u32[]{:S(2)}) %collective-permute-start.42) | collective-permute-done | bytes 65568 | tf_op jit(solution)/shard_map/ppermute | solution.py:21
  147.8 2.0 collective-permute-done.41
  154.0 2.3 collective-permute-done.45.refs_3_
  158.4 2.0 shard_map.112
  160.4 2.2 collective-permute-start.50
  162.5 2.0 shard_map.113
  165.2 2.0 shard_map.114
  168.6 2.0 shard_map.111
  171.1 4.2 %collective-permute-done.51 = bf16[4,256,128]{2,1,0:T(8,128)(2,1)S(1)} collective-permute-done((bf16[4,256,128]{2,1,0:T(8,128)(2,1)S(1)}, bf16[4,256,128]{2,1,0:T(8,128)(2,1)S(1)}, u32[]{:S(2)}, u32[]{:S(2)}) %collective-permute-start.51) | collective-permute-done | bytes 262176 | tf_op jit(solution)/shard_map/ppermute | solution.py:21
  180.3 4.1 %collective-permute-done.53 = bf16[2,256,128]{2,1,0:T(8,128)(2,1)S(1)} collective-permute-done((bf16[2,256,128]{2,1,0:T(8,128)(2,1)S(1)}, bf16[2,256,128]{2,1,0:T(8,128)(2,1)S(1)}, u32[]{:S(2)}, u32[]{:S(2)}) %collective-permute-start.53) | collective-permute-done | bytes 131104 | tf_op jit(solution)/shard_map/ppermute | solution.py:21
  187.1 2.3 collective-permute-start.57
  189.4 2.9 %collective-permute-done.58.refs_3_ = bf16[256,128]{1,0:T(8,128)(2,1)S(1)} collective-permute-done((bf16[256,128]{1,0:T(8,128)(2,1)S(1)}, bf16[256,128]{1,0:T(8,128)(2,1)S(1)}, u32[]{:S(2)}, u32[]{:S(2)}) %collective-permute-start.58) | collective-permute-done | bytes 65568 | tf_op jit(solution)/shard_map/ppermute | solution.py:21
  194.9 2.2 copy-done.3
  197.1 3.3 %shard_map.115 = (f32[2,256,128]{2,1,0:T(8,128)S(1)}, bf16[2,256,128]{2,1,0:T(8,128)(2,1)S(1)}, bf16[2,256,128]{2,1,0:T(8,128)(2,1)S(1)}, bf16[2,256,128]{2,1,0:T(8,128)(2,1)S(1)}) custom-call(s32[8]{0:T(128)S(1)} %concatenate.3.s, bf16[1024,2048]{1,0:T(8,128)(2,1)S(1)} %copy-done.3, bf16[256,128]{1,0:T(8,128)(2,1)S(1)} %get-tuple-element.78.refs_0_.down_ref, ...), custom_call_target="tpu_custom_call" | custom-call | flops 1073741824 | bytes 1048576 | tf_op jit(solution)/shard_map/pallas_call | solution.py:76
  201.0 2.2 collective-permute-start.64
  204.6 2.2 collective-permute-done.63
  206.8 3.4 %collective-permute-done.64 = bf16[2,256,128]{2,1,0:T(8,128)(2,1)S(1)} collective-permute-done((bf16[2,256,128]{2,1,0:T(8,128)(2,1)S(1)}, bf16[2,256,128]{2,1,0:T(8,128)(2,1)S(1)}, u32[]{:S(2)}, u32[]{:S(2)}) %collective-permute-start.64) | collective-permute-done | bytes 131104 | tf_op jit(solution)/shard_map/ppermute | solution.py:21
  211.1 3.6 %collective-permute-done.66 = bf16[256,128]{1,0:T(8,128)(2,1)S(1)} collective-permute-done((bf16[256,128]{1,0:T(8,128)(2,1)S(1)}, bf16[256,128]{1,0:T(8,128)(2,1)S(1)}, u32[]{:S(2)}, u32[]{:S(2)}) %collective-permute-start.66) | collective-permute-done | bytes 65568 | tf_op jit(solution)/shard_map/ppermute | solution.py:21
  215.6 1.9 collective-permute-start.68
  218.3 2.3 collective-permute-done.69.refs_3_
  223.0 3.3 %shard_map.116 = (f32[2,256,128]{2,1,0:T(8,128)S(1)}, bf16[2,256,128]{2,1,0:T(8,128)(2,1)S(1)}, bf16[2,256,128]{2,1,0:T(8,128)(2,1)S(1)}, bf16[2,256,128]{2,1,0:T(8,128)(2,1)S(1)}) custom-call(s32[8]{0:T(128)S(1)} %concatenate.3.s, bf16[1024,2048]{1,0:T(8,128)(2,1)S(1)} %copy-done.1, bf16[256,128]{1,0:T(8,128)(2,1)S(1)} %fusion.6.refs_0_, ...), custom_call_target="tpu_custom_call" | custom-call | flops 1073741824 | bytes 1048576 | tf_op jit(solution)/shard_map/pallas_call | solution.py:76
  226.7 2.1 collective-permute-start.75
  230.5 2.2 collective-permute-done.74.a
  232.8 1.9 collective-permute-done.75.b
  234.7 1.8 collective-permute-done.76.c
  237.2 6.1 %collective-permute-done.77.got_ref = bf16[3,256,128]{2,1,0:T(8,128)(2,1)S(1)} collective-permute-done((bf16[3,256,128]{2,1,0:T(8,128)(2,1)S(1)}, bf16[3,256,128]{2,1,0:T(8,128)(2,1)S(1)}, u32[]{:S(2)}, u32[]{:S(2)}) %collective-permute-start.77) | collective-permute-done | bytes 196640 | tf_op jit(solution)/shard_map/ppermute | solution.py:21
  247.5 2.7 collective-permute-done.80.refs_3_
  252.9 2.0 shard_map.119
  255.0 1.8 collective-permute-start.86
  256.8 2.2 collective-permute-start.87
  260.6 2.0 collective-permute-done.87
  266.2 2.8 collective-permute-done.90.refs_3_
  271.1 2.0 shard_map.120
  273.2 2.2 collective-permute-start.97
  277.4 6.2 %collective-permute-done.95.a = bf16[2,256,128]{2,1,0:T(8,128)(2,1)S(1)} collective-permute-done((bf16[2,256,128]{2,1,0:T(8,128)(2,1)S(1)}, bf16[2,256,128]{2,1,0:T(8,128)(2,1)S(1)}, u32[]{:S(2)}, u32[]{:S(2)}) %collective-permute-start.95) | collective-permute-done | bytes 131104 | tf_op jit(solution)/shard_map/ppermute | solution.py:21
  (212 shorter events, 95.9 us)
Async XLA Ops:
  4.2 10.0 %collective-permute-start.2 = (bf16[272,256]{1,0:T(8,128)(2,1)S(1)}, bf16[272,256]{1,0:T(8,128)(2,1)S(1)}, u32[]{:S(2)}, u32[]{:S(2)}) collective-permute-start(bf16[272,256]{1,0:T(8,128)(2,1)S(1)} %shard_map.96.refs_0_), channel_id=1, source_target_pairs={{0,3},{1,2},{2,1},{3,0},{4,7},{5,6},{6,5},{7,4},{8,11},{9,10},{10,... | collective-permute-start | bytes 417800 | tf_op jit(solution)/shard_map/ppermute | solution.py:21
  7.1 8.1 %collective-permute-start.1 = (bf16[272,256]{1,0:T(8,128)(2,1)S(1)}, bf16[272,256]{1,0:T(8,128)(2,1)S(1)}, u32[]{:S(2)}, u32[]{:S(2)}) collective-permute-start(bf16[272,256]{1,0:T(8,128)(2,1)S(1)} %shard_map.96.refs_0_), channel_id=1, source_target_pairs={{0,2},{1,3},{2,0},{3,1},{4,6},{5,7},{6,4},{7,5},{8,10},{9,11},{10,... | collective-permute-start | bytes 417800 | tf_op jit(solution)/shard_map/ppermute | solution.py:21
  7.9 7.3 %collective-permute-start = (bf16[272,256]{1,0:T(8,128)(2,1)S(1)}, bf16[272,256]{1,0:T(8,128)(2,1)S(1)}, u32[]{:S(2)}, u32[]{:S(2)}) collective-permute-start(bf16[272,256]{1,0:T(8,128)(2,1)S(1)} %shard_map.96.refs_0_), channel_id=1, source_target_pairs={{0,1},{1,0},{2,3},{3,2},{4,5},{5,4},{6,7},{7,6},{8,9},{9,8},{10,11... | collective-permute-start | bytes 417800 | tf_op jit(solution)/shard_map/ppermute | solution.py:21
  18.9 5.6 %collective-permute-start.4 = (bf16[128,256]{1,0:T(8,128)(2,1)S(1)}, bf16[128,256]{1,0:T(8,128)(2,1)S(1)}, u32[]{:S(2)}, u32[]{:S(2)}) collective-permute-start(bf16[128,256]{1,0:T(8,128)(2,1)S(1)} %get-tuple-element.104), channel_id=1, source_target_pairs={{0,32},{16,48},{32,0},{48,16},{64,96},{80,112},{96,64},{112,80},{1... | collective-permute-start | bytes 196616 | tf_op jit(solution)/shard_map/ppermute | solution.py:21
  20.9 7.1 %collective-permute-start.6 = (bf16[128,256]{1,0:T(8,128)(2,1)S(1)}, bf16[128,256]{1,0:T(8,128)(2,1)S(1)}, u32[]{:S(2)}, u32[]{:S(2)}) collective-permute-start(bf16[128,256]{1,0:T(8,128)(2,1)S(1)} %get-tuple-element.105), channel_id=1, source_target_pairs={{0,64},{16,80},{32,96},{48,112},{64,0},{80,16},{96,32},{112,48},{1... | collective-permute-start | bytes 196616 | tf_op jit(solution)/shard_map/ppermute | solution.py:21
  24.5 5.5 %collective-permute-start.5 = (bf16[128,256]{1,0:T(8,128)(2,1)S(1)}, bf16[128,256]{1,0:T(8,128)(2,1)S(1)}, u32[]{:S(2)}, u32[]{:S(2)}) collective-permute-start(bf16[128,256]{1,0:T(8,128)(2,1)S(1)} %get-tuple-element.106), channel_id=1, source_target_pairs={{0,96},{16,112},{32,64},{48,80},{64,32},{80,48},{96,0},{112,16},{1... | collective-permute-start | bytes 196616 | tf_op jit(solution)/shard_map/ppermute | solution.py:21
  30.0 7.7 %collective-permute-start.9 = (bf16[128,256]{1,0:T(8,128)(2,1)S(1)}, bf16[128,256]{1,0:T(8,128)(2,1)S(1)}, u32[]{:S(2)}, u32[]{:S(2)}) collective-permute-start(bf16[128,256]{1,0:T(8,128)(2,1)S(1)} %get-tuple-element.89.refs_0_), channel_id=1, source_target_pairs={{0,3},{1,2},{2,1},{3,0},{4,7},{5,6},{6,5},{7,4},{8,11},{9,10},{10,... | collective-permute-start | bytes 196616 | tf_op jit(solution)/shard_map/ppermute | solution.py:21
  32.2 5.8 %collective-permute-start.8 = (bf16[128,256]{1,0:T(8,128)(2,1)S(1)}, bf16[128,256]{1,0:T(8,128)(2,1)S(1)}, u32[]{:S(2)}, u32[]{:S(2)}) collective-permute-start(bf16[128,256]{1,0:T(8,128)(2,1)S(1)} %get-tuple-element.89.refs_0_), channel_id=1, source_target_pairs={{0,2},{1,3},{2,0},{3,1},{4,6},{5,7},{6,4},{7,5},{8,10},{9,11},{10,... | collective-permute-start | bytes 196616 | tf_op jit(solution)/shard_map/ppermute | solution.py:21
  33.0 5.0 %collective-permute-start.7 = (bf16[128,256]{1,0:T(8,128)(2,1)S(1)}, bf16[128,256]{1,0:T(8,128)(2,1)S(1)}, u32[]{:S(2)}, u32[]{:S(2)}) collective-permute-start(bf16[128,256]{1,0:T(8,128)(2,1)S(1)} %get-tuple-element.89.refs_0_), channel_id=1, source_target_pairs={{0,1},{1,0},{2,3},{3,2},{4,5},{5,4},{6,7},{7,6},{8,9},{9,8},{10,11... | collective-permute-start | bytes 196616 | tf_op jit(solution)/shard_map/ppermute | solution.py:21
  41.4 6.4 %collective-permute-start.11 = (bf16[128,256]{1,0:T(8,128)(2,1)S(1)}, bf16[128,256]{1,0:T(8,128)(2,1)S(1)}, u32[]{:S(2)}, u32[]{:S(2)}) collective-permute-start(bf16[128,256]{1,0:T(8,128)(2,1)S(1)} %get-tuple-element.101), channel_id=1, source_target_pairs={{0,32},{16,48},{32,0},{48,16},{64,96},{80,112},{96,64},{112,80},{1... | collective-permute-start | bytes 196616 | tf_op jit(solution)/shard_map/ppermute | solution.py:21
  41.5 6.3 %collective-permute-start.13 = (bf16[128,256]{1,0:T(8,128)(2,1)S(1)}, bf16[128,256]{1,0:T(8,128)(2,1)S(1)}, u32[]{:S(2)}, u32[]{:S(2)}) collective-permute-start(bf16[128,256]{1,0:T(8,128)(2,1)S(1)} %get-tuple-element.102), channel_id=1, source_target_pairs={{0,64},{16,80},{32,96},{48,112},{64,0},{80,16},{96,32},{112,48},{1... | collective-permute-start | bytes 196616 | tf_op jit(solution)/shard_map/ppermute | solution.py:21
  43.3 5.5 %collective-permute-start.12 = (bf16[128,256]{1,0:T(8,128)(2,1)S(1)}, bf16[128,256]{1,0:T(8,128)(2,1)S(1)}, u32[]{:S(2)}, u32[]{:S(2)}) collective-permute-start(bf16[128,256]{1,0:T(8,128)(2,1)S(1)} %get-tuple-element.103), channel_id=1, source_target_pairs={{0,96},{16,112},{32,64},{48,80},{64,32},{80,48},{96,0},{112,16},{1... | collective-permute-start | bytes 196616 | tf_op jit(solution)/shard_map/ppermute | solution.py:21
  46.2 5.8 %collective-permute-start.15 = (bf16[288,256]{1,0:T(8,128)(2,1)S(1)}, bf16[288,256]{1,0:T(8,128)(2,1)S(1)}, u32[]{:S(2)}, u32[]{:S(2)}) collective-permute-start(bf16[288,256]{1,0:T(8,128)(2,1)S(1)} %get-tuple-element.45), channel_id=1, source_target_pairs={{0,4},{1,5},{2,6},{3,7},{4,0},{5,1},{6,2},{7,3},{8,12},{9,13},{10,... | collective-permute-start | bytes 442376 | tf_op jit(solution)/shard_map/ppermute | solution.py:21
  53.8 10.8 %collective-permute-start.18 = (bf16[2,128,256]{2,1,0:T(8,128)(2,1)S(1)}, bf16[2,128,256]{2,1,0:T(8,128)(2,1)S(1)}, u32[]{:S(2)}, u32[]{:S(2)}) collective-permute-start(bf16[2,128,256]{2,1,0:T(8,128)(2,1)S(1)} %get-tuple-element.46.refs_0_), channel_id=1, source_target_pairs={{0,3},{1,2},{2,1},{3,0},{4,7},{5,6},{6,5},{7,4},{8,11},{9,10},{10,... | collective-permute-start | bytes 393224 | tf_op jit(solution)/shard_map/ppermute | solution.py:21
  55.7 8.9 %collective-permute-start.17 = (bf16[2,128,256]{2,1,0:T(8,128)(2,1)S(1)}, bf16[2,128,256]{2,1,0:T(8,128)(2,1)S(1)}, u32[]{:S(2)}, u32[]{:S(2)}) collective-permute-start(bf16[2,128,256]{2,1,0:T(8,128)(2,1)S(1)} %get-tuple-element.46.refs_0_), channel_id=1, source_target_pairs={{0,2},{1,3},{2,0},{3,1},{4,6},{5,7},{6,4},{7,5},{8,10},{9,11},{10,... | collective-permute-start | bytes 393224 | tf_op jit(solution)/shard_map/ppermute | solution.py:21
  56.5 8.1 %collective-permute-start.16 = (bf16[2,128,256]{2,1,0:T(8,128)(2,1)S(1)}, bf16[2,128,256]{2,1,0:T(8,128)(2,1)S(1)}, u32[]{:S(2)}, u32[]{:S(2)}) collective-permute-start(bf16[2,128,256]{2,1,0:T(8,128)(2,1)S(1)} %get-tuple-element.46.refs_0_), channel_id=1, source_target_pairs={{0,1},{1,0},{2,3},{3,2},{4,5},{5,4},{6,7},{7,6},{8,9},{9,8},{10,11... | collective-permute-start | bytes 393224 | tf_op jit(solution)/shard_map/ppermute | solution.py:21
  70.6 4.8 %collective-permute-start.20 = (bf16[128,256]{1,0:T(8,128)(2,1)S(1)}, bf16[128,256]{1,0:T(8,128)(2,1)S(1)}, u32[]{:S(2)}, u32[]{:S(2)}) collective-permute-start(bf16[128,256]{1,0:T(8,128)(2,1)S(1)} %get-tuple-element.98), channel_id=1, source_target_pairs={{0,32},{16,48},{32,0},{48,16},{64,96},{80,112},{96,64},{112,80},{1... | collective-permute-start | bytes 196616 | tf_op jit(solution)/shard_map/ppermute | solution.py:21
  71.3 7.4 %collective-permute-start.22 = (bf16[128,256]{1,0:T(8,128)(2,1)S(1)}, bf16[128,256]{1,0:T(8,128)(2,1)S(1)}, u32[]{:S(2)}, u32[]{:S(2)}) collective-permute-start(bf16[128,256]{1,0:T(8,128)(2,1)S(1)} %get-tuple-element.99), channel_id=1, source_target_pairs={{0,64},{16,80},{32,96},{48,112},{64,0},{80,16},{96,32},{112,48},{1... | collective-permute-start | bytes 196616 | tf_op jit(solution)/shard_map/ppermute | solution.py:21
  75.1 5.5 %collective-permute-start.21 = (bf16[128,256]{1,0:T(8,128)(2,1)S(1)}, bf16[128,256]{1,0:T(8,128)(2,1)S(1)}, u32[]{:S(2)}, u32[]{:S(2)}) collective-permute-start(bf16[128,256]{1,0:T(8,128)(2,1)S(1)} %get-tuple-element.100), channel_id=1, source_target_pairs={{0,96},{16,112},{32,64},{48,80},{64,32},{80,48},{96,0},{112,16},{1... | collective-permute-start | bytes 196616 | tf_op jit(solution)/shard_map/ppermute | solution.py:21
  85.5 10.8 %collective-permute-start.26 = (bf16[2,128,256]{2,1,0:T(8,128)(2,1)S(1)}, bf16[2,128,256]{2,1,0:T(8,128)(2,1)S(1)}, u32[]{:S(2)}, u32[]{:S(2)}) collective-permute-start(bf16[2,128,256]{2,1,0:T(8,128)(2,1)S(1)} %shard_map.106.refs_0_), channel_id=1, source_target_pairs={{0,3},{1,2},{2,1},{3,0},{4,7},{5,6},{6,5},{7,4},{8,11},{9,10},{10,... | collective-permute-start | bytes 393224 | tf_op jit(solution)/shard_map/ppermute | solution.py:21
  87.5 8.9 %collective-permute-start.25 = (bf16[2,128,256]{2,1,0:T(8,128)(2,1)S(1)}, bf16[2,128,256]{2,1,0:T(8,128)(2,1)S(1)}, u32[]{:S(2)}, u32[]{:S(2)}) collective-permute-start(bf16[2,128,256]{2,1,0:T(8,128)(2,1)S(1)} %shard_map.106.refs_0_), channel_id=1, source_target_pairs={{0,2},{1,3},{2,0},{3,1},{4,6},{5,7},{6,4},{7,5},{8,10},{9,11},{10,... | collective-permute-start | bytes 393224 | tf_op jit(solution)/shard_map/ppermute | solution.py:21
  88.3 8.1 %collective-permute-start.24 = (bf16[2,128,256]{2,1,0:T(8,128)(2,1)S(1)}, bf16[2,128,256]{2,1,0:T(8,128)(2,1)S(1)}, u32[]{:S(2)}, u32[]{:S(2)}) collective-permute-start(bf16[2,128,256]{2,1,0:T(8,128)(2,1)S(1)} %shard_map.106.refs_0_), channel_id=1, source_target_pairs={{0,1},{1,0},{2,3},{3,2},{4,5},{5,4},{6,7},{7,6},{8,9},{9,8},{10,11... | collective-permute-start | bytes 393224 | tf_op jit(solution)/shard_map/ppermute | solution.py:21
  100.5 9.0 %collective-permute-start.28 = (bf16[128,256]{1,0:T(8,128)(2,1)S(1)}, bf16[128,256]{1,0:T(8,128)(2,1)S(1)}, u32[]{:S(2)}, u32[]{:S(2)}) collective-permute-start(bf16[128,256]{1,0:T(8,128)(2,1)S(1)} %get-tuple-element.95), channel_id=1, source_target_pairs={{0,32},{16,48},{32,0},{48,16},{64,96},{80,112},{96,64},{112,80},{1... | collective-permute-start | bytes 196616 | tf_op jit(solution)/shard_map/ppermute | solution.py:21
  100.5 8.9 %collective-permute-start.30 = (bf16[128,256]{1,0:T(8,128)(2,1)S(1)}, bf16[128,256]{1,0:T(8,128)(2,1)S(1)}, u32[]{:S(2)}, u32[]{:S(2)}) collective-permute-start(bf16[128,256]{1,0:T(8,128)(2,1)S(1)} %get-tuple-element.96), channel_id=1, source_target_pairs={{0,64},{16,80},{32,96},{48,112},{64,0},{80,16},{96,32},{112,48},{1... | collective-permute-start | bytes 196616 | tf_op jit(solution)/shard_map/ppermute | solution.py:21
  102.3 7.2 %collective-permute-start.29 = (bf16[128,256]{1,0:T(8,128)(2,1)S(1)}, bf16[128,256]{1,0:T(8,128)(2,1)S(1)}, u32[]{:S(2)}, u32[]{:S(2)}) collective-permute-start(bf16[128,256]{1,0:T(8,128)(2,1)S(1)} %get-tuple-element.97), channel_id=1, source_target_pairs={{0,96},{16,112},{32,64},{48,80},{64,32},{80,48},{96,0},{112,16},{1... | collective-permute-start | bytes 196616 | tf_op jit(solution)/shard_map/ppermute | solution.py:21
  105.2 8.0 %collective-permute-start.35 = (bf16[144,256]{1,0:T(8,128)(2,1)S(1)}, bf16[144,256]{1,0:T(8,128)(2,1)S(1)}, u32[]{:S(2)}, u32[]{:S(2)}) collective-permute-start(bf16[144,256]{1,0:T(8,128)(2,1)S(1)} %get-tuple-element.54), channel_id=1, source_target_pairs={{0,8},{1,9},{2,10},{3,11},{4,12},{5,13},{6,14},{7,15},{8,0},{9,1},... | collective-permute-start | bytes 221192 | tf_op jit(solution)/shard_map/ppermute | solution.py:21
  108.4 5.9 %collective-permute-start.34 = (bf16[144,256]{1,0:T(8,128)(2,1)S(1)}, bf16[144,256]{1,0:T(8,128)(2,1)S(1)}, u32[]{:S(2)}, u32[]{:S(2)}) collective-permute-start(bf16[144,256]{1,0:T(8,128)(2,1)S(1)} %get-tuple-element.54), channel_id=1, source_target_pairs={{0,12},{1,13},{2,14},{3,15},{4,8},{5,9},{6,10},{7,11},{8,4},{9,5},... | collective-permute-start | bytes 221192 | tf_op jit(solution)/shard_map/ppermute | solution.py:21
  109.5 6.5 %collective-permute-start.33 = (bf16[128,256]{1,0:T(8,128)(2,1)S(1)}, bf16[128,256]{1,0:T(8,128)(2,1)S(1)}, u32[]{:S(2)}, u32[]{:S(2)}) collective-permute-start(bf16[128,256]{1,0:T(8,128)(2,1)S(1)} %get-tuple-element.83), channel_id=1, source_target_pairs={{0,8},{1,9},{2,10},{3,11},{4,12},{5,13},{6,14},{7,15},{8,0},{9,1},... | collective-permute-start | bytes 196616 | tf_op jit(solution)/shard_map/ppermute | solution.py:21
  111.5 5.5 %collective-permute-start.32 = (bf16[128,256]{1,0:T(8,128)(2,1)S(1)}, bf16[128,256]{1,0:T(8,128)(2,1)S(1)}, u32[]{:S(2)}, u32[]{:S(2)}) collective-permute-start(bf16[128,256]{1,0:T(8,128)(2,1)S(1)} %get-tuple-element.83), channel_id=1, source_target_pairs={{0,12},{1,13},{2,14},{3,15},{4,8},{5,9},{6,10},{7,11},{8,4},{9,5},... | collective-permute-start | bytes 196616 | tf_op jit(solution)/shard_map/ppermute | solution.py:21
  117.7 17.0 %collective-permute-start.38 = (bf16[4,128,256]{2,1,0:T(8,128)(2,1)S(1)}, bf16[4,128,256]{2,1,0:T(8,128)(2,1)S(1)}, u32[]{:S(2)}, u32[]{:S(2)}) collective-permute-start(bf16[4,128,256]{2,1,0:T(8,128)(2,1)S(1)} %shard_map.108.refs_0_), channel_id=1, source_target_pairs={{0,3},{1,2},{2,1},{3,0},{4,7},{5,6},{6,5},{7,4},{8,11},{9,10},{10,... | collective-permute-start | bytes 786440 | tf_op jit(solution)/shard_map/ppermute | solution.py:21
  119.5 15.1 %collective-permute-start.37 = (bf16[4,128,256]{2,1,0:T(8,128)(2,1)S(1)}, bf16[4,128,256]{2,1,0:T(8,128)(2,1)S(1)}, u32[]{:S(2)}, u32[]{:S(2)}) collective-permute-start(bf16[4,128,256]{2,1,0:T(8,128)(2,1)S(1)} %shard_map.108.refs_0_), channel_id=1, source_target_pairs={{0,2},{1,3},{2,0},{3,1},{4,6},{5,7},{6,4},{7,5},{8,10},{9,11},{10,... | collective-permute-start | bytes 786440 | tf_op jit(solution)/shard_map/ppermute | solution.py:21
  120.3 14.4 %collective-permute-start.36 = (bf16[4,128,256]{2,1,0:T(8,128)(2,1)S(1)}, bf16[4,128,256]{2,1,0:T(8,128)(2,1)S(1)}, u32[]{:S(2)}, u32[]{:S(2)}) collective-permute-start(bf16[4,128,256]{2,1,0:T(8,128)(2,1)S(1)} %shard_map.108.refs_0_), channel_id=1, source_target_pairs={{0,1},{1,0},{2,3},{3,2},{4,5},{5,4},{6,7},{7,6},{8,9},{9,8},{10,11... | collective-permute-start | bytes 786440 | tf_op jit(solution)/shard_map/ppermute | solution.py:21
  140.0 4.8 %collective-permute-start.40 = (bf16[128,256]{1,0:T(8,128)(2,1)S(1)}, bf16[128,256]{1,0:T(8,128)(2,1)S(1)}, u32[]{:S(2)}, u32[]{:S(2)}) collective-permute-start(bf16[128,256]{1,0:T(8,128)(2,1)S(1)} %get-tuple-element.92), channel_id=1, source_target_pairs={{0,32},{16,48},{32,0},{48,16},{64,96},{80,112},{96,64},{112,80},{1... | collective-permute-start | bytes 196616 | tf_op jit(solution)/shard_map/ppermute | solution.py:21
  140.4 7.4 %collective-permute-start.42 = (bf16[128,256]{1,0:T(8,128)(2,1)S(1)}, bf16[128,256]{1,0:T(8,128)(2,1)S(1)}, u32[]{:S(2)}, u32[]{:S(2)}) collective-permute-start(bf16[128,256]{1,0:T(8,128)(2,1)S(1)} %get-tuple-element.93), channel_id=1, source_target_pairs={{0,64},{16,80},{32,96},{48,112},{64,0},{80,16},{96,32},{112,48},{1... | collective-permute-start | bytes 196616 | tf_op jit(solution)/shard_map/ppermute | solution.py:21
  144.2 5.5 %collective-permute-start.41 = (bf16[128,256]{1,0:T(8,128)(2,1)S(1)}, bf16[128,256]{1,0:T(8,128)(2,1)S(1)}, u32[]{:S(2)}, u32[]{:S(2)}) collective-permute-start(bf16[128,256]{1,0:T(8,128)(2,1)S(1)} %get-tuple-element.94), channel_id=1, source_target_pairs={{0,96},{16,112},{32,64},{48,80},{64,32},{80,48},{96,0},{112,16},{1... | collective-permute-start | bytes 196616 | tf_op jit(solution)/shard_map/ppermute | solution.py:21
  150.4 5.9 %collective-permute-start.45 = (bf16[256,128]{1,0:T(8,128)(2,1)S(1)}, bf16[256,128]{1,0:T(8,128)(2,1)S(1)}, u32[]{:S(2)}, u32[]{:S(2)}) collective-permute-start(bf16[256,128]{1,0:T(8,128)(2,1)S(1)} %shard_map.110.refs_0_), channel_id=1, source_target_pairs={{0,64},{16,80},{32,96},{48,112},{64,0},{80,16},{96,32},{112,48},{1... | collective-permute-start | bytes 196616 | tf_op jit(solution)/shard_map/ppermute | solution.py:21
  150.8 6.2 %collective-permute-start.44 = (bf16[256,128]{1,0:T(8,128)(2,1)S(1)}, bf16[256,128]{1,0:T(8,128)(2,1)S(1)}, u32[]{:S(2)}, u32[]{:S(2)}) collective-permute-start(bf16[256,128]{1,0:T(8,128)(2,1)S(1)} %shard_map.110.refs_0_), channel_id=1, source_target_pairs={{0,96},{16,112},{32,64},{48,80},{64,32},{80,48},{96,0},{112,16},{1... | collective-permute-start | bytes 196616 | tf_op jit(solution)/shard_map/ppermute | solution.py:21
  152.3 4.7 %collective-permute-start.43 = (bf16[256,128]{1,0:T(8,128)(2,1)S(1)}, bf16[256,128]{1,0:T(8,128)(2,1)S(1)}, u32[]{:S(2)}, u32[]{:S(2)}) collective-permute-start(bf16[256,128]{1,0:T(8,128)(2,1)S(1)} %shard_map.110.refs_0_), channel_id=1, source_target_pairs={{0,32},{16,48},{32,0},{48,16},{64,96},{80,112},{96,64},{112,80},{1... | collective-permute-start | bytes 196616 | tf_op jit(solution)/shard_map/ppermute | solution.py:21
  160.4 10.7 %collective-permute-start.50 = (bf16[4,256,128]{2,1,0:T(8,128)(2,1)S(1)}, bf16[4,256,128]{2,1,0:T(8,128)(2,1)S(1)}, u32[]{:S(2)}, u32[]{:S(2)}) collective-permute-start(bf16[4,256,128]{2,1,0:T(8,128)(2,1)S(1)} %shard_map.112), channel_id=1, source_target_pairs={{0,2},{1,3},{2,0},{3,1},{4,6},{5,7},{6,4},{7,5},{8,10},{9,11},{10,... | collective-permute-start | bytes 786440 | tf_op jit(solution)/shard_map/ppermute | solution.py:21
  164.5 10.7 %collective-permute-start.51 = (bf16[4,256,128]{2,1,0:T(8,128)(2,1)S(1)}, bf16[4,256,128]{2,1,0:T(8,128)(2,1)S(1)}, u32[]{:S(2)}, u32[]{:S(2)}) collective-permute-start(bf16[4,256,128]{2,1,0:T(8,128)(2,1)S(1)} %shard_map.113), channel_id=1, source_target_pairs={{0,1},{1,0},{2,3},{3,2},{4,5},{5,4},{6,7},{7,6},{8,9},{9,8},{10,11... | collective-permute-start | bytes 786440 | tf_op jit(solution)/shard_map/ppermute | solution.py:21
  167.1 9.4 %collective-permute-start.52 = (bf16[4,256,128]{2,1,0:T(8,128)(2,1)S(1)}, bf16[4,256,128]{2,1,0:T(8,128)(2,1)S(1)}, u32[]{:S(2)}, u32[]{:S(2)}) collective-permute-start(bf16[4,256,128]{2,1,0:T(8,128)(2,1)S(1)} %shard_map.114), channel_id=1, source_target_pairs={{0,3},{1,2},{2,1},{3,0},{4,7},{5,6},{6,5},{7,4},{8,11},{9,10},{10,... | collective-permute-start | bytes 786440 | tf_op jit(solution)/shard_map/ppermute | solution.py:21
  176.7 7.8 %collective-permute-start.53 = (bf16[2,256,128]{2,1,0:T(8,128)(2,1)S(1)}, bf16[2,256,128]{2,1,0:T(8,128)(2,1)S(1)}, u32[]{:S(2)}, u32[]{:S(2)}) collective-permute-start(bf16[2,256,128]{2,1,0:T(8,128)(2,1)S(1)} %get-tuple-element.81), channel_id=1, source_target_pairs={{0,8},{1,9},{2,10},{3,11},{4,12},{5,13},{6,14},{7,15},{8,0},{9,1},... | collective-permute-start | bytes 393224 | tf_op jit(solution)/shard_map/ppermute | solution.py:21
  178.3 7.2 %collective-permute-start.55 = (bf16[2,256,128]{2,1,0:T(8,128)(2,1)S(1)}, bf16[2,256,128]{2,1,0:T(8,128)(2,1)S(1)}, u32[]{:S(2)}, u32[]{:S(2)}) collective-permute-start(bf16[2,256,128]{2,1,0:T(8,128)(2,1)S(1)} %get-tuple-element.91), channel_id=1, source_target_pairs={{0,12},{1,13},{2,14},{3,15},{4,8},{5,9},{6,10},{7,11},{8,4},{9,5},... | collective-permute-start | bytes 393224 | tf_op jit(solution)/shard_map/ppermute | solution.py:21
  179.3 6.3 %collective-permute-start.54 = (bf16[2,256,128]{2,1,0:T(8,128)(2,1)S(1)}, bf16[2,256,128]{2,1,0:T(8,128)(2,1)S(1)}, u32[]{:S(2)}, u32[]{:S(2)}) collective-permute-start(bf16[2,256,128]{2,1,0:T(8,128)(2,1)S(1)} %get-tuple-element.91), channel_id=1, source_target_pairs={{0,4},{1,5},{2,6},{3,7},{4,0},{5,1},{6,2},{7,3},{8,12},{9,13},{10,... | collective-permute-start | bytes 393224 | tf_op jit(solution)/shard_map/ppermute | solution.py:21
  185.7 6.6 %collective-permute-start.58 = (bf16[256,128]{1,0:T(8,128)(2,1)S(1)}, bf16[256,128]{1,0:T(8,128)(2,1)S(1)}, u32[]{:S(2)}, u32[]{:S(2)}) collective-permute-start(bf16[256,128]{1,0:T(8,128)(2,1)S(1)} %get-tuple-element.78.refs_0_.down_ref), channel_id=1, source_target_pairs={{0,64},{16,80},{32,96},{48,112},{64,0},{80,16},{96,32},{112,48},{1... | collective-permute-start | bytes 196616 | tf_op jit(solution)/shard_map/ppermute | solution.py:21
  187.1 5.7 %collective-permute-start.57 = (bf16[256,128]{1,0:T(8,128)(2,1)S(1)}, bf16[256,128]{1,0:T(8,128)(2,1)S(1)}, u32[]{:S(2)}, u32[]{:S(2)}) collective-permute-start(bf16[256,128]{1,0:T(8,128)(2,1)S(1)} %get-tuple-element.78.refs_0_.down_ref), channel_id=1, source_target_pairs={{0,96},{16,112},{32,64},{48,80},{64,32},{80,48},{96,0},{112,16},{1... | collective-permute-start | bytes 196616 | tf_op jit(solution)/shard_map/ppermute | solution.py:21
  200.4 6.4 %collective-permute-start.63 = (bf16[2,256,128]{2,1,0:T(8,128)(2,1)S(1)}, bf16[2,256,128]{2,1,0:T(8,128)(2,1)S(1)}, u32[]{:S(2)}, u32[]{:S(2)}) collective-permute-start(bf16[2,256,128]{2,1,0:T(8,128)(2,1)S(1)} %get-tuple-element.58), channel_id=1, source_target_pairs={{0,1},{1,0},{2,3},{3,2},{4,5},{5,4},{6,7},{7,6},{8,9},{9,8},{10,11... | collective-permute-start | bytes 393224 | tf_op jit(solution)/shard_map/ppermute | solution.py:21
  201.0 9.3 %collective-permute-start.64 = (bf16[2,256,128]{2,1,0:T(8,128)(2,1)S(1)}, bf16[2,256,128]{2,1,0:T(8,128)(2,1)S(1)}, u32[]{:S(2)}, u32[]{:S(2)}) collective-permute-start(bf16[2,256,128]{2,1,0:T(8,128)(2,1)S(1)} %get-tuple-element.59), channel_id=1, source_target_pairs={{0,3},{1,2},{2,1},{3,0},{4,7},{5,6},{6,5},{7,4},{8,11},{9,10},{10,... | collective-permute-start | bytes 393224 | tf_op jit(solution)/shard_map/ppermute | solution.py:21
  203.1 7.1 %collective-permute-start.65 = (bf16[2,256,128]{2,1,0:T(8,128)(2,1)S(1)}, bf16[2,256,128]{2,1,0:T(8,128)(2,1)S(1)}, u32[]{:S(2)}, u32[]{:S(2)}) collective-permute-start(bf16[2,256,128]{2,1,0:T(8,128)(2,1)S(1)} %get-tuple-element.60), channel_id=1, source_target_pairs={{0,2},{1,3},{2,0},{3,1},{4,6},{5,7},{6,4},{7,5},{8,10},{9,11},{10,... | collective-permute-start | bytes 393224 | tf_op jit(solution)/shard_map/ppermute | solution.py:21
  214.7 5.9 %collective-permute-start.69 = (bf16[256,128]{1,0:T(8,128)(2,1)S(1)}, bf16[256,128]{1,0:T(8,128)(2,1)S(1)}, u32[]{:S(2)}, u32[]{:S(2)}) collective-permute-start(bf16[256,128]{1,0:T(8,128)(2,1)S(1)} %fusion.6.refs_0_), channel_id=1, source_target_pairs={{0,64},{16,80},{32,96},{48,112},{64,0},{80,16},{96,32},{112,48},{1... | collective-permute-start | bytes 196616 | tf_op jit(solution)/shard_map/ppermute | solution.py:21
  215.6 5.7 %collective-permute-start.68 = (bf16[256,128]{1,0:T(8,128)(2,1)S(1)}, bf16[256,128]{1,0:T(8,128)(2,1)S(1)}, u32[]{:S(2)}, u32[]{:S(2)}) collective-permute-start(bf16[256,128]{1,0:T(8,128)(2,1)S(1)} %fusion.6.refs_0_), channel_id=1, source_target_pairs={{0,96},{16,112},{32,64},{48,80},{64,32},{80,48},{96,0},{112,16},{1... | collective-permute-start | bytes 196616 | tf_op jit(solution)/shard_map/ppermute | solution.py:21
  226.4 6.4 %collective-permute-start.74 = (bf16[2,256,128]{2,1,0:T(8,128)(2,1)S(1)}, bf16[2,256,128]{2,1,0:T(8,128)(2,1)S(1)}, u32[]{:S(2)}, u32[]{:S(2)}) collective-permute-start(bf16[2,256,128]{2,1,0:T(8,128)(2,1)S(1)} %get-tuple-element.62), channel_id=1, source_target_pairs={{0,1},{1,0},{2,3},{3,2},{4,5},{5,4},{6,7},{7,6},{8,9},{9,8},{10,11... | collective-permute-start | bytes 393224 | tf_op jit(solution)/shard_map/ppermute | solution.py:21
  226.7 8.0 %collective-permute-start.75 = (bf16[2,256,128]{2,1,0:T(8,128)(2,1)S(1)}, bf16[2,256,128]{2,1,0:T(8,128)(2,1)S(1)}, u32[]{:S(2)}, u32[]{:S(2)}) collective-permute-start(bf16[2,256,128]{2,1,0:T(8,128)(2,1)S(1)} %get-tuple-element.63), channel_id=1, source_target_pairs={{0,3},{1,2},{2,1},{3,0},{4,7},{5,6},{6,5},{7,4},{8,11},{9,10},{10,... | collective-permute-start | bytes 393224 | tf_op jit(solution)/shard_map/ppermute | solution.py:21
  228.8 7.7 %collective-permute-start.76 = (bf16[2,256,128]{2,1,0:T(8,128)(2,1)S(1)}, bf16[2,256,128]{2,1,0:T(8,128)(2,1)S(1)}, u32[]{:S(2)}, u32[]{:S(2)}) collective-permute-start(bf16[2,256,128]{2,1,0:T(8,128)(2,1)S(1)} %get-tuple-element.64), channel_id=1, source_target_pairs={{0,2},{1,3},{2,0},{3,1},{4,6},{5,7},{6,4},{7,5},{8,10},{9,11},{10,... | collective-permute-start | bytes 393224 | tf_op jit(solution)/shard_map/ppermute | solution.py:21
  237.1 6.2 %collective-permute-start.77 = (bf16[3,256,128]{2,1,0:T(8,128)(2,1)S(1)}, bf16[3,256,128]{2,1,0:T(8,128)(2,1)S(1)}, u32[]{:S(2)}, u32[]{:S(2)}) collective-permute-start(bf16[3,256,128]{2,1,0:T(8,128)(2,1)S(1)} %get-tuple-element.66), channel_id=1, source_target_pairs={{0,4},{1,5},{2,6},{3,7},{4,0},{5,1},{6,2},{7,3},{8,12},{9,13},{10,... | collective-permute-start | bytes 589832 | tf_op jit(solution)/shard_map/ppermute | solution.py:21
  243.9 6.3 %collective-permute-start.80 = (bf16[256,128]{1,0:T(8,128)(2,1)S(1)}, bf16[256,128]{1,0:T(8,128)(2,1)S(1)}, u32[]{:S(2)}, u32[]{:S(2)}) collective-permute-start(bf16[256,128]{1,0:T(8,128)(2,1)S(1)} %get-tuple-element.67.refs_0_.refs_8_), channel_id=1, source_target_pairs={{0,64},{16,80},{32,96},{48,112},{64,0},{80,16},{96,32},{112,48},{1... | collective-permute-start | bytes 196616 | tf_op jit(solution)/shard_map/ppermute | solution.py:21
  245.7 5.5 %collective-permute-start.79 = (bf16[256,128]{1,0:T(8,128)(2,1)S(1)}, bf16[256,128]{1,0:T(8,128)(2,1)S(1)}, u32[]{:S(2)}, u32[]{:S(2)}) collective-permute-start(bf16[256,128]{1,0:T(8,128)(2,1)S(1)} %get-tuple-element.67.refs_0_.refs_8_), channel_id=1, source_target_pairs={{0,96},{16,112},{32,64},{48,80},{64,32},{80,48},{96,0},{112,16},{1... | collective-permute-start | bytes 196616 | tf_op jit(solution)/shard_map/ppermute | solution.py:21
  255.0 5.6 %collective-permute-start.86 = (bf16[1,256,128]{2,1,0:T(8,128)(2,1)S(1)}, bf16[1,256,128]{2,1,0:T(8,128)(2,1)S(1)}, u32[]{:S(2)}, u32[]{:S(2)}) collective-permute-start(bf16[1,256,128]{2,1,0:T(8,128)(2,1)S(1)} %get-tuple-element.70), channel_id=1, source_target_pairs={{0,3},{1,2},{2,1},{3,0},{4,7},{5,6},{6,5},{7,4},{8,11},{9,10},{10,... | collective-permute-start | bytes 196616 | tf_op jit(solution)/shard_map/ppermute | solution.py:21
  256.8 5.8 %collective-permute-start.87 = (bf16[1,256,128]{2,1,0:T(8,128)(2,1)S(1)}, bf16[1,256,128]{2,1,0:T(8,128)(2,1)S(1)}, u32[]{:S(2)}, u32[]{:S(2)}) collective-permute-start(bf16[1,256,128]{2,1,0:T(8,128)(2,1)S(1)} %get-tuple-element.71), channel_id=1, source_target_pairs={{0,2},{1,3},{2,0},{3,1},{4,6},{5,7},{6,4},{7,5},{8,10},{9,11},{10,... | collective-permute-start | bytes 196616 | tf_op jit(solution)/shard_map/ppermute | solution.py:21
  262.6 6.4 %collective-permute-start.90 = (bf16[256,128]{1,0:T(8,128)(2,1)S(1)}, bf16[256,128]{1,0:T(8,128)(2,1)S(1)}, u32[]{:S(2)}, u32[]{:S(2)}) collective-permute-start(bf16[256,128]{1,0:T(8,128)(2,1)S(1)} %fusion.4.refs_0_), channel_id=1, source_target_pairs={{0,64},{16,80},{32,96},{48,112},{64,0},{80,16},{96,32},{112,48},{1... | collective-permute-start | bytes 196616 | tf_op jit(solution)/shard_map/ppermute | solution.py:21
  264.2 5.5 %collective-permute-start.89 = (bf16[256,128]{1,0:T(8,128)(2,1)S(1)}, bf16[256,128]{1,0:T(8,128)(2,1)S(1)}, u32[]{:S(2)}, u32[]{:S(2)}) collective-permute-start(bf16[256,128]{1,0:T(8,128)(2,1)S(1)} %fusion.4.refs_0_), channel_id=1, source_target_pairs={{0,96},{16,112},{32,64},{48,80},{64,32},{80,48},{96,0},{112,16},{1... | collective-permute-start | bytes 196616 | tf_op jit(solution)/shard_map/ppermute | solution.py:21
  273.2 11.6 %collective-permute-start.97 = (bf16[3,256,128]{2,1,0:T(8,128)(2,1)S(1)}, bf16[3,256,128]{2,1,0:T(8,128)(2,1)S(1)}, u32[]{:S(2)}, u32[]{:S(2)}) collective-permute-start(bf16[3,256,128]{2,1,0:T(8,128)(2,1)S(1)} %get-tuple-element.75), channel_id=1, source_target_pairs={{0,2},{1,3},{2,0},{3,1},{4,6},{5,7},{6,4},{7,5},{8,10},{9,11},{10,... | collective-permute-start | bytes 589832 | tf_op jit(solution)/shard_map/ppermute | solution.py:21
  275.4 8.2 %collective-permute-start.95 = (bf16[2,256,128]{2,1,0:T(8,128)(2,1)S(1)}, bf16[2,256,128]{2,1,0:T(8,128)(2,1)S(1)}, u32[]{:S(2)}, u32[]{:S(2)}) collective-permute-start(bf16[2,256,128]{2,1,0:T(8,128)(2,1)S(1)} %get-tuple-element.73), channel_id=1, source_target_pairs={{0,1},{1,0},{2,3},{3,2},{4,5},{5,4},{6,7},{7,6},{8,9},{9,8},{10,11... | collective-permute-start | bytes 393224 | tf_op jit(solution)/shard_map/ppermute | solution.py:21
  275.6 9.1 %collective-permute-start.96 = (bf16[2,256,128]{2,1,0:T(8,128)(2,1)S(1)}, bf16[2,256,128]{2,1,0:T(8,128)(2,1)S(1)}, u32[]{:S(2)}, u32[]{:S(2)}) collective-permute-start(bf16[2,256,128]{2,1,0:T(8,128)(2,1)S(1)} %get-tuple-element.74), channel_id=1, source_target_pairs={{0,3},{1,2},{2,1},{3,0},{4,7},{5,6},{6,5},{7,4},{8,11},{9,10},{10,... | collective-permute-start | bytes 393224 | tf_op jit(solution)/shard_map/ppermute | solution.py:21
  (50 other events, 396.5 us)
where the time goes:
time: 287 us; the launch traced here: 286 us
  starting transfers between devices  103 us (36%)
  waiting for transfers between devices  102 us (36%)
  Pallas kernels  70.4 us (25%)
  local copies, waits for them, and re-layouts  9.23 us (3%)
    ppermute x98, starting transfers between devices, swap(): return lax.ppermute(value, axis, [(i, i ^ mask) for i in range(count)])  103 us
    ppermute x98, waiting for transfers between devices, swap(): return lax.ppermute(value, axis, [(i, i ^ mask) for i in range(count)])  102 us
    pallas_call x5, Pallas kernels, relay(): pl.pallas_call(functools.partial(relay_body, groups), grid=(tiles,), out_...  32.9 us
    pallas_call x13, Pallas kernels, call(): pl.pallas_call(body, out_shape=[jax.ShapeDtypeStruct(*o) for o in outs],...  30.7 us
    unnamed x33, local copies, waits for them, and re-layouts  8.49 us
    pallas_call x8, Pallas kernels, small(): pl.pallas_call(body, out_shape=[jax.ShapeDtypeStruct(*o) for o in outs],...  5.85 us
  transfers between devices with their start and end apart: 98, of which 61 were waited for; matrix products, arithmetic and copies ran while one was open for 0% of the time, Pallas kernels for 14%

commit v1 on v0

--- a/solution.py
+++ b/solution.py
@@ -40,13 +40,12 @@
     source = lax.broadcasted_iota(jnp.int32, (C, C), 1)
     place = (source == (target & span - 1) * groups + (target >> shift)).astype(BF)
 
-    @pl.loop(0, B * groups // C)
-    def _(chunk):
-        rows = pl.ds(pl.multiple_of(chunk * C, C), C)
+    for chunk in range(B * groups // C):
+        rows = slice(chunk * C, (chunk + 1) * C)
         both = jnp.concatenate([real_ref[rows, :], imag_ref[rows, :]], axis=1)
         moved = jnp.dot(place, both, preferred_element_type=F32).astype(BF)
         for p in range(groups):
-            out_ref[pl.ds(pl.multiple_of(chunk * span, span), span), p * C : (p + 1) * C] = moved[
+            out_ref[chunk * span : (chunk + 1) * span, p * C : (p + 1) * C] = moved[
                 p * span : (p + 1) * span
             ]
 
@@ -151,7 +150,7 @@
             return
         acc = scratch[1]
 
-        @pl.loop(0, 4 * tiles)
+        @pl.loop(0, 4 * tiles, unroll=2)
         def _(step):
             k, j = step & 3, step >> 2
             acc[k, j] = block(((s[Y] & mask) ^ j) * 4 + (s[X] ^ k))

time: 287 us -> 277 us (0.965)
  Pallas kernels: 70.4 us -> 48.1 us
  waiting for transfers between devices: 102 us -> 114 us
    pallas_call x5, Pallas kernels: 32.9 us -> 12.5 us  [relay(): pl.pallas_call(functools.partial(relay_body, groups), grid=(tiles,), out_...]
    ppermute x98, waiting for transfers between devices: 102 us -> 114 us  [swap(): return lax.ppermute(value, axis, [(i, i ^ mask) for i in range(count)])]
  transfers between devices with their start and end apart: 98 -> 98, of which waited for: 61 -> 71; matrix products, arithmetic and copies ran while one was open for 0% -> 0% of each run, Pallas kernels for 14% -> 7%
where the time goes in v1:
time: 277 us; the launch traced here: 276 us
  waiting for transfers between devices  114 us (41%)
  starting transfers between devices  102 us (37%)
  Pallas kernels  48.1 us (17%)
  local copies, waits for them, and re-layouts  9.23 us (3%)
    ppermute x98, waiting for transfers between devices, swap(): return lax.ppermute(value, axis, [(i, i ^ mask) for i in range(count)])  114 us
    ppermute x98, starting transfers between devices, swap(): return lax.ppermute(value, axis, [(i, i ^ mask) for i in range(count)])  102 us
    pallas_call x13, Pallas kernels, call(): pl.pallas_call(body, out_shape=[jax.ShapeDtypeStruct(*o) for o in outs],...  28.7 us
    pallas_call x5, Pallas kernels, relay(): pl.pallas_call(functools.partial(relay_body, groups), grid=(tiles,), out_...  12.5 us
    unnamed x33, local copies, waits for them, and re-layouts  8.49 us
    pallas_call x8, Pallas kernels, small(): pl.pallas_call(body, out_shape=[jax.ShapeDtypeStruct(*o) for o in outs],...  5.85 us
  transfers between devices with their start and end apart: 98, of which 71 were waited for; matrix products, arithmetic and copies ran while one was open for 0% of the time, Pallas kernels for 7%

profile of v1, /device:TPU:0, one launch (start us, length us, event | category | flops | bytes accessed | tf_op | source)
XLA Modules:
  0.0 275.6 jit_solution(1566034595763240076)
XLA Ops:
  4.2 2.9 %collective-permute-start.2 = (bf16[272,256]{1,0:T(8,128)(2,1)S(1)}, bf16[272,256]{1,0:T(8,128)(2,1)S(1)}, u32[]{:S(2)}, u32[]{:S(2)}) collective-permute-start(bf16[272,256]{1,0:T(8,128)(2,1)S(1)} %shard_map.96.refs_0_), channel_id=1, source_target_pairs={{0,3},{1,2},{2,1},{3,0},{4,7},{5,6},{6,5},{7,4},{8,11},{9,10},{10,... | collective-permute-start | bytes 417800 | tf_op jit(solution)/shard_map/ppermute | solution.py:21
  10.7 1.9 shard_map.95.w_ref
  13.1 2.2 collective-permute-done.1.refs_2_
  15.3 2.0 shard_map.97
  18.9 2.0 collective-permute-start.4
  20.9 3.6 %collective-permute-start.6 = (bf16[128,256]{1,0:T(8,128)(2,1)S(1)}, bf16[128,256]{1,0:T(8,128)(2,1)S(1)}, u32[]{:S(2)}, u32[]{:S(2)}) collective-permute-start(bf16[128,256]{1,0:T(8,128)(2,1)S(1)} %get-tuple-element.105), channel_id=1, source_target_pairs={{0,64},{16,80},{32,96},{48,112},{64,0},{80,16},{96,32},{112,48},{1... | collective-permute-start | bytes 196616 | tf_op jit(solution)/shard_map/ppermute | solution.py:21
  24.5 3.5 %collective-permute-done.6 = bf16[128,256]{1,0:T(8,128)(2,1)S(1)} collective-permute-done((bf16[128,256]{1,0:T(8,128)(2,1)S(1)}, bf16[128,256]{1,0:T(8,128)(2,1)S(1)}, u32[]{:S(2)}, u32[]{:S(2)}) %collective-permute-start.6) | collective-permute-done | bytes 65568 | tf_op jit(solution)/shard_map/ppermute | solution.py:21
  28.0 2.0 collective-permute-done.5
  30.0 2.2 collective-permute-start.9
  34.2 1.9 shard_map.99.w_ref
  36.1 1.8 collective-permute-done.8.refs_2_
  38.0 1.8 shard_map.100
  43.3 2.9 %collective-permute-start.12 = (bf16[128,256]{1,0:T(8,128)(2,1)S(1)}, bf16[128,256]{1,0:T(8,128)(2,1)S(1)}, u32[]{:S(2)}, u32[]{:S(2)}) collective-permute-start(bf16[128,256]{1,0:T(8,128)(2,1)S(1)} %get-tuple-element.103), channel_id=1, source_target_pairs={{0,96},{16,112},{32,64},{48,80},{64,32},{80,48},{96,0},{112,16},{1... | collective-permute-start | bytes 196616 | tf_op jit(solution)/shard_map/ppermute | solution.py:21
  58.0 2.5 shard_map.98.w_ref
  62.8 2.4 shard_map.102
  65.2 2.0 copy-done
  69.0 3.8 %collective-permute-start.22 = (bf16[128,256]{1,0:T(8,128)(2,1)S(1)}, bf16[128,256]{1,0:T(8,128)(2,1)S(1)}, u32[]{:S(2)}, u32[]{:S(2)}) collective-permute-start(bf16[128,256]{1,0:T(8,128)(2,1)S(1)} %get-tuple-element.99), channel_id=1, source_target_pairs={{0,64},{16,80},{32,96},{48,112},{64,0},{80,16},{96,32},{112,48},{1... | collective-permute-start | bytes 196616 | tf_op jit(solution)/shard_map/ppermute | solution.py:21
  73.6 2.7 collective-permute-done.22
  76.3 2.0 collective-permute-done.21
  80.0 2.7 collective-permute-done.23.b_ref
  87.4 2.5 shard_map.104.w_ref
  91.8 2.4 shard_map.107
  95.9 2.2 collective-permute-start.30
  98.2 2.4 collective-permute-start.29
  100.6 3.2 %collective-permute-start.35 = (bf16[144,256]{1,0:T(8,128)(2,1)S(1)}, bf16[144,256]{1,0:T(8,128)(2,1)S(1)}, u32[]{:S(2)}, u32[]{:S(2)}) collective-permute-start(bf16[144,256]{1,0:T(8,128)(2,1)S(1)} %get-tuple-element.54), channel_id=1, source_target_pairs={{0,8},{1,9},{2,10},{3,11},{4,12},{5,13},{6,14},{7,15},{8,0},{9,1},... | collective-permute-start | bytes 221192 | tf_op jit(solution)/shard_map/ppermute | solution.py:21
  104.9 2.0 collective-permute-start.33
  117.3 3.6 %shard_map.105.w_ref = bf16[1024,4096]{1,0:T(8,128)(2,1)S(1)} custom-call(bf16[32768,128]{1,0:T(8,128)(2,1)S(1)} %bitcast.103, bf16[32768,128]{1,0:T(8,128)(2,1)S(1)} %bitcast.104), custom_call_target="tpu_custom_call" | custom-call | flops 2147483648 | bytes 16777216 | tf_op jit(solution)/shard_map/pallas_call | solution.py:57
  121.0 4.7 %collective-permute-done.38.refs_3_ = bf16[4,128,256]{2,1,0:T(8,128)(2,1)S(1)} collective-permute-done((bf16[4,128,256]{2,1,0:T(8,128)(2,1)S(1)}, bf16[4,128,256]{2,1,0:T(8,128)(2,1)S(1)}, u32[]{:S(2)}, u32[]{:S(2)}) %collective-permute-start.38) | collective-permute-done | bytes 262176 | tf_op jit(solution)/shard_map/ppermute | solution.py:21
  126.3 3.6 %shard_map.109 = (f32[4,128,256]{2,1,0:T(8,128)S(1)}, bf16[4,128,256]{2,1,0:T(8,128)(2,1)S(1)}) custom-call(s32[8]{0:T(128)S(1)} %concatenate.3.s, bf16[1024,4096]{1,0:T(8,128)(2,1)S(1)} %shard_map.105.w_ref, bf16[4,128,256]{2,1,0:T(8,128)(2,1)S(1)} %shard_map.108.refs_0_, bf16[4,128,256]{2,1,0:T(8,128)(2,1)S(1)} %collective-permute-done.36.refs_1_, ...), custom_call_target="tpu_custom_call" | custom-call | flops 2147483648 | bytes 1048576 | tf_op jit(solution)/shard_map/pallas_call | solution.py:75
  132.0 3.8 %collective-permute-start.42 = (bf16[128,256]{1,0:T(8,128)(2,1)S(1)}, bf16[128,256]{1,0:T(8,128)(2,1)S(1)}, u32[]{:S(2)}, u32[]{:S(2)}) collective-permute-start(bf16[128,256]{1,0:T(8,128)(2,1)S(1)} %get-tuple-element.93), channel_id=1, source_target_pairs={{0,64},{16,80},{32,96},{48,112},{64,0},{80,16},{96,32},{112,48},{1... | collective-permute-start | bytes 196616 | tf_op jit(solution)/shard_map/ppermute | solution.py:21
  136.4 2.9 %collective-permute-done.42 = bf16[128,256]{1,0:T(8,128)(2,1)S(1)} collective-permute-done((bf16[128,256]{1,0:T(8,128)(2,1)S(1)}, bf16[128,256]{1,0:T(8,128)(2,1)S(1)}, u32[]{:S(2)}, u32[]{:S(2)}) %collective-permute-start.42) | collective-permute-done | bytes 65568 | tf_op jit(solution)/shard_map/ppermute | solution.py:21
  139.3 2.0 collective-permute-done.41
  145.5 2.3 collective-permute-done.45.refs_3_
  149.9 2.0 shard_map.112
  151.9 2.1 collective-permute-start.50
  154.0 2.0 shard_map.113
  156.3 2.0 shard_map.114
  158.3 1.9 collective-permute-start.52
  160.2 2.0 shard_map.111
  162.6 3.8 %collective-permute-done.51 = bf16[4,256,128]{2,1,0:T(8,128)(2,1)S(1)} collective-permute-done((bf16[4,256,128]{2,1,0:T(8,128)(2,1)S(1)}, bf16[4,256,128]{2,1,0:T(8,128)(2,1)S(1)}, u32[]{:S(2)}, u32[]{:S(2)}) %collective-permute-start.51) | collective-permute-done | bytes 262176 | tf_op jit(solution)/shard_map/ppermute | solution.py:21
  171.7 3.9 %collective-permute-done.53 = bf16[2,256,128]{2,1,0:T(8,128)(2,1)S(1)} collective-permute-done((bf16[2,256,128]{2,1,0:T(8,128)(2,1)S(1)}, bf16[2,256,128]{2,1,0:T(8,128)(2,1)S(1)}, u32[]{:S(2)}, u32[]{:S(2)}) %collective-permute-start.53) | collective-permute-done | bytes 131104 | tf_op jit(solution)/shard_map/ppermute | solution.py:21
  178.7 2.3 collective-permute-start.57
  181.0 2.6 collective-permute-done.58.refs_3_
  186.5 2.2 copy-done.3
  188.7 2.6 shard_map.115
  192.2 1.9 collective-permute-start.64
  195.8 2.2 collective-permute-done.63
  198.0 3.5 %collective-permute-done.64 = bf16[2,256,128]{2,1,0:T(8,128)(2,1)S(1)} collective-permute-done((bf16[2,256,128]{2,1,0:T(8,128)(2,1)S(1)}, bf16[2,256,128]{2,1,0:T(8,128)(2,1)S(1)}, u32[]{:S(2)}, u32[]{:S(2)}) %collective-permute-start.64) | collective-permute-done | bytes 131104 | tf_op jit(solution)/shard_map/ppermute | solution.py:21
  202.3 3.6 %collective-permute-done.66 = bf16[256,128]{1,0:T(8,128)(2,1)S(1)} collective-permute-done((bf16[256,128]{1,0:T(8,128)(2,1)S(1)}, bf16[256,128]{1,0:T(8,128)(2,1)S(1)}, u32[]{:S(2)}, u32[]{:S(2)}) %collective-permute-start.66) | collective-permute-done | bytes 65568 | tf_op jit(solution)/shard_map/ppermute | solution.py:21
  206.6 2.1 collective-permute-start.68
  209.5 2.3 collective-permute-done.69.refs_3_
  214.2 2.6 shard_map.116
  219.1 2.0 collective-permute-start.76
  221.1 2.2 collective-permute-done.74.a
  225.0 1.8 collective-permute-done.76.c
  227.5 6.1 %collective-permute-done.77.got_ref = bf16[3,256,128]{2,1,0:T(8,128)(2,1)S(1)} collective-permute-done((bf16[3,256,128]{2,1,0:T(8,128)(2,1)S(1)}, bf16[3,256,128]{2,1,0:T(8,128)(2,1)S(1)}, u32[]{:S(2)}, u32[]{:S(2)}) %collective-permute-start.77) | collective-permute-done | bytes 196640 | tf_op jit(solution)/shard_map/ppermute | solution.py:21
  234.2 1.8 collective-permute-start.80
  237.8 2.7 collective-permute-done.80.refs_3_
  245.0 1.8 collective-permute-start.86
  246.8 2.2 collective-permute-start.87
  250.5 2.0 collective-permute-done.87
  256.2 2.3 collective-permute-done.90.refs_3_
  262.7 2.3 collective-permute-start.97
  266.9 6.2 %collective-permute-done.95.a = bf16[2,256,128]{2,1,0:T(8,128)(2,1)S(1)} collective-permute-done((bf16[2,256,128]{2,1,0:T(8,128)(2,1)S(1)}, bf16[2,256,128]{2,1,0:T(8,128)(2,1)S(1)}, u32[]{:S(2)}, u32[]{:S(2)}) %collective-permute-start.95) | collective-permute-done | bytes 131104 | tf_op jit(solution)/shard_map/ppermute | solution.py:21
  (212 shorter events, 106.5 us)
Async XLA Ops:
  4.2 8.9 %collective-permute-start.2 = (bf16[272,256]{1,0:T(8,128)(2,1)S(1)}, bf16[272,256]{1,0:T(8,128)(2,1)S(1)}, u32[]{:S(2)}, u32[]{:S(2)}) collective-permute-start(bf16[272,256]{1,0:T(8,128)(2,1)S(1)} %shard_map.96.refs_0_), channel_id=1, source_target_pairs={{0,3},{1,2},{2,1},{3,0},{4,7},{5,6},{6,5},{7,4},{8,11},{9,10},{10,... | collective-permute-start | bytes 417800 | tf_op jit(solution)/shard_map/ppermute | solution.py:21
  7.1 8.1 %collective-permute-start.1 = (bf16[272,256]{1,0:T(8,128)(2,1)S(1)}, bf16[272,256]{1,0:T(8,128)(2,1)S(1)}, u32[]{:S(2)}, u32[]{:S(2)}) collective-permute-start(bf16[272,256]{1,0:T(8,128)(2,1)S(1)} %shard_map.96.refs_0_), channel_id=1, source_target_pairs={{0,2},{1,3},{2,0},{3,1},{4,6},{5,7},{6,4},{7,5},{8,10},{9,11},{10,... | collective-permute-start | bytes 417800 | tf_op jit(solution)/shard_map/ppermute | solution.py:21
  7.9 7.3 %collective-permute-start = (bf16[272,256]{1,0:T(8,128)(2,1)S(1)}, bf16[272,256]{1,0:T(8,128)(2,1)S(1)}, u32[]{:S(2)}, u32[]{:S(2)}) collective-permute-start(bf16[272,256]{1,0:T(8,128)(2,1)S(1)} %shard_map.96.refs_0_), channel_id=1, source_target_pairs={{0,1},{1,0},{2,3},{3,2},{4,5},{5,4},{6,7},{7,6},{8,9},{9,8},{10,11... | collective-permute-start | bytes 417800 | tf_op jit(solution)/shard_map/ppermute | solution.py:21
  18.9 5.6 %collective-permute-start.4 = (bf16[128,256]{1,0:T(8,128)(2,1)S(1)}, bf16[128,256]{1,0:T(8,128)(2,1)S(1)}, u32[]{:S(2)}, u32[]{:S(2)}) collective-permute-start(bf16[128,256]{1,0:T(8,128)(2,1)S(1)} %get-tuple-element.104), channel_id=1, source_target_pairs={{0,32},{16,48},{32,0},{48,16},{64,96},{80,112},{96,64},{112,80},{1... | collective-permute-start | bytes 196616 | tf_op jit(solution)/shard_map/ppermute | solution.py:21
  20.9 7.1 %collective-permute-start.6 = (bf16[128,256]{1,0:T(8,128)(2,1)S(1)}, bf16[128,256]{1,0:T(8,128)(2,1)S(1)}, u32[]{:S(2)}, u32[]{:S(2)}) collective-permute-start(bf16[128,256]{1,0:T(8,128)(2,1)S(1)} %get-tuple-element.105), channel_id=1, source_target_pairs={{0,64},{16,80},{32,96},{48,112},{64,0},{80,16},{96,32},{112,48},{1... | collective-permute-start | bytes 196616 | tf_op jit(solution)/shard_map/ppermute | solution.py:21
  24.5 5.5 %collective-permute-start.5 = (bf16[128,256]{1,0:T(8,128)(2,1)S(1)}, bf16[128,256]{1,0:T(8,128)(2,1)S(1)}, u32[]{:S(2)}, u32[]{:S(2)}) collective-permute-start(bf16[128,256]{1,0:T(8,128)(2,1)S(1)} %get-tuple-element.106), channel_id=1, source_target_pairs={{0,96},{16,112},{32,64},{48,80},{64,32},{80,48},{96,0},{112,16},{1... | collective-permute-start | bytes 196616 | tf_op jit(solution)/shard_map/ppermute | solution.py:21
  30.0 6.1 %collective-permute-start.9 = (bf16[128,256]{1,0:T(8,128)(2,1)S(1)}, bf16[128,256]{1,0:T(8,128)(2,1)S(1)}, u32[]{:S(2)}, u32[]{:S(2)}) collective-permute-start(bf16[128,256]{1,0:T(8,128)(2,1)S(1)} %get-tuple-element.89.refs_0_), channel_id=1, source_target_pairs={{0,3},{1,2},{2,1},{3,0},{4,7},{5,6},{6,5},{7,4},{8,11},{9,10},{10,... | collective-permute-start | bytes 196616 | tf_op jit(solution)/shard_map/ppermute | solution.py:21
  32.2 5.8 %collective-permute-start.8 = (bf16[128,256]{1,0:T(8,128)(2,1)S(1)}, bf16[128,256]{1,0:T(8,128)(2,1)S(1)}, u32[]{:S(2)}, u32[]{:S(2)}) collective-permute-start(bf16[128,256]{1,0:T(8,128)(2,1)S(1)} %get-tuple-element.89.refs_0_), channel_id=1, source_target_pairs={{0,2},{1,3},{2,0},{3,1},{4,6},{5,7},{6,4},{7,5},{8,10},{9,11},{10,... | collective-permute-start | bytes 196616 | tf_op jit(solution)/shard_map/ppermute | solution.py:21
  33.0 5.0 %collective-permute-start.7 = (bf16[128,256]{1,0:T(8,128)(2,1)S(1)}, bf16[128,256]{1,0:T(8,128)(2,1)S(1)}, u32[]{:S(2)}, u32[]{:S(2)}) collective-permute-start(bf16[128,256]{1,0:T(8,128)(2,1)S(1)} %get-tuple-element.89.refs_0_), channel_id=1, source_target_pairs={{0,1},{1,0},{2,3},{3,2},{4,5},{5,4},{6,7},{7,6},{8,9},{9,8},{10,11... | collective-permute-start | bytes 196616 | tf_op jit(solution)/shard_map/ppermute | solution.py:21
  41.4 6.4 %collective-permute-start.11 = (bf16[128,256]{1,0:T(8,128)(2,1)S(1)}, bf16[128,256]{1,0:T(8,128)(2,1)S(1)}, u32[]{:S(2)}, u32[]{:S(2)}) collective-permute-start(bf16[128,256]{1,0:T(8,128)(2,1)S(1)} %get-tuple-element.101), channel_id=1, source_target_pairs={{0,32},{16,48},{32,0},{48,16},{64,96},{80,112},{96,64},{112,80},{1... | collective-permute-start | bytes 196616 | tf_op jit(solution)/shard_map/ppermute | solution.py:21
  41.5 6.3 %collective-permute-start.13 = (bf16[128,256]{1,0:T(8,128)(2,1)S(1)}, bf16[128,256]{1,0:T(8,128)(2,1)S(1)}, u32[]{:S(2)}, u32[]{:S(2)}) collective-permute-start(bf16[128,256]{1,0:T(8,128)(2,1)S(1)} %get-tuple-element.102), channel_id=1, source_target_pairs={{0,64},{16,80},{32,96},{48,112},{64,0},{80,16},{96,32},{112,48},{1... | collective-permute-start | bytes 196616 | tf_op jit(solution)/shard_map/ppermute | solution.py:21
  43.3 5.5 %collective-permute-start.12 = (bf16[128,256]{1,0:T(8,128)(2,1)S(1)}, bf16[128,256]{1,0:T(8,128)(2,1)S(1)}, u32[]{:S(2)}, u32[]{:S(2)}) collective-permute-start(bf16[128,256]{1,0:T(8,128)(2,1)S(1)} %get-tuple-element.103), channel_id=1, source_target_pairs={{0,96},{16,112},{32,64},{48,80},{64,32},{80,48},{96,0},{112,16},{1... | collective-permute-start | bytes 196616 | tf_op jit(solution)/shard_map/ppermute | solution.py:21
  46.2 5.8 %collective-permute-start.15 = (bf16[288,256]{1,0:T(8,128)(2,1)S(1)}, bf16[288,256]{1,0:T(8,128)(2,1)S(1)}, u32[]{:S(2)}, u32[]{:S(2)}) collective-permute-start(bf16[288,256]{1,0:T(8,128)(2,1)S(1)} %get-tuple-element.45), channel_id=1, source_target_pairs={{0,4},{1,5},{2,6},{3,7},{4,0},{5,1},{6,2},{7,3},{8,12},{9,13},{10,... | collective-permute-start | bytes 442376 | tf_op jit(solution)/shard_map/ppermute | solution.py:21
  53.8 7.5 %collective-permute-start.18 = (bf16[2,128,256]{2,1,0:T(8,128)(2,1)S(1)}, bf16[2,128,256]{2,1,0:T(8,128)(2,1)S(1)}, u32[]{:S(2)}, u32[]{:S(2)}) collective-permute-start(bf16[2,128,256]{2,1,0:T(8,128)(2,1)S(1)} %get-tuple-element.46.refs_0_), channel_id=1, source_target_pairs={{0,3},{1,2},{2,1},{3,0},{4,7},{5,6},{6,5},{7,4},{8,11},{9,10},{10,... | collective-permute-start | bytes 393224 | tf_op jit(solution)/shard_map/ppermute | solution.py:21
  55.3 7.0 %collective-permute-start.17 = (bf16[2,128,256]{2,1,0:T(8,128)(2,1)S(1)}, bf16[2,128,256]{2,1,0:T(8,128)(2,1)S(1)}, u32[]{:S(2)}, u32[]{:S(2)}) collective-permute-start(bf16[2,128,256]{2,1,0:T(8,128)(2,1)S(1)} %get-tuple-element.46.refs_0_), channel_id=1, source_target_pairs={{0,2},{1,3},{2,0},{3,1},{4,6},{5,7},{6,4},{7,5},{8,10},{9,11},{10,... | collective-permute-start | bytes 393224 | tf_op jit(solution)/shard_map/ppermute | solution.py:21
  56.4 6.4 %collective-permute-start.16 = (bf16[2,128,256]{2,1,0:T(8,128)(2,1)S(1)}, bf16[2,128,256]{2,1,0:T(8,128)(2,1)S(1)}, u32[]{:S(2)}, u32[]{:S(2)}) collective-permute-start(bf16[2,128,256]{2,1,0:T(8,128)(2,1)S(1)} %get-tuple-element.46.refs_0_), channel_id=1, source_target_pairs={{0,1},{1,0},{2,3},{3,2},{4,5},{5,4},{6,7},{7,6},{8,9},{9,8},{10,11... | collective-permute-start | bytes 393224 | tf_op jit(solution)/shard_map/ppermute | solution.py:21
  68.8 4.8 %collective-permute-start.20 = (bf16[128,256]{1,0:T(8,128)(2,1)S(1)}, bf16[128,256]{1,0:T(8,128)(2,1)S(1)}, u32[]{:S(2)}, u32[]{:S(2)}) collective-permute-start(bf16[128,256]{1,0:T(8,128)(2,1)S(1)} %get-tuple-element.98), channel_id=1, source_target_pairs={{0,32},{16,48},{32,0},{48,16},{64,96},{80,112},{96,64},{112,80},{1... | collective-permute-start | bytes 196616 | tf_op jit(solution)/shard_map/ppermute | solution.py:21
  69.0 7.4 %collective-permute-start.22 = (bf16[128,256]{1,0:T(8,128)(2,1)S(1)}, bf16[128,256]{1,0:T(8,128)(2,1)S(1)}, u32[]{:S(2)}, u32[]{:S(2)}) collective-permute-start(bf16[128,256]{1,0:T(8,128)(2,1)S(1)} %get-tuple-element.99), channel_id=1, source_target_pairs={{0,64},{16,80},{32,96},{48,112},{64,0},{80,16},{96,32},{112,48},{1... | collective-permute-start | bytes 196616 | tf_op jit(solution)/shard_map/ppermute | solution.py:21
  72.8 5.5 %collective-permute-start.21 = (bf16[128,256]{1,0:T(8,128)(2,1)S(1)}, bf16[128,256]{1,0:T(8,128)(2,1)S(1)}, u32[]{:S(2)}, u32[]{:S(2)}) collective-permute-start(bf16[128,256]{1,0:T(8,128)(2,1)S(1)} %get-tuple-element.100), channel_id=1, source_target_pairs={{0,96},{16,112},{32,64},{48,80},{64,32},{80,48},{96,0},{112,16},{1... | collective-permute-start | bytes 196616 | tf_op jit(solution)/shard_map/ppermute | solution.py:21
  83.2 6.7 %collective-permute-start.26 = (bf16[2,128,256]{2,1,0:T(8,128)(2,1)S(1)}, bf16[2,128,256]{2,1,0:T(8,128)(2,1)S(1)}, u32[]{:S(2)}, u32[]{:S(2)}) collective-permute-start(bf16[2,128,256]{2,1,0:T(8,128)(2,1)S(1)} %shard_map.106.refs_0_), channel_id=1, source_target_pairs={{0,3},{1,2},{2,1},{3,0},{4,7},{5,6},{6,5},{7,4},{8,11},{9,10},{10,... | collective-permute-start | bytes 393224 | tf_op jit(solution)/shard_map/ppermute | solution.py:21
  84.7 6.5 %collective-permute-start.25 = (bf16[2,128,256]{2,1,0:T(8,128)(2,1)S(1)}, bf16[2,128,256]{2,1,0:T(8,128)(2,1)S(1)}, u32[]{:S(2)}, u32[]{:S(2)}) collective-permute-start(bf16[2,128,256]{2,1,0:T(8,128)(2,1)S(1)} %shard_map.106.refs_0_), channel_id=1, source_target_pairs={{0,2},{1,3},{2,0},{3,1},{4,6},{5,7},{6,4},{7,5},{8,10},{9,11},{10,... | collective-permute-start | bytes 393224 | tf_op jit(solution)/shard_map/ppermute | solution.py:21
  86.0 5.8 %collective-permute-start.24 = (bf16[2,128,256]{2,1,0:T(8,128)(2,1)S(1)}, bf16[2,128,256]{2,1,0:T(8,128)(2,1)S(1)}, u32[]{:S(2)}, u32[]{:S(2)}) collective-permute-start(bf16[2,128,256]{2,1,0:T(8,128)(2,1)S(1)} %shard_map.106.refs_0_), channel_id=1, source_target_pairs={{0,1},{1,0},{2,3},{3,2},{4,5},{5,4},{6,7},{7,6},{8,9},{9,8},{10,11... | collective-permute-start | bytes 393224 | tf_op jit(solution)/shard_map/ppermute | solution.py:21
  95.9 9.0 %collective-permute-start.28 = (bf16[128,256]{1,0:T(8,128)(2,1)S(1)}, bf16[128,256]{1,0:T(8,128)(2,1)S(1)}, u32[]{:S(2)}, u32[]{:S(2)}) collective-permute-start(bf16[128,256]{1,0:T(8,128)(2,1)S(1)} %get-tuple-element.95), channel_id=1, source_target_pairs={{0,32},{16,48},{32,0},{48,16},{64,96},{80,112},{96,64},{112,80},{1... | collective-permute-start | bytes 196616 | tf_op jit(solution)/shard_map/ppermute | solution.py:21
  95.9 8.9 %collective-permute-start.30 = (bf16[128,256]{1,0:T(8,128)(2,1)S(1)}, bf16[128,256]{1,0:T(8,128)(2,1)S(1)}, u32[]{:S(2)}, u32[]{:S(2)}) collective-permute-start(bf16[128,256]{1,0:T(8,128)(2,1)S(1)} %get-tuple-element.96), channel_id=1, source_target_pairs={{0,64},{16,80},{32,96},{48,112},{64,0},{80,16},{96,32},{112,48},{1... | collective-permute-start | bytes 196616 | tf_op jit(solution)/shard_map/ppermute | solution.py:21
  98.2 6.7 %collective-permute-start.29 = (bf16[128,256]{1,0:T(8,128)(2,1)S(1)}, bf16[128,256]{1,0:T(8,128)(2,1)S(1)}, u32[]{:S(2)}, u32[]{:S(2)}) collective-permute-start(bf16[128,256]{1,0:T(8,128)(2,1)S(1)} %get-tuple-element.97), channel_id=1, source_target_pairs={{0,96},{16,112},{32,64},{48,80},{64,32},{80,48},{96,0},{112,16},{1... | collective-permute-start | bytes 196616 | tf_op jit(solution)/shard_map/ppermute | solution.py:21
  100.6 7.9 %collective-permute-start.35 = (bf16[144,256]{1,0:T(8,128)(2,1)S(1)}, bf16[144,256]{1,0:T(8,128)(2,1)S(1)}, u32[]{:S(2)}, u32[]{:S(2)}) collective-permute-start(bf16[144,256]{1,0:T(8,128)(2,1)S(1)} %get-tuple-element.54), channel_id=1, source_target_pairs={{0,8},{1,9},{2,10},{3,11},{4,12},{5,13},{6,14},{7,15},{8,0},{9,1},... | collective-permute-start | bytes 221192 | tf_op jit(solution)/shard_map/ppermute | solution.py:21
  103.8 5.8 %collective-permute-start.34 = (bf16[144,256]{1,0:T(8,128)(2,1)S(1)}, bf16[144,256]{1,0:T(8,128)(2,1)S(1)}, u32[]{:S(2)}, u32[]{:S(2)}) collective-permute-start(bf16[144,256]{1,0:T(8,128)(2,1)S(1)} %get-tuple-element.54), channel_id=1, source_target_pairs={{0,12},{1,13},{2,14},{3,15},{4,8},{5,9},{6,10},{7,11},{8,4},{9,5},... | collective-permute-start | bytes 221192 | tf_op jit(solution)/shard_map/ppermute | solution.py:21
  104.9 6.2 %collective-permute-start.33 = (bf16[128,256]{1,0:T(8,128)(2,1)S(1)}, bf16[128,256]{1,0:T(8,128)(2,1)S(1)}, u32[]{:S(2)}, u32[]{:S(2)}) collective-permute-start(bf16[128,256]{1,0:T(8,128)(2,1)S(1)} %get-tuple-element.83), channel_id=1, source_target_pairs={{0,8},{1,9},{2,10},{3,11},{4,12},{5,13},{6,14},{7,15},{8,0},{9,1},... | collective-permute-start | bytes 196616 | tf_op jit(solution)/shard_map/ppermute | solution.py:21
  107.0 5.5 %collective-permute-start.32 = (bf16[128,256]{1,0:T(8,128)(2,1)S(1)}, bf16[128,256]{1,0:T(8,128)(2,1)S(1)}, u32[]{:S(2)}, u32[]{:S(2)}) collective-permute-start(bf16[128,256]{1,0:T(8,128)(2,1)S(1)} %get-tuple-element.83), channel_id=1, source_target_pairs={{0,12},{1,13},{2,14},{3,15},{4,8},{5,9},{6,10},{7,11},{8,4},{9,5},... | collective-permute-start | bytes 196616 | tf_op jit(solution)/shard_map/ppermute | solution.py:21
  113.2 12.6 %collective-permute-start.38 = (bf16[4,128,256]{2,1,0:T(8,128)(2,1)S(1)}, bf16[4,128,256]{2,1,0:T(8,128)(2,1)S(1)}, u32[]{:S(2)}, u32[]{:S(2)}) collective-permute-start(bf16[4,128,256]{2,1,0:T(8,128)(2,1)S(1)} %shard_map.108.refs_0_), channel_id=1, source_target_pairs={{0,3},{1,2},{2,1},{3,0},{4,7},{5,6},{6,5},{7,4},{8,11},{9,10},{10,... | collective-permute-start | bytes 786440 | tf_op jit(solution)/shard_map/ppermute | solution.py:21
  114.6 11.1 %collective-permute-start.37 = (bf16[4,128,256]{2,1,0:T(8,128)(2,1)S(1)}, bf16[4,128,256]{2,1,0:T(8,128)(2,1)S(1)}, u32[]{:S(2)}, u32[]{:S(2)}) collective-permute-start(bf16[4,128,256]{2,1,0:T(8,128)(2,1)S(1)} %shard_map.108.refs_0_), channel_id=1, source_target_pairs={{0,2},{1,3},{2,0},{3,1},{4,6},{5,7},{6,4},{7,5},{8,10},{9,11},{10,... | collective-permute-start | bytes 786440 | tf_op jit(solution)/shard_map/ppermute | solution.py:21
  115.9 10.4 %collective-permute-start.36 = (bf16[4,128,256]{2,1,0:T(8,128)(2,1)S(1)}, bf16[4,128,256]{2,1,0:T(8,128)(2,1)S(1)}, u32[]{:S(2)}, u32[]{:S(2)}) collective-permute-start(bf16[4,128,256]{2,1,0:T(8,128)(2,1)S(1)} %shard_map.108.refs_0_), channel_id=1, source_target_pairs={{0,1},{1,0},{2,3},{3,2},{4,5},{5,4},{6,7},{7,6},{8,9},{9,8},{10,11... | collective-permute-start | bytes 786440 | tf_op jit(solution)/shard_map/ppermute | solution.py:21
  131.6 4.8 %collective-permute-start.40 = (bf16[128,256]{1,0:T(8,128)(2,1)S(1)}, bf16[128,256]{1,0:T(8,128)(2,1)S(1)}, u32[]{:S(2)}, u32[]{:S(2)}) collective-permute-start(bf16[128,256]{1,0:T(8,128)(2,1)S(1)} %get-tuple-element.92), channel_id=1, source_target_pairs={{0,32},{16,48},{32,0},{48,16},{64,96},{80,112},{96,64},{112,80},{1... | collective-permute-start | bytes 196616 | tf_op jit(solution)/shard_map/ppermute | solution.py:21
  132.0 7.3 %collective-permute-start.42 = (bf16[128,256]{1,0:T(8,128)(2,1)S(1)}, bf16[128,256]{1,0:T(8,128)(2,1)S(1)}, u32[]{:S(2)}, u32[]{:S(2)}) collective-permute-start(bf16[128,256]{1,0:T(8,128)(2,1)S(1)} %get-tuple-element.93), channel_id=1, source_target_pairs={{0,64},{16,80},{32,96},{48,112},{64,0},{80,16},{96,32},{112,48},{1... | collective-permute-start | bytes 196616 | tf_op jit(solution)/shard_map/ppermute | solution.py:21
  135.8 5.5 %collective-permute-start.41 = (bf16[128,256]{1,0:T(8,128)(2,1)S(1)}, bf16[128,256]{1,0:T(8,128)(2,1)S(1)}, u32[]{:S(2)}, u32[]{:S(2)}) collective-permute-start(bf16[128,256]{1,0:T(8,128)(2,1)S(1)} %get-tuple-element.94), channel_id=1, source_target_pairs={{0,96},{16,112},{32,64},{48,80},{64,32},{80,48},{96,0},{112,16},{1... | collective-permute-start | bytes 196616 | tf_op jit(solution)/shard_map/ppermute | solution.py:21
  142.0 5.9 %collective-permute-start.45 = (bf16[256,128]{1,0:T(8,128)(2,1)S(1)}, bf16[256,128]{1,0:T(8,128)(2,1)S(1)}, u32[]{:S(2)}, u32[]{:S(2)}) collective-permute-start(bf16[256,128]{1,0:T(8,128)(2,1)S(1)} %shard_map.110.refs_0_), channel_id=1, source_target_pairs={{0,64},{16,80},{32,96},{48,112},{64,0},{80,16},{96,32},{112,48},{1... | collective-permute-start | bytes 196616 | tf_op jit(solution)/shard_map/ppermute | solution.py:21
  142.3 6.2 %collective-permute-start.44 = (bf16[256,128]{1,0:T(8,128)(2,1)S(1)}, bf16[256,128]{1,0:T(8,128)(2,1)S(1)}, u32[]{:S(2)}, u32[]{:S(2)}) collective-permute-start(bf16[256,128]{1,0:T(8,128)(2,1)S(1)} %shard_map.110.refs_0_), channel_id=1, source_target_pairs={{0,96},{16,112},{32,64},{48,80},{64,32},{80,48},{96,0},{112,16},{1... | collective-permute-start | bytes 196616 | tf_op jit(solution)/shard_map/ppermute | solution.py:21
  143.9 4.6 %collective-permute-start.43 = (bf16[256,128]{1,0:T(8,128)(2,1)S(1)}, bf16[256,128]{1,0:T(8,128)(2,1)S(1)}, u32[]{:S(2)}, u32[]{:S(2)}) collective-permute-start(bf16[256,128]{1,0:T(8,128)(2,1)S(1)} %shard_map.110.refs_0_), channel_id=1, source_target_pairs={{0,32},{16,48},{32,0},{48,16},{64,96},{80,112},{96,64},{112,80},{1... | collective-permute-start | bytes 196616 | tf_op jit(solution)/shard_map/ppermute | solution.py:21
  151.9 10.7 %collective-permute-start.50 = (bf16[4,256,128]{2,1,0:T(8,128)(2,1)S(1)}, bf16[4,256,128]{2,1,0:T(8,128)(2,1)S(1)}, u32[]{:S(2)}, u32[]{:S(2)}) collective-permute-start(bf16[4,256,128]{2,1,0:T(8,128)(2,1)S(1)} %shard_map.112), channel_id=1, source_target_pairs={{0,2},{1,3},{2,0},{3,1},{4,6},{5,7},{6,4},{7,5},{8,10},{9,11},{10,... | collective-permute-start | bytes 786440 | tf_op jit(solution)/shard_map/ppermute | solution.py:21
  156.0 10.4 %collective-permute-start.51 = (bf16[4,256,128]{2,1,0:T(8,128)(2,1)S(1)}, bf16[4,256,128]{2,1,0:T(8,128)(2,1)S(1)}, u32[]{:S(2)}, u32[]{:S(2)}) collective-permute-start(bf16[4,256,128]{2,1,0:T(8,128)(2,1)S(1)} %shard_map.113), channel_id=1, source_target_pairs={{0,1},{1,0},{2,3},{3,2},{4,5},{5,4},{6,7},{7,6},{8,9},{9,8},{10,11... | collective-permute-start | bytes 786440 | tf_op jit(solution)/shard_map/ppermute | solution.py:21
  158.3 9.7 %collective-permute-start.52 = (bf16[4,256,128]{2,1,0:T(8,128)(2,1)S(1)}, bf16[4,256,128]{2,1,0:T(8,128)(2,1)S(1)}, u32[]{:S(2)}, u32[]{:S(2)}) collective-permute-start(bf16[4,256,128]{2,1,0:T(8,128)(2,1)S(1)} %shard_map.114), channel_id=1, source_target_pairs={{0,3},{1,2},{2,1},{3,0},{4,7},{5,6},{6,5},{7,4},{8,11},{9,10},{10,... | collective-permute-start | bytes 786440 | tf_op jit(solution)/shard_map/ppermute | solution.py:21
  168.1 7.6 %collective-permute-start.53 = (bf16[2,256,128]{2,1,0:T(8,128)(2,1)S(1)}, bf16[2,256,128]{2,1,0:T(8,128)(2,1)S(1)}, u32[]{:S(2)}, u32[]{:S(2)}) collective-permute-start(bf16[2,256,128]{2,1,0:T(8,128)(2,1)S(1)} %get-tuple-element.81), channel_id=1, source_target_pairs={{0,8},{1,9},{2,10},{3,11},{4,12},{5,13},{6,14},{7,15},{8,0},{9,1},... | collective-permute-start | bytes 393224 | tf_op jit(solution)/shard_map/ppermute | solution.py:21
  169.7 7.5 %collective-permute-start.55 = (bf16[2,256,128]{2,1,0:T(8,128)(2,1)S(1)}, bf16[2,256,128]{2,1,0:T(8,128)(2,1)S(1)}, u32[]{:S(2)}, u32[]{:S(2)}) collective-permute-start(bf16[2,256,128]{2,1,0:T(8,128)(2,1)S(1)} %get-tuple-element.91), channel_id=1, source_target_pairs={{0,12},{1,13},{2,14},{3,15},{4,8},{5,9},{6,10},{7,11},{8,4},{9,5},... | collective-permute-start | bytes 393224 | tf_op jit(solution)/shard_map/ppermute | solution.py:21
  170.5 6.7 %collective-permute-start.54 = (bf16[2,256,128]{2,1,0:T(8,128)(2,1)S(1)}, bf16[2,256,128]{2,1,0:T(8,128)(2,1)S(1)}, u32[]{:S(2)}, u32[]{:S(2)}) collective-permute-start(bf16[2,256,128]{2,1,0:T(8,128)(2,1)S(1)} %get-tuple-element.91), channel_id=1, source_target_pairs={{0,4},{1,5},{2,6},{3,7},{4,0},{5,1},{6,2},{7,3},{8,12},{9,13},{10,... | collective-permute-start | bytes 393224 | tf_op jit(solution)/shard_map/ppermute | solution.py:21
  177.3 6.3 %collective-permute-start.58 = (bf16[256,128]{1,0:T(8,128)(2,1)S(1)}, bf16[256,128]{1,0:T(8,128)(2,1)S(1)}, u32[]{:S(2)}, u32[]{:S(2)}) collective-permute-start(bf16[256,128]{1,0:T(8,128)(2,1)S(1)} %get-tuple-element.78.refs_0_.down_ref), channel_id=1, source_target_pairs={{0,64},{16,80},{32,96},{48,112},{64,0},{80,16},{96,32},{112,48},{1... | collective-permute-start | bytes 196616 | tf_op jit(solution)/shard_map/ppermute | solution.py:21
  178.7 5.5 %collective-permute-start.57 = (bf16[256,128]{1,0:T(8,128)(2,1)S(1)}, bf16[256,128]{1,0:T(8,128)(2,1)S(1)}, u32[]{:S(2)}, u32[]{:S(2)}) collective-permute-start(bf16[256,128]{1,0:T(8,128)(2,1)S(1)} %get-tuple-element.78.refs_0_.down_ref), channel_id=1, source_target_pairs={{0,96},{16,112},{32,64},{48,80},{64,32},{80,48},{96,0},{112,16},{1... | collective-permute-start | bytes 196616 | tf_op jit(solution)/shard_map/ppermute | solution.py:21
  191.4 6.6 %collective-permute-start.63 = (bf16[2,256,128]{2,1,0:T(8,128)(2,1)S(1)}, bf16[2,256,128]{2,1,0:T(8,128)(2,1)S(1)}, u32[]{:S(2)}, u32[]{:S(2)}) collective-permute-start(bf16[2,256,128]{2,1,0:T(8,128)(2,1)S(1)} %get-tuple-element.58), channel_id=1, source_target_pairs={{0,1},{1,0},{2,3},{3,2},{4,5},{5,4},{6,7},{7,6},{8,9},{9,8},{10,11... | collective-permute-start | bytes 393224 | tf_op jit(solution)/shard_map/ppermute | solution.py:21
  192.2 9.3 %collective-permute-start.64 = (bf16[2,256,128]{2,1,0:T(8,128)(2,1)S(1)}, bf16[2,256,128]{2,1,0:T(8,128)(2,1)S(1)}, u32[]{:S(2)}, u32[]{:S(2)}) collective-permute-start(bf16[2,256,128]{2,1,0:T(8,128)(2,1)S(1)} %get-tuple-element.59), channel_id=1, source_target_pairs={{0,3},{1,2},{2,1},{3,0},{4,7},{5,6},{6,5},{7,4},{8,11},{9,10},{10,... | collective-permute-start | bytes 393224 | tf_op jit(solution)/shard_map/ppermute | solution.py:21
  194.1 7.4 %collective-permute-start.65 = (bf16[2,256,128]{2,1,0:T(8,128)(2,1)S(1)}, bf16[2,256,128]{2,1,0:T(8,128)(2,1)S(1)}, u32[]{:S(2)}, u32[]{:S(2)}) collective-permute-start(bf16[2,256,128]{2,1,0:T(8,128)(2,1)S(1)} %get-tuple-element.60), channel_id=1, source_target_pairs={{0,2},{1,3},{2,0},{3,1},{4,6},{5,7},{6,4},{7,5},{8,10},{9,11},{10,... | collective-permute-start | bytes 393224 | tf_op jit(solution)/shard_map/ppermute | solution.py:21
  206.0 5.9 %collective-permute-start.69 = (bf16[256,128]{1,0:T(8,128)(2,1)S(1)}, bf16[256,128]{1,0:T(8,128)(2,1)S(1)}, u32[]{:S(2)}, u32[]{:S(2)}) collective-permute-start(bf16[256,128]{1,0:T(8,128)(2,1)S(1)} %fusion.6.refs_0_), channel_id=1, source_target_pairs={{0,64},{16,80},{32,96},{48,112},{64,0},{80,16},{96,32},{112,48},{1... | collective-permute-start | bytes 196616 | tf_op jit(solution)/shard_map/ppermute | solution.py:21
  206.6 5.9 %collective-permute-start.68 = (bf16[256,128]{1,0:T(8,128)(2,1)S(1)}, bf16[256,128]{1,0:T(8,128)(2,1)S(1)}, u32[]{:S(2)}, u32[]{:S(2)}) collective-permute-start(bf16[256,128]{1,0:T(8,128)(2,1)S(1)} %fusion.6.refs_0_), channel_id=1, source_target_pairs={{0,96},{16,112},{32,64},{48,80},{64,32},{80,48},{96,0},{112,16},{1... | collective-permute-start | bytes 196616 | tf_op jit(solution)/shard_map/ppermute | solution.py:21
  216.9 6.4 %collective-permute-start.74 = (bf16[2,256,128]{2,1,0:T(8,128)(2,1)S(1)}, bf16[2,256,128]{2,1,0:T(8,128)(2,1)S(1)}, u32[]{:S(2)}, u32[]{:S(2)}) collective-permute-start(bf16[2,256,128]{2,1,0:T(8,128)(2,1)S(1)} %get-tuple-element.62), channel_id=1, source_target_pairs={{0,1},{1,0},{2,3},{3,2},{4,5},{5,4},{6,7},{7,6},{8,9},{9,8},{10,11... | collective-permute-start | bytes 393224 | tf_op jit(solution)/shard_map/ppermute | solution.py:21
  217.3 7.7 %collective-permute-start.75 = (bf16[2,256,128]{2,1,0:T(8,128)(2,1)S(1)}, bf16[2,256,128]{2,1,0:T(8,128)(2,1)S(1)}, u32[]{:S(2)}, u32[]{:S(2)}) collective-permute-start(bf16[2,256,128]{2,1,0:T(8,128)(2,1)S(1)} %get-tuple-element.63), channel_id=1, source_target_pairs={{0,3},{1,2},{2,1},{3,0},{4,7},{5,6},{6,5},{7,4},{8,11},{9,10},{10,... | collective-permute-start | bytes 393224 | tf_op jit(solution)/shard_map/ppermute | solution.py:21
  219.1 7.7 %collective-permute-start.76 = (bf16[2,256,128]{2,1,0:T(8,128)(2,1)S(1)}, bf16[2,256,128]{2,1,0:T(8,128)(2,1)S(1)}, u32[]{:S(2)}, u32[]{:S(2)}) collective-permute-start(bf16[2,256,128]{2,1,0:T(8,128)(2,1)S(1)} %get-tuple-element.64), channel_id=1, source_target_pairs={{0,2},{1,3},{2,0},{3,1},{4,6},{5,7},{6,4},{7,5},{8,10},{9,11},{10,... | collective-permute-start | bytes 393224 | tf_op jit(solution)/shard_map/ppermute | solution.py:21
  227.4 6.2 %collective-permute-start.77 = (bf16[3,256,128]{2,1,0:T(8,128)(2,1)S(1)}, bf16[3,256,128]{2,1,0:T(8,128)(2,1)S(1)}, u32[]{:S(2)}, u32[]{:S(2)}) collective-permute-start(bf16[3,256,128]{2,1,0:T(8,128)(2,1)S(1)} %get-tuple-element.66), channel_id=1, source_target_pairs={{0,4},{1,5},{2,6},{3,7},{4,0},{5,1},{6,2},{7,3},{8,12},{9,13},{10,... | collective-permute-start | bytes 589832 | tf_op jit(solution)/shard_map/ppermute | solution.py:21
  234.2 6.3 %collective-permute-start.80 = (bf16[256,128]{1,0:T(8,128)(2,1)S(1)}, bf16[256,128]{1,0:T(8,128)(2,1)S(1)}, u32[]{:S(2)}, u32[]{:S(2)}) collective-permute-start(bf16[256,128]{1,0:T(8,128)(2,1)S(1)} %get-tuple-element.67.refs_0_.refs_8_), channel_id=1, source_target_pairs={{0,64},{16,80},{32,96},{48,112},{64,0},{80,16},{96,32},{112,48},{1... | collective-permute-start | bytes 196616 | tf_op jit(solution)/shard_map/ppermute | solution.py:21
  236.0 5.5 %collective-permute-start.79 = (bf16[256,128]{1,0:T(8,128)(2,1)S(1)}, bf16[256,128]{1,0:T(8,128)(2,1)S(1)}, u32[]{:S(2)}, u32[]{:S(2)}) collective-permute-start(bf16[256,128]{1,0:T(8,128)(2,1)S(1)} %get-tuple-element.67.refs_0_.refs_8_), channel_id=1, source_target_pairs={{0,96},{16,112},{32,64},{48,80},{64,32},{80,48},{96,0},{112,16},{1... | collective-permute-start | bytes 196616 | tf_op jit(solution)/shard_map/ppermute | solution.py:21
  245.0 5.6 %collective-permute-start.86 = (bf16[1,256,128]{2,1,0:T(8,128)(2,1)S(1)}, bf16[1,256,128]{2,1,0:T(8,128)(2,1)S(1)}, u32[]{:S(2)}, u32[]{:S(2)}) collective-permute-start(bf16[1,256,128]{2,1,0:T(8,128)(2,1)S(1)} %get-tuple-element.70), channel_id=1, source_target_pairs={{0,3},{1,2},{2,1},{3,0},{4,7},{5,6},{6,5},{7,4},{8,11},{9,10},{10,... | collective-permute-start | bytes 196616 | tf_op jit(solution)/shard_map/ppermute | solution.py:21
  246.8 5.8 %collective-permute-start.87 = (bf16[1,256,128]{2,1,0:T(8,128)(2,1)S(1)}, bf16[1,256,128]{2,1,0:T(8,128)(2,1)S(1)}, u32[]{:S(2)}, u32[]{:S(2)}) collective-permute-start(bf16[1,256,128]{2,1,0:T(8,128)(2,1)S(1)} %get-tuple-element.71), channel_id=1, source_target_pairs={{0,2},{1,3},{2,0},{3,1},{4,6},{5,7},{6,4},{7,5},{8,10},{9,11},{10,... | collective-permute-start | bytes 196616 | tf_op jit(solution)/shard_map/ppermute | solution.py:21
  252.6 5.9 %collective-permute-start.90 = (bf16[256,128]{1,0:T(8,128)(2,1)S(1)}, bf16[256,128]{1,0:T(8,128)(2,1)S(1)}, u32[]{:S(2)}, u32[]{:S(2)}) collective-permute-start(bf16[256,128]{1,0:T(8,128)(2,1)S(1)} %fusion.4.refs_0_), channel_id=1, source_target_pairs={{0,64},{16,80},{32,96},{48,112},{64,0},{80,16},{96,32},{112,48},{1... | collective-permute-start | bytes 196616 | tf_op jit(solution)/shard_map/ppermute | solution.py:21
  253.8 5.5 %collective-permute-start.89 = (bf16[256,128]{1,0:T(8,128)(2,1)S(1)}, bf16[256,128]{1,0:T(8,128)(2,1)S(1)}, u32[]{:S(2)}, u32[]{:S(2)}) collective-permute-start(bf16[256,128]{1,0:T(8,128)(2,1)S(1)} %fusion.4.refs_0_), channel_id=1, source_target_pairs={{0,96},{16,112},{32,64},{48,80},{64,32},{80,48},{96,0},{112,16},{1... | collective-permute-start | bytes 196616 | tf_op jit(solution)/shard_map/ppermute | solution.py:21
  262.7 11.4 %collective-permute-start.97 = (bf16[3,256,128]{2,1,0:T(8,128)(2,1)S(1)}, bf16[3,256,128]{2,1,0:T(8,128)(2,1)S(1)}, u32[]{:S(2)}, u32[]{:S(2)}) collective-permute-start(bf16[3,256,128]{2,1,0:T(8,128)(2,1)S(1)} %get-tuple-element.75), channel_id=1, source_target_pairs={{0,2},{1,3},{2,0},{3,1},{4,6},{5,7},{6,4},{7,5},{8,10},{9,11},{10,... | collective-permute-start | bytes 589832 | tf_op jit(solution)/shard_map/ppermute | solution.py:21
  265.0 8.1 %collective-permute-start.95 = (bf16[2,256,128]{2,1,0:T(8,128)(2,1)S(1)}, bf16[2,256,128]{2,1,0:T(8,128)(2,1)S(1)}, u32[]{:S(2)}, u32[]{:S(2)}) collective-permute-start(bf16[2,256,128]{2,1,0:T(8,128)(2,1)S(1)} %get-tuple-element.73), channel_id=1, source_target_pairs={{0,1},{1,0},{2,3},{3,2},{4,5},{5,4},{6,7},{7,6},{8,9},{9,8},{10,11... | collective-permute-start | bytes 393224 | tf_op jit(solution)/shard_map/ppermute | solution.py:21
  265.1 9.0 %collective-permute-start.96 = (bf16[2,256,128]{2,1,0:T(8,128)(2,1)S(1)}, bf16[2,256,128]{2,1,0:T(8,128)(2,1)S(1)}, u32[]{:S(2)}, u32[]{:S(2)}) collective-permute-start(bf16[2,256,128]{2,1,0:T(8,128)(2,1)S(1)} %get-tuple-element.74), channel_id=1, source_target_pairs={{0,3},{1,2},{2,1},{3,0},{4,7},{5,6},{6,5},{7,4},{8,11},{9,10},{10,... | collective-permute-start | bytes 393224 | tf_op jit(solution)/shard_map/ppermute | solution.py:21
  (50 other events, 396.3 us)

commit v2 on v1

--- a/solution.py
+++ b/solution.py
@@ -246,11 +246,7 @@
         message = extra[1]
         rhs_ref = refs[4]
         message[:B] = rhs_ref[1].astype(BF)
-        message[B : 2 * B] = rhs_ref[0].astype(BF)
-        message[2 * B : 2 * B + 16] = jnp.full((16, C), s[T1].astype(F32), F32).astype(BF)
-        message[2 * B + 16 : 2 * B + 32] = jnp.full((16, C), s[T0].astype(F32), F32).astype(BF)
-        extra[2][:B] = rhs_ref[0].astype(BF)
-        extra[2][B:] = jnp.full((16, C), s[T0].astype(F32), F32).astype(BF)
+        message[B:] = jnp.full((16, C), s[T1].astype(F32), F32).astype(BF)
         for k in range(4):
             slot = (s[X] ^ k) * 8 + s[ROW]
             yield s[X] ^ k, (
@@ -259,16 +255,14 @@
                 + same(goal[k ^ 2], slot) * child[k ^ 2]
             )
 
-    own, others, update, to_y1, to_y3 = forward(
+    own, others, update, to_y1 = forward(
         w_low,
         scal,
         [*got, rhs],
         gather_low,
-        extras=[((B, C), F32), ((2 * B + 32, C), BF), ((B + 16, C), BF)],
+        extras=[((B, C), F32), ((B + 16, C), BF)],
     )
     from_y1 = swap(to_y1, "leaf", 4)
-    from_y3 = swap(to_y3, "leaf", 12)
-    from_y2 = swap(to_y3, "leaf", 8)
     y_low = reduce_row(own, others)
 
     def gather_plain(s, refs, extra):
@@ -283,7 +277,7 @@
     def extend_mid(s, own_ref, other_ref, rhs_ref, y1_ref, pair_ref, up_ref):
         position = (s[Y] & 1) * 4 + s[X]
         goal_own = jnp.full((1, C), s[T1].astype(F32), F32)
-        goal_other = y1_ref[2 * B : 2 * B + 16, :].astype(F32)[:1]
+        goal_other = y1_ref[B : B + 16, :].astype(F32)[:1]
 
         def landed(slot):
             return same(goal_own, slot) * own_ref[...] + same(goal_other, slot) * other_ref[
@@ -315,8 +309,17 @@
 
     (pair,) = small(join, [((2, B, C), BF)], scal, half, swap(half, "leaf", 4))
     own, others = forward(b_mid, scal, gather_x(pair), gather_mid)
-    children = update - reduce_row(own, others)
-    half = children.astype(BF)
+
+    def pack(s, up_ref, total_ref, rhs_ref, full_ref, out_ref):
+        full = up_ref[...] - total_ref[...]
+        full_ref[...] = full
+        out_ref[:B] = full.astype(BF)
+        out_ref[B : 2 * B] = rhs_ref[0].astype(BF)
+        out_ref[2 * B :] = jnp.full((16, C), s[T0].astype(F32), F32).astype(BF)
+
+    children, sent = small(
+        pack, [((B, C), F32), ((2 * B + 16, C), BF)], scal, update, reduce_row(own, others), rhs
+    )
 
     def flip(s, low_ref, mid_ref, low_out, mid_out):
         low_out[...] = low_ref[...].T
@@ -324,27 +327,25 @@
 
     turned_low, turned_mid = small(flip, [((C, B), F32)] * 2, scal, y_low, y_mid)
 
-    moved = [swap(half, "leaf", 4 * k) for k in STEPS]
-
-    def extend_top(s, own_ref, m1, m3, m2, rhs_ref, y1_ref, y3_ref, y2_ref, out_ref):
-        child = [own_ref[...], m1[...].astype(F32), m2[...].astype(F32), m3[...].astype(F32)]
-        base = [rhs_ref[0], y1_ref[B : 2 * B, :], y2_ref[:B, :], y3_ref[:B, :]]
-        goal = [
-            jnp.full((1, C), s[T0].astype(F32), F32),
-            y1_ref[2 * B + 16 : 2 * B + 32, :].astype(F32)[:1],
-            y2_ref[B : B + 16, :].astype(F32)[:1],
-            y3_ref[B : B + 16, :].astype(F32)[:1],
+    moved = [swap(sent, "leaf", 4 * k) for k in (1, 2, 3)]
+
+    def extend_top(s, own_ref, m1, m2, m3, rhs_ref, out_ref):
+        others = (m1, m2, m3)
+        child = [own_ref[...]] + [m[:B, :].astype(F32) for m in others]
+        base = [rhs_ref[0]] + [m[B : 2 * B, :].astype(F32) for m in others]
+        goal = [jnp.full((1, C), s[T0].astype(F32), F32)] + [
+            m[2 * B :, :].astype(F32)[:1] for m in others
         ]
         for k in range(4):
             slot = ((s[Y] ^ k) * 4 + s[X]) * 8 + s[ROW]
             out_ref[k] = (
-                base[k].astype(F32)
+                base[k]
                 + same(goal[k], slot) * child[k]
                 + same(goal[k ^ 2], slot) * child[k ^ 2]
             ).astype(BF)
 
     (column,) = small(
-        extend_top, [((4, B, C), BF)], scal, children, *moved, rhs, from_y1, from_y3, from_y2
+        extend_top, [((4, B, C), BF)], scal, children, *moved, rhs
     )
 
     def gather_top(s, refs, extra):
@@ -358,6 +359,7 @@
         out_ref[...] = total_ref[...].T.astype(BF)
 
     (half,) = small(turn, [((C, B), BF)], scal, reduce_row(own, others))
+    b_mid = relay(lax.optimization_barrier((couple_mid, half))[0])
     pieces = gather_row(half)
     got = [swap(transposed(w_top, scal, pieces, only=k)[0], "leaf", k) for k in (2, 1, 3)]
     (own,) = transposed(w_top, scal, pieces, only=0)
@@ -374,6 +376,7 @@
     half = down_mid.astype(BF)
 
     down_half = half
+    w_mid = relay(lax.optimization_barrier((inv_mid, half))[0])
     parts = transposed(b_mid, scal, gather_row(half))
     got = [swap(parts[k], "leaf", k) for k in STEPS]
     full, cross = [parts[0][j] + sum(g[j].astype(F32) for g in got) for j in range(2)]

time: 277 us -> 280 us (1.011)
  Pallas kernels: 48.1 us -> 53.7 us
    pallas_call x5 -> x7, Pallas kernels: 12.5 us -> 17.5 us  [relay(): pl.pallas_call(functools.partial(relay_body, groups), grid=(tiles,), out_...]
    unnamed x33 -> x29, local copies, waits for them, and re-layouts: 8.49 us -> 6.47 us
    ppermute x98 -> x96, starting transfers between devices: 102 us -> 101 us  [swap(): return lax.ppermute(value, axis, [(i, i ^ mask) for i in range(count)])]
    ppermute x98 -> x96, waiting for transfers between devices: 114 us -> 116 us  [swap(): return lax.ppermute(value, axis, [(i, i ^ mask) for i in range(count)])]
    pallas_call x8 -> x9, Pallas kernels: 5.85 us -> 6.42 us  [small(): pl.pallas_call(body, out_shape=[jax.ShapeDtypeStruct(*o) for o in outs],...]
  transfers between devices with their start and end apart: 98 -> 96, of which waited for: 71 -> 65; matrix products, arithmetic and copies ran while one was open for 0% -> 0% of each run, Pallas kernels for 7% -> 9%
where the time goes in v2:
time: 280 us; the launch traced here: 279 us
  waiting for transfers between devices  116 us (41%)
  starting transfers between devices  101 us (36%)
  Pallas kernels  53.7 us (19%)
  local copies, waits for them, and re-layouts  7.2 us (3%)
    ppermute x96, waiting for transfers between devices, swap(): return lax.ppermute(value, axis, [(i, i ^ mask) for i in range(count)])  116 us
    ppermute x96, starting transfers between devices, swap(): return lax.ppermute(value, axis, [(i, i ^ mask) for i in range(count)])  101 us
    pallas_call x13, Pallas kernels, call(): pl.pallas_call(body, out_shape=[jax.ShapeDtypeStruct(*o) for o in outs],...  28.8 us
    pallas_call x7, Pallas kernels, relay(): pl.pallas_call(functools.partial(relay_body, groups), grid=(tiles,), out_...  17.5 us
    unnamed x29, local copies, waits for them, and re-layouts  6.47 us
    pallas_call x9, Pallas kernels, small(): pl.pallas_call(body, out_shape=[jax.ShapeDtypeStruct(*o) for o in outs],...  6.42 us
  transfers between devices with their start and end apart: 96, of which 65 were waited for; matrix products, arithmetic and copies ran while one was open for 0% of the time, Pallas kernels for 9%

profile of v2, /device:TPU:0, one launch (start us, length us, event | category | flops | bytes accessed | tf_op | source)
XLA Modules:
  0.0 279.2 jit_solution(11608313160734883661)
XLA Ops:
  4.2 2.9 %collective-permute-start.2 = (bf16[272,256]{1,0:T(8,128)(2,1)S(1)}, bf16[272,256]{1,0:T(8,128)(2,1)S(1)}, u32[]{:S(2)}, u32[]{:S(2)}) collective-permute-start(bf16[272,256]{1,0:T(8,128)(2,1)S(1)} %shard_map.96.refs_0_), channel_id=1, source_target_pairs={{0,3},{1,2},{2,1},{3,0},{4,7},{5,6},{6,5},{7,4},{8,11},{9,10},{10,... | collective-permute-start | bytes 417800 | tf_op jit(solution)/shard_map/ppermute | solution.py:21
  10.7 1.9 shard_map.95.w_ref
  13.1 2.2 collective-permute-done.1.refs_2_
  15.3 1.9 shard_map.97
  18.9 2.0 collective-permute-start.4
  20.9 3.6 %collective-permute-start.6 = (bf16[128,256]{1,0:T(8,128)(2,1)S(1)}, bf16[128,256]{1,0:T(8,128)(2,1)S(1)}, u32[]{:S(2)}, u32[]{:S(2)}) collective-permute-start(bf16[128,256]{1,0:T(8,128)(2,1)S(1)} %get-tuple-element.109), channel_id=1, source_target_pairs={{0,64},{16,80},{32,96},{48,112},{64,0},{80,16},{96,32},{112,48},{1... | collective-permute-start | bytes 196616 | tf_op jit(solution)/shard_map/ppermute | solution.py:21
  24.5 3.5 %collective-permute-done.6 = bf16[128,256]{1,0:T(8,128)(2,1)S(1)} collective-permute-done((bf16[128,256]{1,0:T(8,128)(2,1)S(1)}, bf16[128,256]{1,0:T(8,128)(2,1)S(1)}, u32[]{:S(2)}, u32[]{:S(2)}) %collective-permute-start.6) | collective-permute-done | bytes 65568 | tf_op jit(solution)/shard_map/ppermute | solution.py:21
  28.0 2.0 collective-permute-done.5
  30.0 2.2 collective-permute-start.9
  34.2 1.9 shard_map.99.w_ref
  43.3 2.9 %collective-permute-start.12 = (bf16[128,256]{1,0:T(8,128)(2,1)S(1)}, bf16[128,256]{1,0:T(8,128)(2,1)S(1)}, u32[]{:S(2)}, u32[]{:S(2)}) collective-permute-start(bf16[128,256]{1,0:T(8,128)(2,1)S(1)} %get-tuple-element.107), channel_id=1, source_target_pairs={{0,96},{16,112},{32,64},{48,80},{64,32},{80,48},{96,0},{112,16},{1... | collective-permute-start | bytes 196616 | tf_op jit(solution)/shard_map/ppermute | solution.py:21
  50.6 2.6 collective-permute-done.14.other_ref
  58.0 2.5 shard_map.98.w_ref
  62.3 2.4 shard_map.102
  67.0 3.8 %collective-permute-start.22 = (bf16[128,256]{1,0:T(8,128)(2,1)S(1)}, bf16[128,256]{1,0:T(8,128)(2,1)S(1)}, u32[]{:S(2)}, u32[]{:S(2)}) collective-permute-start(bf16[128,256]{1,0:T(8,128)(2,1)S(1)} %get-tuple-element.103), channel_id=1, source_target_pairs={{0,64},{16,80},{32,96},{48,112},{64,0},{80,16},{96,32},{112,48},{1... | collective-permute-start | bytes 196616 | tf_op jit(solution)/shard_map/ppermute | solution.py:21
  71.1 3.2 %collective-permute-done.22 = bf16[128,256]{1,0:T(8,128)(2,1)S(1)} collective-permute-done((bf16[128,256]{1,0:T(8,128)(2,1)S(1)}, bf16[128,256]{1,0:T(8,128)(2,1)S(1)}, u32[]{:S(2)}, u32[]{:S(2)}) %collective-permute-start.22) | collective-permute-done | bytes 65568 | tf_op jit(solution)/shard_map/ppermute | solution.py:21
  74.4 2.0 collective-permute-done.21
  78.0 2.7 collective-permute-done.23.b_ref
  85.4 2.5 shard_map.105.w_ref
  89.8 2.4 shard_map.107
  95.7 2.9 %collective-permute-start.29 = (bf16[128,256]{1,0:T(8,128)(2,1)S(1)}, bf16[128,256]{1,0:T(8,128)(2,1)S(1)}, u32[]{:S(2)}, u32[]{:S(2)}) collective-permute-start(bf16[128,256]{1,0:T(8,128)(2,1)S(1)} %get-tuple-element.101), channel_id=1, source_target_pairs={{0,96},{16,112},{32,64},{48,80},{64,32},{80,48},{96,0},{112,16},{1... | collective-permute-start | bytes 196616 | tf_op jit(solution)/shard_map/ppermute | solution.py:21
  101.8 3.1 %collective-permute-start.33 = (bf16[272,256]{1,0:T(8,128)(2,1)S(1)}, bf16[272,256]{1,0:T(8,128)(2,1)S(1)}, u32[]{:S(2)}, u32[]{:S(2)}) collective-permute-start(bf16[272,256]{1,0:T(8,128)(2,1)S(1)} %get-tuple-element.57), channel_id=1, source_target_pairs={{0,12},{1,13},{2,14},{3,15},{4,8},{5,9},{6,10},{7,11},{8,4},{9,5},... | collective-permute-start | bytes 417800 | tf_op jit(solution)/shard_map/ppermute | solution.py:21
  106.1 4.1 %collective-permute-done.33.m3 = bf16[272,256]{1,0:T(8,128)(2,1)S(1)} collective-permute-done((bf16[272,256]{1,0:T(8,128)(2,1)S(1)}, bf16[272,256]{1,0:T(8,128)(2,1)S(1)}, u32[]{:S(2)}, u32[]{:S(2)}) %collective-permute-start.33) | collective-permute-done | bytes 139296 | tf_op jit(solution)/shard_map/ppermute | solution.py:21
  110.2 2.2 collective-permute-done.32.m2
  117.2 3.6 %shard_map.104.w_ref = bf16[1024,4096]{1,0:T(8,128)(2,1)S(1)} custom-call(bf16[32768,128]{1,0:T(8,128)(2,1)S(1)} %bitcast.110, bf16[32768,128]{1,0:T(8,128)(2,1)S(1)} %bitcast.111), custom_call_target="tpu_custom_call" | custom-call | flops 2147483648 | bytes 16777216 | tf_op jit(solution)/shard_map/pallas_call | solution.py:57
  120.9 4.7 %collective-permute-done.36.refs_3_ = bf16[4,128,256]{2,1,0:T(8,128)(2,1)S(1)} collective-permute-done((bf16[4,128,256]{2,1,0:T(8,128)(2,1)S(1)}, bf16[4,128,256]{2,1,0:T(8,128)(2,1)S(1)}, u32[]{:S(2)}, u32[]{:S(2)}) %collective-permute-start.36) | collective-permute-done | bytes 262176 | tf_op jit(solution)/shard_map/ppermute | solution.py:21
  126.2 3.6 %shard_map.110 = (f32[4,128,256]{2,1,0:T(8,128)S(1)}, bf16[4,128,256]{2,1,0:T(8,128)(2,1)S(1)}) custom-call(s32[8]{0:T(128)S(1)} %concatenate.3.s, bf16[1024,4096]{1,0:T(8,128)(2,1)S(1)} %shard_map.104.w_ref, bf16[4,128,256]{2,1,0:T(8,128)(2,1)S(1)} %shard_map.109.refs_0_, bf16[4,128,256]{2,1,0:T(8,128)(2,1)S(1)} %collective-permute-done.34.refs_1_, ...), custom_call_target="tpu_custom_call" | custom-call | flops 2147483648 | bytes 1048576 | tf_op jit(solution)/shard_map/pallas_call | solution.py:75
  131.8 3.3 %collective-permute-start.40 = (bf16[128,256]{1,0:T(8,128)(2,1)S(1)}, bf16[128,256]{1,0:T(8,128)(2,1)S(1)}, u32[]{:S(2)}, u32[]{:S(2)}) collective-permute-start(bf16[128,256]{1,0:T(8,128)(2,1)S(1)} %get-tuple-element.97), channel_id=1, source_target_pairs={{0,64},{16,80},{32,96},{48,112},{64,0},{80,16},{96,32},{112,48},{1... | collective-permute-start | bytes 196616 | tf_op jit(solution)/shard_map/ppermute | solution.py:21
  136.3 2.3 collective-permute-done.40
  138.6 2.0 collective-permute-done.39
  142.1 2.0 collective-permute-start.42
  144.8 2.3 collective-permute-done.43.refs_3_
  149.6 2.0 shard_map.113
  151.6 2.1 collective-permute-start.48
  153.8 2.0 shard_map.114
  156.0 2.0 shard_map.115
  158.0 1.9 collective-permute-start.50
  159.9 2.0 shard_map.112
  162.4 3.5 %collective-permute-done.49 = bf16[4,256,128]{2,1,0:T(8,128)(2,1)S(1)} collective-permute-done((bf16[4,256,128]{2,1,0:T(8,128)(2,1)S(1)}, bf16[4,256,128]{2,1,0:T(8,128)(2,1)S(1)}, u32[]{:S(2)}, u32[]{:S(2)}) %collective-permute-start.49) | collective-permute-done | bytes 262176 | tf_op jit(solution)/shard_map/ppermute | solution.py:21
  167.7 2.8 collective-permute-start.51
  171.8 2.6 collective-permute-done.51
  174.4 2.7 collective-permute-done.53
  180.8 2.7 collective-permute-done.56.refs_3_
  185.0 2.2 copy-done.1
  187.1 2.5 shard_map.117.w_ref
  189.7 2.7 shard_map.118
  196.6 2.2 collective-permute-done.61
  198.8 3.9 %collective-permute-done.62 = bf16[2,256,128]{2,1,0:T(8,128)(2,1)S(1)} collective-permute-done((bf16[2,256,128]{2,1,0:T(8,128)(2,1)S(1)}, bf16[2,256,128]{2,1,0:T(8,128)(2,1)S(1)}, u32[]{:S(2)}, u32[]{:S(2)}) %collective-permute-start.62) | collective-permute-done | bytes 131104 | tf_op jit(solution)/shard_map/ppermute | solution.py:21
  204.2 2.9 %collective-permute-done.64 = bf16[256,128]{1,0:T(8,128)(2,1)S(1)} collective-permute-done((bf16[256,128]{1,0:T(8,128)(2,1)S(1)}, bf16[256,128]{1,0:T(8,128)(2,1)S(1)}, u32[]{:S(2)}, u32[]{:S(2)}) %collective-permute-start.64) | collective-permute-done | bytes 65568 | tf_op jit(solution)/shard_map/ppermute | solution.py:21
  210.7 2.3 collective-permute-done.67.refs_3_
  214.4 2.5 shard_map.116.w_ref
  217.0 2.7 shard_map.119
  221.9 2.0 collective-permute-start.74
  223.9 2.2 collective-permute-done.72.a
  226.1 3.6 %collective-permute-done.73.b = bf16[2,256,128]{2,1,0:T(8,128)(2,1)S(1)} collective-permute-done((bf16[2,256,128]{2,1,0:T(8,128)(2,1)S(1)}, bf16[2,256,128]{2,1,0:T(8,128)(2,1)S(1)}, u32[]{:S(2)}, u32[]{:S(2)}) %collective-permute-start.73) | collective-permute-done | bytes 131104 | tf_op jit(solution)/shard_map/ppermute | solution.py:21
  231.2 5.2 %collective-permute-done.75.got_ref = bf16[3,256,128]{2,1,0:T(8,128)(2,1)S(1)} collective-permute-done((bf16[3,256,128]{2,1,0:T(8,128)(2,1)S(1)}, bf16[3,256,128]{2,1,0:T(8,128)(2,1)S(1)}, u32[]{:S(2)}, u32[]{:S(2)}) %collective-permute-start.75) | collective-permute-done | bytes 196640 | tf_op jit(solution)/shard_map/ppermute | solution.py:21
  237.0 2.2 collective-permute-start.78
  240.7 2.4 collective-permute-done.78.refs_3_
  249.7 2.4 collective-permute-start.85
  253.6 1.9 collective-permute-done.85
  255.5 2.0 collective-permute-start.88
  259.1 2.8 collective-permute-done.88.refs_3_
  266.1 2.2 collective-permute-start.95
  270.3 6.1 %collective-permute-done.93.a = bf16[2,256,128]{2,1,0:T(8,128)(2,1)S(1)} collective-permute-done((bf16[2,256,128]{2,1,0:T(8,128)(2,1)S(1)}, bf16[2,256,128]{2,1,0:T(8,128)(2,1)S(1)}, u32[]{:S(2)}, u32[]{:S(2)}) %collective-permute-start.93) | collective-permute-done | bytes 131104 | tf_op jit(solution)/shard_map/ppermute | solution.py:21
  (207 shorter events, 105.8 us)
Async XLA Ops:
  4.2 8.9 %collective-permute-start.2 = (bf16[272,256]{1,0:T(8,128)(2,1)S(1)}, bf16[272,256]{1,0:T(8,128)(2,1)S(1)}, u32[]{:S(2)}, u32[]{:S(2)}) collective-permute-start(bf16[272,256]{1,0:T(8,128)(2,1)S(1)} %shard_map.96.refs_0_), channel_id=1, source_target_pairs={{0,3},{1,2},{2,1},{3,0},{4,7},{5,6},{6,5},{7,4},{8,11},{9,10},{10,... | collective-permute-start | bytes 417800 | tf_op jit(solution)/shard_map/ppermute | solution.py:21
  7.1 8.1 %collective-permute-start.1 = (bf16[272,256]{1,0:T(8,128)(2,1)S(1)}, bf16[272,256]{1,0:T(8,128)(2,1)S(1)}, u32[]{:S(2)}, u32[]{:S(2)}) collective-permute-start(bf16[272,256]{1,0:T(8,128)(2,1)S(1)} %shard_map.96.refs_0_), channel_id=1, source_target_pairs={{0,2},{1,3},{2,0},{3,1},{4,6},{5,7},{6,4},{7,5},{8,10},{9,11},{10,... | collective-permute-start | bytes 417800 | tf_op jit(solution)/shard_map/ppermute | solution.py:21
  7.9 7.3 %collective-permute-start = (bf16[272,256]{1,0:T(8,128)(2,1)S(1)}, bf16[272,256]{1,0:T(8,128)(2,1)S(1)}, u32[]{:S(2)}, u32[]{:S(2)}) collective-permute-start(bf16[272,256]{1,0:T(8,128)(2,1)S(1)} %shard_map.96.refs_0_), channel_id=1, source_target_pairs={{0,1},{1,0},{2,3},{3,2},{4,5},{5,4},{6,7},{7,6},{8,9},{9,8},{10,11... | collective-permute-start | bytes 417800 | tf_op jit(solution)/shard_map/ppermute | solution.py:21
  18.9 5.6 %collective-permute-start.4 = (bf16[128,256]{1,0:T(8,128)(2,1)S(1)}, bf16[128,256]{1,0:T(8,128)(2,1)S(1)}, u32[]{:S(2)}, u32[]{:S(2)}) collective-permute-start(bf16[128,256]{1,0:T(8,128)(2,1)S(1)} %get-tuple-element.108), channel_id=1, source_target_pairs={{0,32},{16,48},{32,0},{48,16},{64,96},{80,112},{96,64},{112,80},{1... | collective-permute-start | bytes 196616 | tf_op jit(solution)/shard_map/ppermute | solution.py:21
  20.9 7.1 %collective-permute-start.6 = (bf16[128,256]{1,0:T(8,128)(2,1)S(1)}, bf16[128,256]{1,0:T(8,128)(2,1)S(1)}, u32[]{:S(2)}, u32[]{:S(2)}) collective-permute-start(bf16[128,256]{1,0:T(8,128)(2,1)S(1)} %get-tuple-element.109), channel_id=1, source_target_pairs={{0,64},{16,80},{32,96},{48,112},{64,0},{80,16},{96,32},{112,48},{1... | collective-permute-start | bytes 196616 | tf_op jit(solution)/shard_map/ppermute | solution.py:21
  24.5 5.5 %collective-permute-start.5 = (bf16[128,256]{1,0:T(8,128)(2,1)S(1)}, bf16[128,256]{1,0:T(8,128)(2,1)S(1)}, u32[]{:S(2)}, u32[]{:S(2)}) collective-permute-start(bf16[128,256]{1,0:T(8,128)(2,1)S(1)} %get-tuple-element.110), channel_id=1, source_target_pairs={{0,96},{16,112},{32,64},{48,80},{64,32},{80,48},{96,0},{112,16},{1... | collective-permute-start | bytes 196616 | tf_op jit(solution)/shard_map/ppermute | solution.py:21
  30.0 6.1 %collective-permute-start.9 = (bf16[128,256]{1,0:T(8,128)(2,1)S(1)}, bf16[128,256]{1,0:T(8,128)(2,1)S(1)}, u32[]{:S(2)}, u32[]{:S(2)}) collective-permute-start(bf16[128,256]{1,0:T(8,128)(2,1)S(1)} %get-tuple-element.93.refs_0_), channel_id=1, source_target_pairs={{0,3},{1,2},{2,1},{3,0},{4,7},{5,6},{6,5},{7,4},{8,11},{9,10},{10,... | collective-permute-start | bytes 196616 | tf_op jit(solution)/shard_map/ppermute | solution.py:21
  32.2 5.8 %collective-permute-start.8 = (bf16[128,256]{1,0:T(8,128)(2,1)S(1)}, bf16[128,256]{1,0:T(8,128)(2,1)S(1)}, u32[]{:S(2)}, u32[]{:S(2)}) collective-permute-start(bf16[128,256]{1,0:T(8,128)(2,1)S(1)} %get-tuple-element.93.refs_0_), channel_id=1, source_target_pairs={{0,2},{1,3},{2,0},{3,1},{4,6},{5,7},{6,4},{7,5},{8,10},{9,11},{10,... | collective-permute-start | bytes 196616 | tf_op jit(solution)/shard_map/ppermute | solution.py:21
  33.0 5.0 %collective-permute-start.7 = (bf16[128,256]{1,0:T(8,128)(2,1)S(1)}, bf16[128,256]{1,0:T(8,128)(2,1)S(1)}, u32[]{:S(2)}, u32[]{:S(2)}) collective-permute-start(bf16[128,256]{1,0:T(8,128)(2,1)S(1)} %get-tuple-element.93.refs_0_), channel_id=1, source_target_pairs={{0,1},{1,0},{2,3},{3,2},{4,5},{5,4},{6,7},{7,6},{8,9},{9,8},{10,11... | collective-permute-start | bytes 196616 | tf_op jit(solution)/shard_map/ppermute | solution.py:21
  41.4 6.4 %collective-permute-start.11 = (bf16[128,256]{1,0:T(8,128)(2,1)S(1)}, bf16[128,256]{1,0:T(8,128)(2,1)S(1)}, u32[]{:S(2)}, u32[]{:S(2)}) collective-permute-start(bf16[128,256]{1,0:T(8,128)(2,1)S(1)} %get-tuple-element.105), channel_id=1, source_target_pairs={{0,32},{16,48},{32,0},{48,16},{64,96},{80,112},{96,64},{112,80},{1... | collective-permute-start | bytes 196616 | tf_op jit(solution)/shard_map/ppermute | solution.py:21
  41.5 6.3 %collective-permute-start.13 = (bf16[128,256]{1,0:T(8,128)(2,1)S(1)}, bf16[128,256]{1,0:T(8,128)(2,1)S(1)}, u32[]{:S(2)}, u32[]{:S(2)}) collective-permute-start(bf16[128,256]{1,0:T(8,128)(2,1)S(1)} %get-tuple-element.106), channel_id=1, source_target_pairs={{0,64},{16,80},{32,96},{48,112},{64,0},{80,16},{96,32},{112,48},{1... | collective-permute-start | bytes 196616 | tf_op jit(solution)/shard_map/ppermute | solution.py:21
  43.3 5.5 %collective-permute-start.12 = (bf16[128,256]{1,0:T(8,128)(2,1)S(1)}, bf16[128,256]{1,0:T(8,128)(2,1)S(1)}, u32[]{:S(2)}, u32[]{:S(2)}) collective-permute-start(bf16[128,256]{1,0:T(8,128)(2,1)S(1)} %get-tuple-element.107), channel_id=1, source_target_pairs={{0,96},{16,112},{32,64},{48,80},{64,32},{80,48},{96,0},{112,16},{1... | collective-permute-start | bytes 196616 | tf_op jit(solution)/shard_map/ppermute | solution.py:21
  53.8 6.7 %collective-permute-start.18 = (bf16[2,128,256]{2,1,0:T(8,128)(2,1)S(1)}, bf16[2,128,256]{2,1,0:T(8,128)(2,1)S(1)}, u32[]{:S(2)}, u32[]{:S(2)}) collective-permute-start(bf16[2,128,256]{2,1,0:T(8,128)(2,1)S(1)} %get-tuple-element.49.refs_0_), channel_id=1, source_target_pairs={{0,3},{1,2},{2,1},{3,0},{4,7},{5,6},{6,5},{7,4},{8,11},{9,10},{10,... | collective-permute-start | bytes 393224 | tf_op jit(solution)/shard_map/ppermute | solution.py:21
  55.3 6.5 %collective-permute-start.17 = (bf16[2,128,256]{2,1,0:T(8,128)(2,1)S(1)}, bf16[2,128,256]{2,1,0:T(8,128)(2,1)S(1)}, u32[]{:S(2)}, u32[]{:S(2)}) collective-permute-start(bf16[2,128,256]{2,1,0:T(8,128)(2,1)S(1)} %get-tuple-element.49.refs_0_), channel_id=1, source_target_pairs={{0,2},{1,3},{2,0},{3,1},{4,6},{5,7},{6,4},{7,5},{8,10},{9,11},{10,... | collective-permute-start | bytes 393224 | tf_op jit(solution)/shard_map/ppermute | solution.py:21
  56.4 5.9 %collective-permute-start.16 = (bf16[2,128,256]{2,1,0:T(8,128)(2,1)S(1)}, bf16[2,128,256]{2,1,0:T(8,128)(2,1)S(1)}, u32[]{:S(2)}, u32[]{:S(2)}) collective-permute-start(bf16[2,128,256]{2,1,0:T(8,128)(2,1)S(1)} %get-tuple-element.49.refs_0_), channel_id=1, source_target_pairs={{0,1},{1,0},{2,3},{3,2},{4,5},{5,4},{6,7},{7,6},{8,9},{9,8},{10,11... | collective-permute-start | bytes 393224 | tf_op jit(solution)/shard_map/ppermute | solution.py:21
  66.4 4.8 %collective-permute-start.20 = (bf16[128,256]{1,0:T(8,128)(2,1)S(1)}, bf16[128,256]{1,0:T(8,128)(2,1)S(1)}, u32[]{:S(2)}, u32[]{:S(2)}) collective-permute-start(bf16[128,256]{1,0:T(8,128)(2,1)S(1)} %get-tuple-element.102), channel_id=1, source_target_pairs={{0,32},{16,48},{32,0},{48,16},{64,96},{80,112},{96,64},{112,80},{1... | collective-permute-start | bytes 196616 | tf_op jit(solution)/shard_map/ppermute | solution.py:21
  67.0 7.4 %collective-permute-start.22 = (bf16[128,256]{1,0:T(8,128)(2,1)S(1)}, bf16[128,256]{1,0:T(8,128)(2,1)S(1)}, u32[]{:S(2)}, u32[]{:S(2)}) collective-permute-start(bf16[128,256]{1,0:T(8,128)(2,1)S(1)} %get-tuple-element.103), channel_id=1, source_target_pairs={{0,64},{16,80},{32,96},{48,112},{64,0},{80,16},{96,32},{112,48},{1... | collective-permute-start | bytes 196616 | tf_op jit(solution)/shard_map/ppermute | solution.py:21
  70.8 5.5 %collective-permute-start.21 = (bf16[128,256]{1,0:T(8,128)(2,1)S(1)}, bf16[128,256]{1,0:T(8,128)(2,1)S(1)}, u32[]{:S(2)}, u32[]{:S(2)}) collective-permute-start(bf16[128,256]{1,0:T(8,128)(2,1)S(1)} %get-tuple-element.104), channel_id=1, source_target_pairs={{0,96},{16,112},{32,64},{48,80},{64,32},{80,48},{96,0},{112,16},{1... | collective-permute-start | bytes 196616 | tf_op jit(solution)/shard_map/ppermute | solution.py:21
  81.3 6.7 %collective-permute-start.26 = (bf16[2,128,256]{2,1,0:T(8,128)(2,1)S(1)}, bf16[2,128,256]{2,1,0:T(8,128)(2,1)S(1)}, u32[]{:S(2)}, u32[]{:S(2)}) collective-permute-start(bf16[2,128,256]{2,1,0:T(8,128)(2,1)S(1)} %shard_map.106.refs_0_), channel_id=1, source_target_pairs={{0,3},{1,2},{2,1},{3,0},{4,7},{5,6},{6,5},{7,4},{8,11},{9,10},{10,... | collective-permute-start | bytes 393224 | tf_op jit(solution)/shard_map/ppermute | solution.py:21
  82.7 6.5 %collective-permute-start.25 = (bf16[2,128,256]{2,1,0:T(8,128)(2,1)S(1)}, bf16[2,128,256]{2,1,0:T(8,128)(2,1)S(1)}, u32[]{:S(2)}, u32[]{:S(2)}) collective-permute-start(bf16[2,128,256]{2,1,0:T(8,128)(2,1)S(1)} %shard_map.106.refs_0_), channel_id=1, source_target_pairs={{0,2},{1,3},{2,0},{3,1},{4,6},{5,7},{6,4},{7,5},{8,10},{9,11},{10,... | collective-permute-start | bytes 393224 | tf_op jit(solution)/shard_map/ppermute | solution.py:21
  84.0 5.8 %collective-permute-start.24 = (bf16[2,128,256]{2,1,0:T(8,128)(2,1)S(1)}, bf16[2,128,256]{2,1,0:T(8,128)(2,1)S(1)}, u32[]{:S(2)}, u32[]{:S(2)}) collective-permute-start(bf16[2,128,256]{2,1,0:T(8,128)(2,1)S(1)} %shard_map.106.refs_0_), channel_id=1, source_target_pairs={{0,1},{1,0},{2,3},{3,2},{4,5},{5,4},{6,7},{7,6},{8,9},{9,8},{10,11... | collective-permute-start | bytes 393224 | tf_op jit(solution)/shard_map/ppermute | solution.py:21
  93.9 4.9 %collective-permute-start.28 = (bf16[128,256]{1,0:T(8,128)(2,1)S(1)}, bf16[128,256]{1,0:T(8,128)(2,1)S(1)}, u32[]{:S(2)}, u32[]{:S(2)}) collective-permute-start(bf16[128,256]{1,0:T(8,128)(2,1)S(1)} %get-tuple-element.99), channel_id=1, source_target_pairs={{0,32},{16,48},{32,0},{48,16},{64,96},{80,112},{96,64},{112,80},{1... | collective-permute-start | bytes 196616 | tf_op jit(solution)/shard_map/ppermute | solution.py:21
  94.0 6.0 %collective-permute-start.30 = (bf16[128,256]{1,0:T(8,128)(2,1)S(1)}, bf16[128,256]{1,0:T(8,128)(2,1)S(1)}, u32[]{:S(2)}, u32[]{:S(2)}) collective-permute-start(bf16[128,256]{1,0:T(8,128)(2,1)S(1)} %get-tuple-element.100), channel_id=1, source_target_pairs={{0,64},{16,80},{32,96},{48,112},{64,0},{80,16},{96,32},{112,48},{1... | collective-permute-start | bytes 196616 | tf_op jit(solution)/shard_map/ppermute | solution.py:21
  95.7 5.5 %collective-permute-start.29 = (bf16[128,256]{1,0:T(8,128)(2,1)S(1)}, bf16[128,256]{1,0:T(8,128)(2,1)S(1)}, u32[]{:S(2)}, u32[]{:S(2)}) collective-permute-start(bf16[128,256]{1,0:T(8,128)(2,1)S(1)} %get-tuple-element.101), channel_id=1, source_target_pairs={{0,96},{16,112},{32,64},{48,80},{64,32},{80,48},{96,0},{112,16},{1... | collective-permute-start | bytes 196616 | tf_op jit(solution)/shard_map/ppermute | solution.py:21
  101.8 8.3 %collective-permute-start.33 = (bf16[272,256]{1,0:T(8,128)(2,1)S(1)}, bf16[272,256]{1,0:T(8,128)(2,1)S(1)}, u32[]{:S(2)}, u32[]{:S(2)}) collective-permute-start(bf16[272,256]{1,0:T(8,128)(2,1)S(1)} %get-tuple-element.57), channel_id=1, source_target_pairs={{0,12},{1,13},{2,14},{3,15},{4,8},{5,9},{6,10},{7,11},{8,4},{9,5},... | collective-permute-start | bytes 417800 | tf_op jit(solution)/shard_map/ppermute | solution.py:21
  104.9 7.5 %collective-permute-start.32 = (bf16[272,256]{1,0:T(8,128)(2,1)S(1)}, bf16[272,256]{1,0:T(8,128)(2,1)S(1)}, u32[]{:S(2)}, u32[]{:S(2)}) collective-permute-start(bf16[272,256]{1,0:T(8,128)(2,1)S(1)} %get-tuple-element.57), channel_id=1, source_target_pairs={{0,8},{1,9},{2,10},{3,11},{4,12},{5,13},{6,14},{7,15},{8,0},{9,1},... | collective-permute-start | bytes 417800 | tf_op jit(solution)/shard_map/ppermute | solution.py:21
  105.6 6.8 %collective-permute-start.31 = (bf16[272,256]{1,0:T(8,128)(2,1)S(1)}, bf16[272,256]{1,0:T(8,128)(2,1)S(1)}, u32[]{:S(2)}, u32[]{:S(2)}) collective-permute-start(bf16[272,256]{1,0:T(8,128)(2,1)S(1)} %get-tuple-element.57), channel_id=1, source_target_pairs={{0,4},{1,5},{2,6},{3,7},{4,0},{5,1},{6,2},{7,3},{8,12},{9,13},{10,... | collective-permute-start | bytes 417800 | tf_op jit(solution)/shard_map/ppermute | solution.py:21
  113.1 12.5 %collective-permute-start.36 = (bf16[4,128,256]{2,1,0:T(8,128)(2,1)S(1)}, bf16[4,128,256]{2,1,0:T(8,128)(2,1)S(1)}, u32[]{:S(2)}, u32[]{:S(2)}) collective-permute-start(bf16[4,128,256]{2,1,0:T(8,128)(2,1)S(1)} %shard_map.109.refs_0_), channel_id=1, source_target_pairs={{0,3},{1,2},{2,1},{3,0},{4,7},{5,6},{6,5},{7,4},{8,11},{9,10},{10,... | collective-permute-start | bytes 786440 | tf_op jit(solution)/shard_map/ppermute | solution.py:21
  114.5 11.0 %collective-permute-start.35 = (bf16[4,128,256]{2,1,0:T(8,128)(2,1)S(1)}, bf16[4,128,256]{2,1,0:T(8,128)(2,1)S(1)}, u32[]{:S(2)}, u32[]{:S(2)}) collective-permute-start(bf16[4,128,256]{2,1,0:T(8,128)(2,1)S(1)} %shard_map.109.refs_0_), channel_id=1, source_target_pairs={{0,2},{1,3},{2,0},{3,1},{4,6},{5,7},{6,4},{7,5},{8,10},{9,11},{10,... | collective-permute-start | bytes 786440 | tf_op jit(solution)/shard_map/ppermute | solution.py:21
  115.8 10.4 %collective-permute-start.34 = (bf16[4,128,256]{2,1,0:T(8,128)(2,1)S(1)}, bf16[4,128,256]{2,1,0:T(8,128)(2,1)S(1)}, u32[]{:S(2)}, u32[]{:S(2)}) collective-permute-start(bf16[4,128,256]{2,1,0:T(8,128)(2,1)S(1)} %shard_map.109.refs_0_), channel_id=1, source_target_pairs={{0,1},{1,0},{2,3},{3,2},{4,5},{5,4},{6,7},{7,6},{8,9},{9,8},{10,11... | collective-permute-start | bytes 786440 | tf_op jit(solution)/shard_map/ppermute | solution.py:21
  131.8 6.9 %collective-permute-start.40 = (bf16[128,256]{1,0:T(8,128)(2,1)S(1)}, bf16[128,256]{1,0:T(8,128)(2,1)S(1)}, u32[]{:S(2)}, u32[]{:S(2)}) collective-permute-start(bf16[128,256]{1,0:T(8,128)(2,1)S(1)} %get-tuple-element.97), channel_id=1, source_target_pairs={{0,64},{16,80},{32,96},{48,112},{64,0},{80,16},{96,32},{112,48},{1... | collective-permute-start | bytes 196616 | tf_op jit(solution)/shard_map/ppermute | solution.py:21
  135.1 5.5 %collective-permute-start.39 = (bf16[128,256]{1,0:T(8,128)(2,1)S(1)}, bf16[128,256]{1,0:T(8,128)(2,1)S(1)}, u32[]{:S(2)}, u32[]{:S(2)}) collective-permute-start(bf16[128,256]{1,0:T(8,128)(2,1)S(1)} %get-tuple-element.98), channel_id=1, source_target_pairs={{0,96},{16,112},{32,64},{48,80},{64,32},{80,48},{96,0},{112,16},{1... | collective-permute-start | bytes 196616 | tf_op jit(solution)/shard_map/ppermute | solution.py:21
  141.2 5.9 %collective-permute-start.43 = (bf16[256,128]{1,0:T(8,128)(2,1)S(1)}, bf16[256,128]{1,0:T(8,128)(2,1)S(1)}, u32[]{:S(2)}, u32[]{:S(2)}) collective-permute-start(bf16[256,128]{1,0:T(8,128)(2,1)S(1)} %shard_map.111.refs_0_), channel_id=1, source_target_pairs={{0,64},{16,80},{32,96},{48,112},{64,0},{80,16},{96,32},{112,48},{1... | collective-permute-start | bytes 196616 | tf_op jit(solution)/shard_map/ppermute | solution.py:21
  142.1 5.7 %collective-permute-start.42 = (bf16[256,128]{1,0:T(8,128)(2,1)S(1)}, bf16[256,128]{1,0:T(8,128)(2,1)S(1)}, u32[]{:S(2)}, u32[]{:S(2)}) collective-permute-start(bf16[256,128]{1,0:T(8,128)(2,1)S(1)} %shard_map.111.refs_0_), channel_id=1, source_target_pairs={{0,96},{16,112},{32,64},{48,80},{64,32},{80,48},{96,0},{112,16},{1... | collective-permute-start | bytes 196616 | tf_op jit(solution)/shard_map/ppermute | solution.py:21
  151.6 10.7 %collective-permute-start.48 = (bf16[4,256,128]{2,1,0:T(8,128)(2,1)S(1)}, bf16[4,256,128]{2,1,0:T(8,128)(2,1)S(1)}, u32[]{:S(2)}, u32[]{:S(2)}) collective-permute-start(bf16[4,256,128]{2,1,0:T(8,128)(2,1)S(1)} %shard_map.113), channel_id=1, source_target_pairs={{0,2},{1,3},{2,0},{3,1},{4,6},{5,7},{6,4},{7,5},{8,10},{9,11},{10,... | collective-permute-start | bytes 786440 | tf_op jit(solution)/shard_map/ppermute | solution.py:21
  155.8 10.2 %collective-permute-start.49 = (bf16[4,256,128]{2,1,0:T(8,128)(2,1)S(1)}, bf16[4,256,128]{2,1,0:T(8,128)(2,1)S(1)}, u32[]{:S(2)}, u32[]{:S(2)}) collective-permute-start(bf16[4,256,128]{2,1,0:T(8,128)(2,1)S(1)} %shard_map.114), channel_id=1, source_target_pairs={{0,1},{1,0},{2,3},{3,2},{4,5},{5,4},{6,7},{7,6},{8,9},{9,8},{10,11... | collective-permute-start | bytes 786440 | tf_op jit(solution)/shard_map/ppermute | solution.py:21
  158.0 9.6 %collective-permute-start.50 = (bf16[4,256,128]{2,1,0:T(8,128)(2,1)S(1)}, bf16[4,256,128]{2,1,0:T(8,128)(2,1)S(1)}, u32[]{:S(2)}, u32[]{:S(2)}) collective-permute-start(bf16[4,256,128]{2,1,0:T(8,128)(2,1)S(1)} %shard_map.115), channel_id=1, source_target_pairs={{0,3},{1,2},{2,1},{3,0},{4,7},{5,6},{6,5},{7,4},{8,11},{9,10},{10,... | collective-permute-start | bytes 786440 | tf_op jit(solution)/shard_map/ppermute | solution.py:21
  167.7 6.7 %collective-permute-start.51 = (bf16[2,256,128]{2,1,0:T(8,128)(2,1)S(1)}, bf16[2,256,128]{2,1,0:T(8,128)(2,1)S(1)}, u32[]{:S(2)}, u32[]{:S(2)}) collective-permute-start(bf16[2,256,128]{2,1,0:T(8,128)(2,1)S(1)} %get-tuple-element.87), channel_id=1, source_target_pairs={{0,8},{1,9},{2,10},{3,11},{4,12},{5,13},{6,14},{7,15},{8,0},{9,1},... | collective-permute-start | bytes 393224 | tf_op jit(solution)/shard_map/ppermute | solution.py:21
  170.5 6.6 %collective-permute-start.53 = (bf16[2,256,128]{2,1,0:T(8,128)(2,1)S(1)}, bf16[2,256,128]{2,1,0:T(8,128)(2,1)S(1)}, u32[]{:S(2)}, u32[]{:S(2)}) collective-permute-start(bf16[2,256,128]{2,1,0:T(8,128)(2,1)S(1)} %get-tuple-element.95), channel_id=1, source_target_pairs={{0,12},{1,13},{2,14},{3,15},{4,8},{5,9},{6,10},{7,11},{8,4},{9,5},... | collective-permute-start | bytes 393224 | tf_op jit(solution)/shard_map/ppermute | solution.py:21
  171.7 5.4 %collective-permute-start.52 = (bf16[2,256,128]{2,1,0:T(8,128)(2,1)S(1)}, bf16[2,256,128]{2,1,0:T(8,128)(2,1)S(1)}, u32[]{:S(2)}, u32[]{:S(2)}) collective-permute-start(bf16[2,256,128]{2,1,0:T(8,128)(2,1)S(1)} %get-tuple-element.95), channel_id=1, source_target_pairs={{0,4},{1,5},{2,6},{3,7},{4,0},{5,1},{6,2},{7,3},{8,12},{9,13},{10,... | collective-permute-start | bytes 393224 | tf_op jit(solution)/shard_map/ppermute | solution.py:21
  177.2 6.2 %collective-permute-start.56 = (bf16[256,128]{1,0:T(8,128)(2,1)S(1)}, bf16[256,128]{1,0:T(8,128)(2,1)S(1)}, u32[]{:S(2)}, u32[]{:S(2)}) collective-permute-start(bf16[256,128]{1,0:T(8,128)(2,1)S(1)} %get-tuple-element.84.refs_0_.down_ref), channel_id=1, source_target_pairs={{0,64},{16,80},{32,96},{48,112},{64,0},{80,16},{96,32},{112,48},{1... | collective-permute-start | bytes 196616 | tf_op jit(solution)/shard_map/ppermute | solution.py:21
  179.0 5.5 %collective-permute-start.55 = (bf16[256,128]{1,0:T(8,128)(2,1)S(1)}, bf16[256,128]{1,0:T(8,128)(2,1)S(1)}, u32[]{:S(2)}, u32[]{:S(2)}) collective-permute-start(bf16[256,128]{1,0:T(8,128)(2,1)S(1)} %get-tuple-element.84.refs_0_.down_ref), channel_id=1, source_target_pairs={{0,96},{16,112},{32,64},{48,80},{64,32},{80,48},{96,0},{112,16},{1... | collective-permute-start | bytes 196616 | tf_op jit(solution)/shard_map/ppermute | solution.py:21
  180.8 8.9 %collective-permute-start.57 = (bf16[256,128]{1,0:T(8,128)(2,1)S(1)}, bf16[256,128]{1,0:T(8,128)(2,1)S(1)}, u32[]{:S(2)}, u32[]{:S(2)}) collective-permute-start(bf16[256,128]{1,0:T(8,128)(2,1)S(1)} %get-tuple-element.84.refs_0_.down_ref), channel_id=1, source_target_pairs={{0,16},{16,0},{32,48},{48,32},{64,80},{80,64},{96,112},{112,96},{1... | collective-permute-start | bytes 196616 | tf_op jit(solution)/shard_map/ppermute | solution.py:21
  183.5 6.2 %collective-permute-start.60 = (bf16[256,128]{1,0:T(8,128)(2,1)S(1)}, bf16[256,128]{1,0:T(8,128)(2,1)S(1)}, u32[]{:S(2)}, u32[]{:S(2)}) collective-permute-start(bf16[256,128]{1,0:T(8,128)(2,1)S(1)} %collective-permute-done.56.refs_3_), channel_id=1, source_target_pairs={{0,16},{16,0},{32,48},{48,32},{64,80},{80,64},{96,112},{112,96},{1... | collective-permute-start | bytes 196616 | tf_op jit(solution)/shard_map/ppermute | solution.py:21
  184.4 5.3 %collective-permute-start.59 = (bf16[256,128]{1,0:T(8,128)(2,1)S(1)}, bf16[256,128]{1,0:T(8,128)(2,1)S(1)}, u32[]{:S(2)}, u32[]{:S(2)}) collective-permute-start(bf16[256,128]{1,0:T(8,128)(2,1)S(1)} %collective-permute-done.55.refs_2_), channel_id=1, source_target_pairs={{0,16},{16,0},{32,48},{48,32},{64,80},{80,64},{96,112},{112,96},{1... | collective-permute-start | bytes 196616 | tf_op jit(solution)/shard_map/ppermute | solution.py:21
  192.4 6.4 %collective-permute-start.61 = (bf16[2,256,128]{2,1,0:T(8,128)(2,1)S(1)}, bf16[2,256,128]{2,1,0:T(8,128)(2,1)S(1)}, u32[]{:S(2)}, u32[]{:S(2)}) collective-permute-start(bf16[2,256,128]{2,1,0:T(8,128)(2,1)S(1)} %get-tuple-element.64), channel_id=1, source_target_pairs={{0,1},{1,0},{2,3},{3,2},{4,5},{5,4},{6,7},{7,6},{8,9},{9,8},{10,11... | collective-permute-start | bytes 393224 | tf_op jit(solution)/shard_map/ppermute | solution.py:21
  193.0 9.7 %collective-permute-start.62 = (bf16[2,256,128]{2,1,0:T(8,128)(2,1)S(1)}, bf16[2,256,128]{2,1,0:T(8,128)(2,1)S(1)}, u32[]{:S(2)}, u32[]{:S(2)}) collective-permute-start(bf16[2,256,128]{2,1,0:T(8,128)(2,1)S(1)} %get-tuple-element.65), channel_id=1, source_target_pairs={{0,3},{1,2},{2,1},{3,0},{4,7},{5,6},{6,5},{7,4},{8,11},{9,10},{10,... | collective-permute-start | bytes 393224 | tf_op jit(solution)/shard_map/ppermute | solution.py:21
  194.9 7.9 %collective-permute-start.63 = (bf16[2,256,128]{2,1,0:T(8,128)(2,1)S(1)}, bf16[2,256,128]{2,1,0:T(8,128)(2,1)S(1)}, u32[]{:S(2)}, u32[]{:S(2)}) collective-permute-start(bf16[2,256,128]{2,1,0:T(8,128)(2,1)S(1)} %get-tuple-element.66), channel_id=1, source_target_pairs={{0,2},{1,3},{2,0},{3,1},{4,6},{5,7},{6,4},{7,5},{8,10},{9,11},{10,... | collective-permute-start | bytes 393224 | tf_op jit(solution)/shard_map/ppermute | solution.py:21
  207.2 5.8 %collective-permute-start.67 = (bf16[256,128]{1,0:T(8,128)(2,1)S(1)}, bf16[256,128]{1,0:T(8,128)(2,1)S(1)}, u32[]{:S(2)}, u32[]{:S(2)}) collective-permute-start(bf16[256,128]{1,0:T(8,128)(2,1)S(1)} %fusion.6.refs_0_), channel_id=1, source_target_pairs={{0,64},{16,80},{32,96},{48,112},{64,0},{80,16},{96,32},{112,48},{1... | collective-permute-start | bytes 196616 | tf_op jit(solution)/shard_map/ppermute | solution.py:21
  208.4 5.5 %collective-permute-start.66 = (bf16[256,128]{1,0:T(8,128)(2,1)S(1)}, bf16[256,128]{1,0:T(8,128)(2,1)S(1)}, u32[]{:S(2)}, u32[]{:S(2)}) collective-permute-start(bf16[256,128]{1,0:T(8,128)(2,1)S(1)} %fusion.6.refs_0_), channel_id=1, source_target_pairs={{0,96},{16,112},{32,64},{48,80},{64,32},{80,48},{96,0},{112,16},{1... | collective-permute-start | bytes 196616 | tf_op jit(solution)/shard_map/ppermute | solution.py:21
  210.7 6.3 %collective-permute-start.68 = (bf16[256,128]{1,0:T(8,128)(2,1)S(1)}, bf16[256,128]{1,0:T(8,128)(2,1)S(1)}, u32[]{:S(2)}, u32[]{:S(2)}) collective-permute-start(bf16[256,128]{1,0:T(8,128)(2,1)S(1)} %fusion.6.refs_0_), channel_id=1, source_target_pairs={{0,16},{16,0},{32,48},{48,32},{64,80},{80,64},{96,112},{112,96},{1... | collective-permute-start | bytes 196616 | tf_op jit(solution)/shard_map/ppermute | solution.py:21
  219.7 6.4 %collective-permute-start.72 = (bf16[2,256,128]{2,1,0:T(8,128)(2,1)S(1)}, bf16[2,256,128]{2,1,0:T(8,128)(2,1)S(1)}, u32[]{:S(2)}, u32[]{:S(2)}) collective-permute-start(bf16[2,256,128]{2,1,0:T(8,128)(2,1)S(1)} %get-tuple-element.68), channel_id=1, source_target_pairs={{0,1},{1,0},{2,3},{3,2},{4,5},{5,4},{6,7},{7,6},{8,9},{9,8},{10,11... | collective-permute-start | bytes 393224 | tf_op jit(solution)/shard_map/ppermute | solution.py:21
  220.0 9.6 %collective-permute-start.73 = (bf16[2,256,128]{2,1,0:T(8,128)(2,1)S(1)}, bf16[2,256,128]{2,1,0:T(8,128)(2,1)S(1)}, u32[]{:S(2)}, u32[]{:S(2)}) collective-permute-start(bf16[2,256,128]{2,1,0:T(8,128)(2,1)S(1)} %get-tuple-element.69), channel_id=1, source_target_pairs={{0,3},{1,2},{2,1},{3,0},{4,7},{5,6},{6,5},{7,4},{8,11},{9,10},{10,... | collective-permute-start | bytes 393224 | tf_op jit(solution)/shard_map/ppermute | solution.py:21
  221.9 7.8 %collective-permute-start.74 = (bf16[2,256,128]{2,1,0:T(8,128)(2,1)S(1)}, bf16[2,256,128]{2,1,0:T(8,128)(2,1)S(1)}, u32[]{:S(2)}, u32[]{:S(2)}) collective-permute-start(bf16[2,256,128]{2,1,0:T(8,128)(2,1)S(1)} %get-tuple-element.70), channel_id=1, source_target_pairs={{0,2},{1,3},{2,0},{3,1},{4,6},{5,7},{6,4},{7,5},{8,10},{9,11},{10,... | collective-permute-start | bytes 393224 | tf_op jit(solution)/shard_map/ppermute | solution.py:21
  230.3 6.1 %collective-permute-start.75 = (bf16[3,256,128]{2,1,0:T(8,128)(2,1)S(1)}, bf16[3,256,128]{2,1,0:T(8,128)(2,1)S(1)}, u32[]{:S(2)}, u32[]{:S(2)}) collective-permute-start(bf16[3,256,128]{2,1,0:T(8,128)(2,1)S(1)} %get-tuple-element.72), channel_id=1, source_target_pairs={{0,4},{1,5},{2,6},{3,7},{4,0},{5,1},{6,2},{7,3},{8,12},{9,13},{10,... | collective-permute-start | bytes 589832 | tf_op jit(solution)/shard_map/ppermute | solution.py:21
  237.0 6.1 %collective-permute-start.78 = (bf16[256,128]{1,0:T(8,128)(2,1)S(1)}, bf16[256,128]{1,0:T(8,128)(2,1)S(1)}, u32[]{:S(2)}, u32[]{:S(2)}) collective-permute-start(bf16[256,128]{1,0:T(8,128)(2,1)S(1)} %get-tuple-element.73.refs_0_.refs_8_), channel_id=1, source_target_pairs={{0,64},{16,80},{32,96},{48,112},{64,0},{80,16},{96,32},{112,48},{1... | collective-permute-start | bytes 196616 | tf_op jit(solution)/shard_map/ppermute | solution.py:21
  239.2 5.5 %collective-permute-start.77 = (bf16[256,128]{1,0:T(8,128)(2,1)S(1)}, bf16[256,128]{1,0:T(8,128)(2,1)S(1)}, u32[]{:S(2)}, u32[]{:S(2)}) collective-permute-start(bf16[256,128]{1,0:T(8,128)(2,1)S(1)} %get-tuple-element.73.refs_0_.refs_8_), channel_id=1, source_target_pairs={{0,96},{16,112},{32,64},{48,80},{64,32},{80,48},{96,0},{112,16},{1... | collective-permute-start | bytes 196616 | tf_op jit(solution)/shard_map/ppermute | solution.py:21
  248.0 5.6 %collective-permute-start.84 = (bf16[1,256,128]{2,1,0:T(8,128)(2,1)S(1)}, bf16[1,256,128]{2,1,0:T(8,128)(2,1)S(1)}, u32[]{:S(2)}, u32[]{:S(2)}) collective-permute-start(bf16[1,256,128]{2,1,0:T(8,128)(2,1)S(1)} %get-tuple-element.76), channel_id=1, source_target_pairs={{0,3},{1,2},{2,1},{3,0},{4,7},{5,6},{6,5},{7,4},{8,11},{9,10},{10,... | collective-permute-start | bytes 196616 | tf_op jit(solution)/shard_map/ppermute | solution.py:21
  249.7 5.8 %collective-permute-start.85 = (bf16[1,256,128]{2,1,0:T(8,128)(2,1)S(1)}, bf16[1,256,128]{2,1,0:T(8,128)(2,1)S(1)}, u32[]{:S(2)}, u32[]{:S(2)}) collective-permute-start(bf16[1,256,128]{2,1,0:T(8,128)(2,1)S(1)} %get-tuple-element.77), channel_id=1, source_target_pairs={{0,2},{1,3},{2,0},{3,1},{4,6},{5,7},{6,4},{7,5},{8,10},{9,11},{10,... | collective-permute-start | bytes 196616 | tf_op jit(solution)/shard_map/ppermute | solution.py:21
  255.5 6.3 %collective-permute-start.88 = (bf16[256,128]{1,0:T(8,128)(2,1)S(1)}, bf16[256,128]{1,0:T(8,128)(2,1)S(1)}, u32[]{:S(2)}, u32[]{:S(2)}) collective-permute-start(bf16[256,128]{1,0:T(8,128)(2,1)S(1)} %fusion.4.refs_0_), channel_id=1, source_target_pairs={{0,64},{16,80},{32,96},{48,112},{64,0},{80,16},{96,32},{112,48},{1... | collective-permute-start | bytes 196616 | tf_op jit(solution)/shard_map/ppermute | solution.py:21
  257.5 5.5 %collective-permute-start.87 = (bf16[256,128]{1,0:T(8,128)(2,1)S(1)}, bf16[256,128]{1,0:T(8,128)(2,1)S(1)}, u32[]{:S(2)}, u32[]{:S(2)}) collective-permute-start(bf16[256,128]{1,0:T(8,128)(2,1)S(1)} %fusion.4.refs_0_), channel_id=1, source_target_pairs={{0,96},{16,112},{32,64},{48,80},{64,32},{80,48},{96,0},{112,16},{1... | collective-permute-start | bytes 196616 | tf_op jit(solution)/shard_map/ppermute | solution.py:21
  266.1 11.6 %collective-permute-start.95 = (bf16[3,256,128]{2,1,0:T(8,128)(2,1)S(1)}, bf16[3,256,128]{2,1,0:T(8,128)(2,1)S(1)}, u32[]{:S(2)}, u32[]{:S(2)}) collective-permute-start(bf16[3,256,128]{2,1,0:T(8,128)(2,1)S(1)} %get-tuple-element.81), channel_id=1, source_target_pairs={{0,2},{1,3},{2,0},{3,1},{4,6},{5,7},{6,4},{7,5},{8,10},{9,11},{10,... | collective-permute-start | bytes 589832 | tf_op jit(solution)/shard_map/ppermute | solution.py:21
  268.3 8.1 %collective-permute-start.93 = (bf16[2,256,128]{2,1,0:T(8,128)(2,1)S(1)}, bf16[2,256,128]{2,1,0:T(8,128)(2,1)S(1)}, u32[]{:S(2)}, u32[]{:S(2)}) collective-permute-start(bf16[2,256,128]{2,1,0:T(8,128)(2,1)S(1)} %get-tuple-element.79), channel_id=1, source_target_pairs={{0,1},{1,0},{2,3},{3,2},{4,5},{5,4},{6,7},{7,6},{8,9},{9,8},{10,11... | collective-permute-start | bytes 393224 | tf_op jit(solution)/shard_map/ppermute | solution.py:21
  268.4 9.3 %collective-permute-start.94 = (bf16[2,256,128]{2,1,0:T(8,128)(2,1)S(1)}, bf16[2,256,128]{2,1,0:T(8,128)(2,1)S(1)}, u32[]{:S(2)}, u32[]{:S(2)}) collective-permute-start(bf16[2,256,128]{2,1,0:T(8,128)(2,1)S(1)} %get-tuple-element.80), channel_id=1, source_target_pairs={{0,3},{1,2},{2,1},{3,0},{4,7},{5,6},{6,5},{7,4},{8,11},{9,10},{10,... | collective-permute-start | bytes 393224 | tf_op jit(solution)/shard_map/ppermute | solution.py:21
  (46 other events, 341.4 us)

commit v3 on v1

--- a/solution.py
+++ b/solution.py
@@ -90,13 +90,15 @@
 
     def body(s, w_ref, *refs):
         in_refs, out_refs, vec = refs[:count], refs[count:-1], refs[-1]
-        for index, block in gather(s, in_refs, out_refs[2:]):
+        def put(index, block):
             start = pl.multiple_of(index * C, C)
             block = block.astype(F32)
             vec[pl.ds(start, B), :] = block.astype(BF)
             vec[pl.ds(start + B, B), :] = jnp.concatenate(
                 [-block[:, B:], block[:, :B]], axis=1
             ).astype(BF)
+
+        gather(s, in_refs, out_refs[2:], put)
         swapped = s[CORE] == 1
 
         @pl.loop(0, 4)
@@ -150,7 +152,7 @@
             return
         acc = scratch[1]
 
-        @pl.loop(0, 4 * tiles, unroll=2)
+        @pl.loop(0, 4 * tiles, unroll=tiles)
         def _(step):
             k, j = step & 3, step >> 2
             acc[k, j] = block(((s[Y] & mask) ^ j) * 4 + (s[X] ^ k))
@@ -237,7 +239,7 @@
         relay(w) for w in (inv_low, couple_low, inv_mid, couple_mid, inv_top)
     ]
 
-    def gather_low(s, refs, extra):
+    def gather_low(s, refs, extra, put):
         goal = [r[2 * B : 2 * B + 16, :].astype(F32)[:1] for r in refs[:4]]
         child = [r[:B, :].astype(F32) for r in refs[:4]]
         slot = (s[X] + 4) * 8 + s[ROW]
@@ -253,10 +255,11 @@
         extra[2][B:] = jnp.full((16, C), s[T0].astype(F32), F32).astype(BF)
         for k in range(4):
             slot = (s[X] ^ k) * 8 + s[ROW]
-            yield s[X] ^ k, (
+            put(
+                s[X] ^ k,
                 refs[k][B : 2 * B, :].astype(F32)
                 + same(goal[k], slot) * child[k]
-                + same(goal[k ^ 2], slot) * child[k ^ 2]
+                + same(goal[k ^ 2], slot) * child[k ^ 2],
             )
 
     own, others, update, to_y1, to_y3 = forward(
@@ -271,9 +274,9 @@
     from_y2 = swap(to_y3, "leaf", 8)
     y_low = reduce_row(own, others)
 
-    def gather_plain(s, refs, extra):
-        for k in range(4):
-            yield s[X] ^ k, refs[k][...]
+    def gather_plain(s, refs, extra, put):
+        for k in range(4):
+            put(s[X] ^ k, refs[k][...])
 
     own, others = forward(b_low, scal, gather_x(y_low.astype(BF)), gather_plain)
     children = update - reduce_row(own, others)
@@ -300,10 +303,10 @@
         extend_mid, [((2, B, C), BF), ((B, C), F32)], scal, children, theirs, rhs, from_y1
     )
 
-    def gather_mid(s, refs, extra):
+    def gather_mid(s, refs, extra, put):
         for k in range(4):
             for j in range(2):
-                yield ((s[Y] & 1) ^ j) * 4 + (s[X] ^ k), refs[k][j]
+                put(((s[Y] & 1) ^ j) * 4 + (s[X] ^ k), refs[k][j])
 
     own, others = forward(w_mid, scal, gather_x(pair), gather_mid)
     y_mid = reduce_row(own, others)
@@ -347,10 +350,9 @@
         extend_top, [((4, B, C), BF)], scal, children, *moved, rhs, from_y1, from_y3, from_y2
     )
 
-    def gather_top(s, refs, extra):
-        for k in range(4):
-            for j in range(4):
-                yield (s[Y] ^ j) * 4 + (s[X] ^ k), refs[k][j]
+    def gather_top(s, refs, extra, put):
+        for k in range(4):
+            pl.loop(0, 4)(lambda j, k=k: put((s[Y] ^ j) * 4 + (s[X] ^ k), refs[k][j]))
 
     own, others = forward(w_top, scal, gather_x(column), gather_top)
 
@@ -361,13 +363,18 @@
     pieces = gather_row(half)
     got = [swap(transposed(w_top, scal, pieces, only=k)[0], "leaf", k) for k in (2, 1, 3)]
     (own,) = transposed(w_top, scal, pieces, only=0)
+    b_mid = relay(lax.optimization_barrier((couple_mid, half))[0])
+    *got, own, b_mid = lax.optimization_barrier((*got, own, b_mid))
 
     def total(planes):
         return own[planes] + sum(g[planes].astype(F32) for g in got)
 
     pair, cross = total(slice(0, 2)), total(slice(2, 4)).astype(BF)
-    from_1, from_3 = swap(cross, "leaf", 4).astype(F32), swap(cross, "leaf", 12).astype(F32)
-    from_2 = swap(pair.astype(BF), "leaf", 8).astype(F32)
+    from_1, from_3 = swap(cross, "leaf", 4), swap(cross, "leaf", 12)
+    from_2 = swap(pair.astype(BF), "leaf", 8)
+    w_mid = relay(lax.optimization_barrier((inv_mid, half))[0])
+    from_1, from_3, from_2, w_mid = lax.optimization_barrier((from_1, from_3, from_2, w_mid))
+    from_1, from_3, from_2 = from_1.astype(F32), from_3.astype(F32), from_2.astype(F32)
     x_top = pair[0] + from_2[1] + from_1[0] + from_3[1]
     x_other = pair[1] + from_2[0] + from_1[1] + from_3[0]
     down_mid = jnp.where(block_map[0, 0] == leaf * 8 + row, x_top, x_other)

time: 277 us -> 273 us (0.986)
  waiting for transfers between devices: 114 us -> 105 us
  Pallas kernels: 48.1 us -> 53.8 us
    ppermute x98, waiting for transfers between devices: 114 us -> 105 us  [swap(): return lax.ppermute(value, axis, [(i, i ^ mask) for i in range(count)])]
    pallas_call x5 -> x7, Pallas kernels: 12.5 us -> 17.5 us  [relay(): pl.pallas_call(functools.partial(relay_body, groups), grid=(tiles,), out_...]
    unnamed x33 -> x31, local copies, waits for them, and re-layouts: 8.49 us -> 8.49 us
  transfers between devices with their start and end apart: 98 -> 98, of which waited for: 71 -> 68; matrix products, arithmetic and copies ran while one was open for 0% -> 0% of each run, Pallas kernels for 7% -> 9%
where the time goes in v3:
time: 273 us; the launch traced here: 272 us
  waiting for transfers between devices  105 us (38%)
  starting transfers between devices  102 us (37%)
  Pallas kernels  53.8 us (20%)
  local copies, waits for them, and re-layouts  9.22 us (3%)
    ppermute x98, waiting for transfers between devices, swap(): return lax.ppermute(value, axis, [(i, i ^ mask) for i in range(count)])  105 us
    ppermute x98, starting transfers between devices, swap(): return lax.ppermute(value, axis, [(i, i ^ mask) for i in range(count)])  102 us
    pallas_call x13, Pallas kernels, call(): pl.pallas_call(body, out_shape=[jax.ShapeDtypeStruct(*o) for o in outs],...  29.5 us
    pallas_call x7, Pallas kernels, relay(): pl.pallas_call(functools.partial(relay_body, groups), grid=(tiles,), out_...  17.5 us
    unnamed x31, local copies, waits for them, and re-layouts  8.49 us
    pallas_call x8, Pallas kernels, small(): pl.pallas_call(body, out_shape=[jax.ShapeDtypeStruct(*o) for o in outs],...  5.85 us
  transfers between devices with their start and end apart: 98, of which 68 were waited for; matrix products, arithmetic and copies ran while one was open for 0% of the time, Pallas kernels for 9%

profile of v3, /device:TPU:0, one launch (start us, length us, event | category | flops | bytes accessed | tf_op | source)
XLA Modules:
  0.0 272.0 jit_solution(18176947603549609606)
XLA Ops:
  4.2 2.9 %collective-permute-start.2 = (bf16[272,256]{1,0:T(8,128)(2,1)S(1)}, bf16[272,256]{1,0:T(8,128)(2,1)S(1)}, u32[]{:S(2)}, u32[]{:S(2)}) collective-permute-start(bf16[272,256]{1,0:T(8,128)(2,1)S(1)} %shard_map.96.refs_0_), channel_id=1, source_target_pairs={{0,3},{1,2},{2,1},{3,0},{4,7},{5,6},{6,5},{7,4},{8,11},{9,10},{10,... | collective-permute-start | bytes 417800 | tf_op jit(solution)/shard_map/ppermute | solution.py:21
  10.7 1.9 shard_map.95.w_ref
  13.1 2.2 collective-permute-done.1.refs_2_
  15.3 2.0 shard_map.97
  18.9 2.0 collective-permute-start.4
  20.9 3.6 %collective-permute-start.6 = (bf16[128,256]{1,0:T(8,128)(2,1)S(1)}, bf16[128,256]{1,0:T(8,128)(2,1)S(1)}, u32[]{:S(2)}, u32[]{:S(2)}) collective-permute-start(bf16[128,256]{1,0:T(8,128)(2,1)S(1)} %get-tuple-element.127), channel_id=1, source_target_pairs={{0,64},{16,80},{32,96},{48,112},{64,0},{80,16},{96,32},{112,48},{1... | collective-permute-start | bytes 196616 | tf_op jit(solution)/shard_map/ppermute | solution.py:21
  24.5 3.5 %collective-permute-done.6 = bf16[128,256]{1,0:T(8,128)(2,1)S(1)} collective-permute-done((bf16[128,256]{1,0:T(8,128)(2,1)S(1)}, bf16[128,256]{1,0:T(8,128)(2,1)S(1)}, u32[]{:S(2)}, u32[]{:S(2)}) %collective-permute-start.6) | collective-permute-done | bytes 65568 | tf_op jit(solution)/shard_map/ppermute | solution.py:21
  28.0 2.0 collective-permute-done.5
  30.0 2.2 collective-permute-start.9
  34.2 1.9 shard_map.99.w_ref
  36.1 1.8 collective-permute-done.8.refs_2_
  43.3 2.9 %collective-permute-start.12 = (bf16[128,256]{1,0:T(8,128)(2,1)S(1)}, bf16[128,256]{1,0:T(8,128)(2,1)S(1)}, u32[]{:S(2)}, u32[]{:S(2)}) collective-permute-start(bf16[128,256]{1,0:T(8,128)(2,1)S(1)} %get-tuple-element.125), channel_id=1, source_target_pairs={{0,96},{16,112},{32,64},{48,80},{64,32},{80,48},{96,0},{112,16},{1... | collective-permute-start | bytes 196616 | tf_op jit(solution)/shard_map/ppermute | solution.py:21
  58.0 2.5 shard_map.98.w_ref
  62.8 2.4 shard_map.102
  67.0 3.8 %collective-permute-start.22 = (bf16[128,256]{1,0:T(8,128)(2,1)S(1)}, bf16[128,256]{1,0:T(8,128)(2,1)S(1)}, u32[]{:S(2)}, u32[]{:S(2)}) collective-permute-start(bf16[128,256]{1,0:T(8,128)(2,1)S(1)} %get-tuple-element.121), channel_id=1, source_target_pairs={{0,64},{16,80},{32,96},{48,112},{64,0},{80,16},{96,32},{112,48},{1... | collective-permute-start | bytes 196616 | tf_op jit(solution)/shard_map/ppermute | solution.py:21
  71.6 2.7 %collective-permute-done.22 = bf16[128,256]{1,0:T(8,128)(2,1)S(1)} collective-permute-done((bf16[128,256]{1,0:T(8,128)(2,1)S(1)}, bf16[128,256]{1,0:T(8,128)(2,1)S(1)}, u32[]{:S(2)}, u32[]{:S(2)}) %collective-permute-start.22) | collective-permute-done | bytes 65568 | tf_op jit(solution)/shard_map/ppermute | solution.py:21
  74.4 2.0 collective-permute-done.21
  78.0 2.7 collective-permute-done.23.b_ref
  85.4 2.5 shard_map.105.w_ref
  89.8 2.4 shard_map.107
  94.0 2.2 collective-permute-start.30
  96.2 2.4 collective-permute-start.29
  98.6 3.2 %collective-permute-start.35 = (bf16[144,256]{1,0:T(8,128)(2,1)S(1)}, bf16[144,256]{1,0:T(8,128)(2,1)S(1)}, u32[]{:S(2)}, u32[]{:S(2)}) collective-permute-start(bf16[144,256]{1,0:T(8,128)(2,1)S(1)} %get-tuple-element.64), channel_id=1, source_target_pairs={{0,8},{1,9},{2,10},{3,11},{4,12},{5,13},{6,14},{7,15},{8,0},{9,1},... | collective-permute-start | bytes 221192 | tf_op jit(solution)/shard_map/ppermute | solution.py:21
  103.0 2.0 collective-permute-start.33
  115.3 3.6 %shard_map.104.w_ref = bf16[1024,4096]{1,0:T(8,128)(2,1)S(1)} custom-call(bf16[32768,128]{1,0:T(8,128)(2,1)S(1)} %bitcast.113, bf16[32768,128]{1,0:T(8,128)(2,1)S(1)} %bitcast.114), custom_call_target="tpu_custom_call" | custom-call | flops 2147483648 | bytes 16777216 | tf_op jit(solution)/shard_map/pallas_call | solution.py:57
  119.0 4.8 %collective-permute-done.38.refs_3_ = bf16[4,128,256]{2,1,0:T(8,128)(2,1)S(1)} collective-permute-done((bf16[4,128,256]{2,1,0:T(8,128)(2,1)S(1)}, bf16[4,128,256]{2,1,0:T(8,128)(2,1)S(1)}, u32[]{:S(2)}, u32[]{:S(2)}) %collective-permute-start.38) | collective-permute-done | bytes 262176 | tf_op jit(solution)/shard_map/ppermute | solution.py:21
  124.4 3.7 %shard_map.109 = (f32[4,128,256]{2,1,0:T(8,128)S(1)}, bf16[4,128,256]{2,1,0:T(8,128)(2,1)S(1)}) custom-call(s32[8]{0:T(128)S(1)} %concatenate.3.s, bf16[1024,4096]{1,0:T(8,128)(2,1)S(1)} %shard_map.104.w_ref, bf16[4,128,256]{2,1,0:T(8,128)(2,1)S(1)} %shard_map.108.refs_0_, bf16[4,128,256]{2,1,0:T(8,128)(2,1)S(1)} %collective-permute-done.36.refs_1_, ...), custom_call_target="tpu_custom_call" | custom-call | flops 2147483648 | bytes 1048576 | tf_op jit(solution)/shard_map/pallas_call | solution.py:75
  130.1 3.8 %collective-permute-start.42 = (bf16[128,256]{1,0:T(8,128)(2,1)S(1)}, bf16[128,256]{1,0:T(8,128)(2,1)S(1)}, u32[]{:S(2)}, u32[]{:S(2)}) collective-permute-start(bf16[128,256]{1,0:T(8,128)(2,1)S(1)} %get-tuple-element.115), channel_id=1, source_target_pairs={{0,64},{16,80},{32,96},{48,112},{64,0},{80,16},{96,32},{112,48},{1... | collective-permute-start | bytes 196616 | tf_op jit(solution)/shard_map/ppermute | solution.py:21
  134.5 2.9 %collective-permute-done.42 = bf16[128,256]{1,0:T(8,128)(2,1)S(1)} collective-permute-done((bf16[128,256]{1,0:T(8,128)(2,1)S(1)}, bf16[128,256]{1,0:T(8,128)(2,1)S(1)}, u32[]{:S(2)}, u32[]{:S(2)}) %collective-permute-start.42) | collective-permute-done | bytes 65568 | tf_op jit(solution)/shard_map/ppermute | solution.py:21
  137.4 2.0 collective-permute-done.41
  143.6 2.3 collective-permute-done.45.refs_3_
  148.0 2.0 shard_map.111
  150.0 2.1 collective-permute-start.50
  152.1 2.0 shard_map.112
  154.4 2.0 shard_map.113
  156.4 1.9 collective-permute-start.52
  158.3 2.5 shard_map.115.w_ref
  160.8 2.0 copy-done.5
  162.9 2.0 shard_map.114
  169.8 2.2 copy-done.2
  172.0 2.5 shard_map.116.w_ref
  176.9 2.3 collective-permute-start.57
  179.1 2.6 collective-permute-done.58.refs_3_
  184.7 2.7 shard_map.117
  187.9 1.9 collective-permute-start.64
  191.5 2.2 collective-permute-done.63
  193.7 3.5 %collective-permute-done.64 = bf16[2,256,128]{2,1,0:T(8,128)(2,1)S(1)} collective-permute-done((bf16[2,256,128]{2,1,0:T(8,128)(2,1)S(1)}, bf16[2,256,128]{2,1,0:T(8,128)(2,1)S(1)}, u32[]{:S(2)}, u32[]{:S(2)}) %collective-permute-start.64) | collective-permute-done | bytes 131104 | tf_op jit(solution)/shard_map/ppermute | solution.py:21
  198.1 3.6 %collective-permute-done.66 = bf16[256,128]{1,0:T(8,128)(2,1)S(1)} collective-permute-done((bf16[256,128]{1,0:T(8,128)(2,1)S(1)}, bf16[256,128]{1,0:T(8,128)(2,1)S(1)}, u32[]{:S(2)}, u32[]{:S(2)}) %collective-permute-start.66) | collective-permute-done | bytes 65568 | tf_op jit(solution)/shard_map/ppermute | solution.py:21
  202.3 2.1 collective-permute-start.68
  205.2 2.3 collective-permute-done.69.refs_3_
  210.0 2.7 shard_map.118
  213.0 1.8 collective-permute-start.75
  214.8 2.0 collective-permute-start.76
  216.8 2.2 collective-permute-done.74.a
  223.2 6.1 %collective-permute-done.77.got_ref = bf16[3,256,128]{2,1,0:T(8,128)(2,1)S(1)} collective-permute-done((bf16[3,256,128]{2,1,0:T(8,128)(2,1)S(1)}, bf16[3,256,128]{2,1,0:T(8,128)(2,1)S(1)}, u32[]{:S(2)}, u32[]{:S(2)}) %collective-permute-start.77) | collective-permute-done | bytes 196640 | tf_op jit(solution)/shard_map/ppermute | solution.py:21
  233.5 2.7 %collective-permute-done.80.refs_3_ = bf16[256,128]{1,0:T(8,128)(2,1)S(1)} collective-permute-done((bf16[256,128]{1,0:T(8,128)(2,1)S(1)}, bf16[256,128]{1,0:T(8,128)(2,1)S(1)}, u32[]{:S(2)}, u32[]{:S(2)}) %collective-permute-start.80) | collective-permute-done | bytes 65568 | tf_op jit(solution)/shard_map/ppermute | solution.py:21
  238.9 2.0 shard_map.121
  241.0 1.8 collective-permute-start.86
  242.8 2.2 collective-permute-start.87
  246.6 2.0 collective-permute-done.87
  252.2 2.3 collective-permute-done.90.refs_3_
  257.1 2.0 shard_map.122
  259.1 2.3 collective-permute-start.97
  263.3 6.2 %collective-permute-done.95.a = bf16[2,256,128]{2,1,0:T(8,128)(2,1)S(1)} collective-permute-done((bf16[2,256,128]{2,1,0:T(8,128)(2,1)S(1)}, bf16[2,256,128]{2,1,0:T(8,128)(2,1)S(1)}, u32[]{:S(2)}, u32[]{:S(2)}) %collective-permute-start.95) | collective-permute-done | bytes 131104 | tf_op jit(solution)/shard_map/ppermute | solution.py:21
  (212 shorter events, 105.0 us)
Async XLA Ops:
  4.2 8.9 %collective-permute-start.2 = (bf16[272,256]{1,0:T(8,128)(2,1)S(1)}, bf16[272,256]{1,0:T(8,128)(2,1)S(1)}, u32[]{:S(2)}, u32[]{:S(2)}) collective-permute-start(bf16[272,256]{1,0:T(8,128)(2,1)S(1)} %shard_map.96.refs_0_), channel_id=1, source_target_pairs={{0,3},{1,2},{2,1},{3,0},{4,7},{5,6},{6,5},{7,4},{8,11},{9,10},{10,... | collective-permute-start | bytes 417800 | tf_op jit(solution)/shard_map/ppermute | solution.py:21
  7.1 8.1 %collective-permute-start.1 = (bf16[272,256]{1,0:T(8,128)(2,1)S(1)}, bf16[272,256]{1,0:T(8,128)(2,1)S(1)}, u32[]{:S(2)}, u32[]{:S(2)}) collective-permute-start(bf16[272,256]{1,0:T(8,128)(2,1)S(1)} %shard_map.96.refs_0_), channel_id=1, source_target_pairs={{0,2},{1,3},{2,0},{3,1},{4,6},{5,7},{6,4},{7,5},{8,10},{9,11},{10,... | collective-permute-start | bytes 417800 | tf_op jit(solution)/shard_map/ppermute | solution.py:21
  7.9 7.3 %collective-permute-start = (bf16[272,256]{1,0:T(8,128)(2,1)S(1)}, bf16[272,256]{1,0:T(8,128)(2,1)S(1)}, u32[]{:S(2)}, u32[]{:S(2)}) collective-permute-start(bf16[272,256]{1,0:T(8,128)(2,1)S(1)} %shard_map.96.refs_0_), channel_id=1, source_target_pairs={{0,1},{1,0},{2,3},{3,2},{4,5},{5,4},{6,7},{7,6},{8,9},{9,8},{10,11... | collective-permute-start | bytes 417800 | tf_op jit(solution)/shard_map/ppermute | solution.py:21
  18.9 5.6 %collective-permute-start.4 = (bf16[128,256]{1,0:T(8,128)(2,1)S(1)}, bf16[128,256]{1,0:T(8,128)(2,1)S(1)}, u32[]{:S(2)}, u32[]{:S(2)}) collective-permute-start(bf16[128,256]{1,0:T(8,128)(2,1)S(1)} %get-tuple-element.126), channel_id=1, source_target_pairs={{0,32},{16,48},{32,0},{48,16},{64,96},{80,112},{96,64},{112,80},{1... | collective-permute-start | bytes 196616 | tf_op jit(solution)/shard_map/ppermute | solution.py:21
  20.9 7.1 %collective-permute-start.6 = (bf16[128,256]{1,0:T(8,128)(2,1)S(1)}, bf16[128,256]{1,0:T(8,128)(2,1)S(1)}, u32[]{:S(2)}, u32[]{:S(2)}) collective-permute-start(bf16[128,256]{1,0:T(8,128)(2,1)S(1)} %get-tuple-element.127), channel_id=1, source_target_pairs={{0,64},{16,80},{32,96},{48,112},{64,0},{80,16},{96,32},{112,48},{1... | collective-permute-start | bytes 196616 | tf_op jit(solution)/shard_map/ppermute | solution.py:21
  24.5 5.5 %collective-permute-start.5 = (bf16[128,256]{1,0:T(8,128)(2,1)S(1)}, bf16[128,256]{1,0:T(8,128)(2,1)S(1)}, u32[]{:S(2)}, u32[]{:S(2)}) collective-permute-start(bf16[128,256]{1,0:T(8,128)(2,1)S(1)} %get-tuple-element.128), channel_id=1, source_target_pairs={{0,96},{16,112},{32,64},{48,80},{64,32},{80,48},{96,0},{112,16},{1... | collective-permute-start | bytes 196616 | tf_op jit(solution)/shard_map/ppermute | solution.py:21
  30.0 6.1 %collective-permute-start.9 = (bf16[128,256]{1,0:T(8,128)(2,1)S(1)}, bf16[128,256]{1,0:T(8,128)(2,1)S(1)}, u32[]{:S(2)}, u32[]{:S(2)}) collective-permute-start(bf16[128,256]{1,0:T(8,128)(2,1)S(1)} %get-tuple-element.111.refs_0_), channel_id=1, source_target_pairs={{0,3},{1,2},{2,1},{3,0},{4,7},{5,6},{6,5},{7,4},{8,11},{9,10},{10,... | collective-permute-start | bytes 196616 | tf_op jit(solution)/shard_map/ppermute | solution.py:21
  32.2 5.8 %collective-permute-start.8 = (bf16[128,256]{1,0:T(8,128)(2,1)S(1)}, bf16[128,256]{1,0:T(8,128)(2,1)S(1)}, u32[]{:S(2)}, u32[]{:S(2)}) collective-permute-start(bf16[128,256]{1,0:T(8,128)(2,1)S(1)} %get-tuple-element.111.refs_0_), channel_id=1, source_target_pairs={{0,2},{1,3},{2,0},{3,1},{4,6},{5,7},{6,4},{7,5},{8,10},{9,11},{10,... | collective-permute-start | bytes 196616 | tf_op jit(solution)/shard_map/ppermute | solution.py:21
  33.0 5.0 %collective-permute-start.7 = (bf16[128,256]{1,0:T(8,128)(2,1)S(1)}, bf16[128,256]{1,0:T(8,128)(2,1)S(1)}, u32[]{:S(2)}, u32[]{:S(2)}) collective-permute-start(bf16[128,256]{1,0:T(8,128)(2,1)S(1)} %get-tuple-element.111.refs_0_), channel_id=1, source_target_pairs={{0,1},{1,0},{2,3},{3,2},{4,5},{5,4},{6,7},{7,6},{8,9},{9,8},{10,11... | collective-permute-start | bytes 196616 | tf_op jit(solution)/shard_map/ppermute | solution.py:21
  41.4 6.4 %collective-permute-start.11 = (bf16[128,256]{1,0:T(8,128)(2,1)S(1)}, bf16[128,256]{1,0:T(8,128)(2,1)S(1)}, u32[]{:S(2)}, u32[]{:S(2)}) collective-permute-start(bf16[128,256]{1,0:T(8,128)(2,1)S(1)} %get-tuple-element.123), channel_id=1, source_target_pairs={{0,32},{16,48},{32,0},{48,16},{64,96},{80,112},{96,64},{112,80},{1... | collective-permute-start | bytes 196616 | tf_op jit(solution)/shard_map/ppermute | solution.py:21
  41.5 6.3 %collective-permute-start.13 = (bf16[128,256]{1,0:T(8,128)(2,1)S(1)}, bf16[128,256]{1,0:T(8,128)(2,1)S(1)}, u32[]{:S(2)}, u32[]{:S(2)}) collective-permute-start(bf16[128,256]{1,0:T(8,128)(2,1)S(1)} %get-tuple-element.124), channel_id=1, source_target_pairs={{0,64},{16,80},{32,96},{48,112},{64,0},{80,16},{96,32},{112,48},{1... | collective-permute-start | bytes 196616 | tf_op jit(solution)/shard_map/ppermute | solution.py:21
  43.3 5.5 %collective-permute-start.12 = (bf16[128,256]{1,0:T(8,128)(2,1)S(1)}, bf16[128,256]{1,0:T(8,128)(2,1)S(1)}, u32[]{:S(2)}, u32[]{:S(2)}) collective-permute-start(bf16[128,256]{1,0:T(8,128)(2,1)S(1)} %get-tuple-element.125), channel_id=1, source_target_pairs={{0,96},{16,112},{32,64},{48,80},{64,32},{80,48},{96,0},{112,16},{1... | collective-permute-start | bytes 196616 | tf_op jit(solution)/shard_map/ppermute | solution.py:21
  46.2 5.8 %collective-permute-start.15 = (bf16[288,256]{1,0:T(8,128)(2,1)S(1)}, bf16[288,256]{1,0:T(8,128)(2,1)S(1)}, u32[]{:S(2)}, u32[]{:S(2)}) collective-permute-start(bf16[288,256]{1,0:T(8,128)(2,1)S(1)} %get-tuple-element.56), channel_id=1, source_target_pairs={{0,4},{1,5},{2,6},{3,7},{4,0},{5,1},{6,2},{7,3},{8,12},{9,13},{10,... | collective-permute-start | bytes 442376 | tf_op jit(solution)/shard_map/ppermute | solution.py:21
  53.8 7.5 %collective-permute-start.18 = (bf16[2,128,256]{2,1,0:T(8,128)(2,1)S(1)}, bf16[2,128,256]{2,1,0:T(8,128)(2,1)S(1)}, u32[]{:S(2)}, u32[]{:S(2)}) collective-permute-start(bf16[2,128,256]{2,1,0:T(8,128)(2,1)S(1)} %get-tuple-element.57.refs_0_), channel_id=1, source_target_pairs={{0,3},{1,2},{2,1},{3,0},{4,7},{5,6},{6,5},{7,4},{8,11},{9,10},{10,... | collective-permute-start | bytes 393224 | tf_op jit(solution)/shard_map/ppermute | solution.py:21
  55.3 7.0 %collective-permute-start.17 = (bf16[2,128,256]{2,1,0:T(8,128)(2,1)S(1)}, bf16[2,128,256]{2,1,0:T(8,128)(2,1)S(1)}, u32[]{:S(2)}, u32[]{:S(2)}) collective-permute-start(bf16[2,128,256]{2,1,0:T(8,128)(2,1)S(1)} %get-tuple-element.57.refs_0_), channel_id=1, source_target_pairs={{0,2},{1,3},{2,0},{3,1},{4,6},{5,7},{6,4},{7,5},{8,10},{9,11},{10,... | collective-permute-start | bytes 393224 | tf_op jit(solution)/shard_map/ppermute | solution.py:21
  56.4 6.4 %collective-permute-start.16 = (bf16[2,128,256]{2,1,0:T(8,128)(2,1)S(1)}, bf16[2,128,256]{2,1,0:T(8,128)(2,1)S(1)}, u32[]{:S(2)}, u32[]{:S(2)}) collective-permute-start(bf16[2,128,256]{2,1,0:T(8,128)(2,1)S(1)} %get-tuple-element.57.refs_0_), channel_id=1, source_target_pairs={{0,1},{1,0},{2,3},{3,2},{4,5},{5,4},{6,7},{7,6},{8,9},{9,8},{10,11... | collective-permute-start | bytes 393224 | tf_op jit(solution)/shard_map/ppermute | solution.py:21
  66.9 4.8 %collective-permute-start.20 = (bf16[128,256]{1,0:T(8,128)(2,1)S(1)}, bf16[128,256]{1,0:T(8,128)(2,1)S(1)}, u32[]{:S(2)}, u32[]{:S(2)}) collective-permute-start(bf16[128,256]{1,0:T(8,128)(2,1)S(1)} %get-tuple-element.120), channel_id=1, source_target_pairs={{0,32},{16,48},{32,0},{48,16},{64,96},{80,112},{96,64},{112,80},{1... | collective-permute-start | bytes 196616 | tf_op jit(solution)/shard_map/ppermute | solution.py:21
  67.0 7.4 %collective-permute-start.22 = (bf16[128,256]{1,0:T(8,128)(2,1)S(1)}, bf16[128,256]{1,0:T(8,128)(2,1)S(1)}, u32[]{:S(2)}, u32[]{:S(2)}) collective-permute-start(bf16[128,256]{1,0:T(8,128)(2,1)S(1)} %get-tuple-element.121), channel_id=1, source_target_pairs={{0,64},{16,80},{32,96},{48,112},{64,0},{80,16},{96,32},{112,48},{1... | collective-permute-start | bytes 196616 | tf_op jit(solution)/shard_map/ppermute | solution.py:21
  70.8 5.5 %collective-permute-start.21 = (bf16[128,256]{1,0:T(8,128)(2,1)S(1)}, bf16[128,256]{1,0:T(8,128)(2,1)S(1)}, u32[]{:S(2)}, u32[]{:S(2)}) collective-permute-start(bf16[128,256]{1,0:T(8,128)(2,1)S(1)} %get-tuple-element.122), channel_id=1, source_target_pairs={{0,96},{16,112},{32,64},{48,80},{64,32},{80,48},{96,0},{112,16},{1... | collective-permute-start | bytes 196616 | tf_op jit(solution)/shard_map/ppermute | solution.py:21
  81.3 6.7 %collective-permute-start.26 = (bf16[2,128,256]{2,1,0:T(8,128)(2,1)S(1)}, bf16[2,128,256]{2,1,0:T(8,128)(2,1)S(1)}, u32[]{:S(2)}, u32[]{:S(2)}) collective-permute-start(bf16[2,128,256]{2,1,0:T(8,128)(2,1)S(1)} %shard_map.106.refs_0_), channel_id=1, source_target_pairs={{0,3},{1,2},{2,1},{3,0},{4,7},{5,6},{6,5},{7,4},{8,11},{9,10},{10,... | collective-permute-start | bytes 393224 | tf_op jit(solution)/shard_map/ppermute | solution.py:21
  82.7 6.5 %collective-permute-start.25 = (bf16[2,128,256]{2,1,0:T(8,128)(2,1)S(1)}, bf16[2,128,256]{2,1,0:T(8,128)(2,1)S(1)}, u32[]{:S(2)}, u32[]{:S(2)}) collective-permute-start(bf16[2,128,256]{2,1,0:T(8,128)(2,1)S(1)} %shard_map.106.refs_0_), channel_id=1, source_target_pairs={{0,2},{1,3},{2,0},{3,1},{4,6},{5,7},{6,4},{7,5},{8,10},{9,11},{10,... | collective-permute-start | bytes 393224 | tf_op jit(solution)/shard_map/ppermute | solution.py:21
  84.0 5.8 %collective-permute-start.24 = (bf16[2,128,256]{2,1,0:T(8,128)(2,1)S(1)}, bf16[2,128,256]{2,1,0:T(8,128)(2,1)S(1)}, u32[]{:S(2)}, u32[]{:S(2)}) collective-permute-start(bf16[2,128,256]{2,1,0:T(8,128)(2,1)S(1)} %shard_map.106.refs_0_), channel_id=1, source_target_pairs={{0,1},{1,0},{2,3},{3,2},{4,5},{5,4},{6,7},{7,6},{8,9},{9,8},{10,11... | collective-permute-start | bytes 393224 | tf_op jit(solution)/shard_map/ppermute | solution.py:21
  93.9 9.0 %collective-permute-start.28 = (bf16[128,256]{1,0:T(8,128)(2,1)S(1)}, bf16[128,256]{1,0:T(8,128)(2,1)S(1)}, u32[]{:S(2)}, u32[]{:S(2)}) collective-permute-start(bf16[128,256]{1,0:T(8,128)(2,1)S(1)} %get-tuple-element.117), channel_id=1, source_target_pairs={{0,32},{16,48},{32,0},{48,16},{64,96},{80,112},{96,64},{112,80},{1... | collective-permute-start | bytes 196616 | tf_op jit(solution)/shard_map/ppermute | solution.py:21
  94.0 8.9 %collective-permute-start.30 = (bf16[128,256]{1,0:T(8,128)(2,1)S(1)}, bf16[128,256]{1,0:T(8,128)(2,1)S(1)}, u32[]{:S(2)}, u32[]{:S(2)}) collective-permute-start(bf16[128,256]{1,0:T(8,128)(2,1)S(1)} %get-tuple-element.118), channel_id=1, source_target_pairs={{0,64},{16,80},{32,96},{48,112},{64,0},{80,16},{96,32},{112,48},{1... | collective-permute-start | bytes 196616 | tf_op jit(solution)/shard_map/ppermute | solution.py:21
  96.2 6.7 %collective-permute-start.29 = (bf16[128,256]{1,0:T(8,128)(2,1)S(1)}, bf16[128,256]{1,0:T(8,128)(2,1)S(1)}, u32[]{:S(2)}, u32[]{:S(2)}) collective-permute-start(bf16[128,256]{1,0:T(8,128)(2,1)S(1)} %get-tuple-element.119), channel_id=1, source_target_pairs={{0,96},{16,112},{32,64},{48,80},{64,32},{80,48},{96,0},{112,16},{1... | collective-permute-start | bytes 196616 | tf_op jit(solution)/shard_map/ppermute | solution.py:21
  98.6 7.9 %collective-permute-start.35 = (bf16[144,256]{1,0:T(8,128)(2,1)S(1)}, bf16[144,256]{1,0:T(8,128)(2,1)S(1)}, u32[]{:S(2)}, u32[]{:S(2)}) collective-permute-start(bf16[144,256]{1,0:T(8,128)(2,1)S(1)} %get-tuple-element.64), channel_id=1, source_target_pairs={{0,8},{1,9},{2,10},{3,11},{4,12},{5,13},{6,14},{7,15},{8,0},{9,1},... | collective-permute-start | bytes 221192 | tf_op jit(solution)/shard_map/ppermute | solution.py:21
  101.8 5.8 %collective-permute-start.34 = (bf16[144,256]{1,0:T(8,128)(2,1)S(1)}, bf16[144,256]{1,0:T(8,128)(2,1)S(1)}, u32[]{:S(2)}, u32[]{:S(2)}) collective-permute-start(bf16[144,256]{1,0:T(8,128)(2,1)S(1)} %get-tuple-element.64), channel_id=1, source_target_pairs={{0,12},{1,13},{2,14},{3,15},{4,8},{5,9},{6,10},{7,11},{8,4},{9,5},... | collective-permute-start | bytes 221192 | tf_op jit(solution)/shard_map/ppermute | solution.py:21
  103.0 6.3 %collective-permute-start.33 = (bf16[128,256]{1,0:T(8,128)(2,1)S(1)}, bf16[128,256]{1,0:T(8,128)(2,1)S(1)}, u32[]{:S(2)}, u32[]{:S(2)}) collective-permute-start(bf16[128,256]{1,0:T(8,128)(2,1)S(1)} %get-tuple-element.105), channel_id=1, source_target_pairs={{0,8},{1,9},{2,10},{3,11},{4,12},{5,13},{6,14},{7,15},{8,0},{9,1},... | collective-permute-start | bytes 196616 | tf_op jit(solution)/shard_map/ppermute | solution.py:21
  105.0 5.5 %collective-permute-start.32 = (bf16[128,256]{1,0:T(8,128)(2,1)S(1)}, bf16[128,256]{1,0:T(8,128)(2,1)S(1)}, u32[]{:S(2)}, u32[]{:S(2)}) collective-permute-start(bf16[128,256]{1,0:T(8,128)(2,1)S(1)} %get-tuple-element.105), channel_id=1, source_target_pairs={{0,12},{1,13},{2,14},{3,15},{4,8},{5,9},{6,10},{7,11},{8,4},{9,5},... | collective-permute-start | bytes 196616 | tf_op jit(solution)/shard_map/ppermute | solution.py:21
  111.2 12.6 %collective-permute-start.38 = (bf16[4,128,256]{2,1,0:T(8,128)(2,1)S(1)}, bf16[4,128,256]{2,1,0:T(8,128)(2,1)S(1)}, u32[]{:S(2)}, u32[]{:S(2)}) collective-permute-start(bf16[4,128,256]{2,1,0:T(8,128)(2,1)S(1)} %shard_map.108.refs_0_), channel_id=1, source_target_pairs={{0,3},{1,2},{2,1},{3,0},{4,7},{5,6},{6,5},{7,4},{8,11},{9,10},{10,... | collective-permute-start | bytes 786440 | tf_op jit(solution)/shard_map/ppermute | solution.py:21
  112.6 11.1 %collective-permute-start.37 = (bf16[4,128,256]{2,1,0:T(8,128)(2,1)S(1)}, bf16[4,128,256]{2,1,0:T(8,128)(2,1)S(1)}, u32[]{:S(2)}, u32[]{:S(2)}) collective-permute-start(bf16[4,128,256]{2,1,0:T(8,128)(2,1)S(1)} %shard_map.108.refs_0_), channel_id=1, source_target_pairs={{0,2},{1,3},{2,0},{3,1},{4,6},{5,7},{6,4},{7,5},{8,10},{9,11},{10,... | collective-permute-start | bytes 786440 | tf_op jit(solution)/shard_map/ppermute | solution.py:21
  113.9 10.4 %collective-permute-start.36 = (bf16[4,128,256]{2,1,0:T(8,128)(2,1)S(1)}, bf16[4,128,256]{2,1,0:T(8,128)(2,1)S(1)}, u32[]{:S(2)}, u32[]{:S(2)}) collective-permute-start(bf16[4,128,256]{2,1,0:T(8,128)(2,1)S(1)} %shard_map.108.refs_0_), channel_id=1, source_target_pairs={{0,1},{1,0},{2,3},{3,2},{4,5},{5,4},{6,7},{7,6},{8,9},{9,8},{10,11... | collective-permute-start | bytes 786440 | tf_op jit(solution)/shard_map/ppermute | solution.py:21
  129.7 4.8 %collective-permute-start.40 = (bf16[128,256]{1,0:T(8,128)(2,1)S(1)}, bf16[128,256]{1,0:T(8,128)(2,1)S(1)}, u32[]{:S(2)}, u32[]{:S(2)}) collective-permute-start(bf16[128,256]{1,0:T(8,128)(2,1)S(1)} %get-tuple-element.114), channel_id=1, source_target_pairs={{0,32},{16,48},{32,0},{48,16},{64,96},{80,112},{96,64},{112,80},{1... | collective-permute-start | bytes 196616 | tf_op jit(solution)/shard_map/ppermute | solution.py:21
  130.1 7.3 %collective-permute-start.42 = (bf16[128,256]{1,0:T(8,128)(2,1)S(1)}, bf16[128,256]{1,0:T(8,128)(2,1)S(1)}, u32[]{:S(2)}, u32[]{:S(2)}) collective-permute-start(bf16[128,256]{1,0:T(8,128)(2,1)S(1)} %get-tuple-element.115), channel_id=1, source_target_pairs={{0,64},{16,80},{32,96},{48,112},{64,0},{80,16},{96,32},{112,48},{1... | collective-permute-start | bytes 196616 | tf_op jit(solution)/shard_map/ppermute | solution.py:21
  133.9 5.5 %collective-permute-start.41 = (bf16[128,256]{1,0:T(8,128)(2,1)S(1)}, bf16[128,256]{1,0:T(8,128)(2,1)S(1)}, u32[]{:S(2)}, u32[]{:S(2)}) collective-permute-start(bf16[128,256]{1,0:T(8,128)(2,1)S(1)} %get-tuple-element.116), channel_id=1, source_target_pairs={{0,96},{16,112},{32,64},{48,80},{64,32},{80,48},{96,0},{112,16},{1... | collective-permute-start | bytes 196616 | tf_op jit(solution)/shard_map/ppermute | solution.py:21
  140.1 5.9 %collective-permute-start.45 = (bf16[256,128]{1,0:T(8,128)(2,1)S(1)}, bf16[256,128]{1,0:T(8,128)(2,1)S(1)}, u32[]{:S(2)}, u32[]{:S(2)}) collective-permute-start(bf16[256,128]{1,0:T(8,128)(2,1)S(1)} %shard_map.110.refs_0_), channel_id=1, source_target_pairs={{0,64},{16,80},{32,96},{48,112},{64,0},{80,16},{96,32},{112,48},{1... | collective-permute-start | bytes 196616 | tf_op jit(solution)/shard_map/ppermute | solution.py:21
  140.4 6.2 %collective-permute-start.44 = (bf16[256,128]{1,0:T(8,128)(2,1)S(1)}, bf16[256,128]{1,0:T(8,128)(2,1)S(1)}, u32[]{:S(2)}, u32[]{:S(2)}) collective-permute-start(bf16[256,128]{1,0:T(8,128)(2,1)S(1)} %shard_map.110.refs_0_), channel_id=1, source_target_pairs={{0,96},{16,112},{32,64},{48,80},{64,32},{80,48},{96,0},{112,16},{1... | collective-permute-start | bytes 196616 | tf_op jit(solution)/shard_map/ppermute | solution.py:21
  142.0 4.6 %collective-permute-start.43 = (bf16[256,128]{1,0:T(8,128)(2,1)S(1)}, bf16[256,128]{1,0:T(8,128)(2,1)S(1)}, u32[]{:S(2)}, u32[]{:S(2)}) collective-permute-start(bf16[256,128]{1,0:T(8,128)(2,1)S(1)} %shard_map.110.refs_0_), channel_id=1, source_target_pairs={{0,32},{16,48},{32,0},{48,16},{64,96},{80,112},{96,64},{112,80},{1... | collective-permute-start | bytes 196616 | tf_op jit(solution)/shard_map/ppermute | solution.py:21
  150.0 14.8 %collective-permute-start.50 = (bf16[4,256,128]{2,1,0:T(8,128)(2,1)S(1)}, bf16[4,256,128]{2,1,0:T(8,128)(2,1)S(1)}, u32[]{:S(2)}, u32[]{:S(2)}) collective-permute-start(bf16[4,256,128]{2,1,0:T(8,128)(2,1)S(1)} %shard_map.111), channel_id=1, source_target_pairs={{0,2},{1,3},{2,0},{3,1},{4,6},{5,7},{6,4},{7,5},{8,10},{9,11},{10,... | collective-permute-start | bytes 786440 | tf_op jit(solution)/shard_map/ppermute | solution.py:21
  154.1 10.7 %collective-permute-start.51 = (bf16[4,256,128]{2,1,0:T(8,128)(2,1)S(1)}, bf16[4,256,128]{2,1,0:T(8,128)(2,1)S(1)}, u32[]{:S(2)}, u32[]{:S(2)}) collective-permute-start(bf16[4,256,128]{2,1,0:T(8,128)(2,1)S(1)} %shard_map.112), channel_id=1, source_target_pairs={{0,1},{1,0},{2,3},{3,2},{4,5},{5,4},{6,7},{7,6},{8,9},{9,8},{10,11... | collective-permute-start | bytes 786440 | tf_op jit(solution)/shard_map/ppermute | solution.py:21
  156.4 9.7 %collective-permute-start.52 = (bf16[4,256,128]{2,1,0:T(8,128)(2,1)S(1)}, bf16[4,256,128]{2,1,0:T(8,128)(2,1)S(1)}, u32[]{:S(2)}, u32[]{:S(2)}) collective-permute-start(bf16[4,256,128]{2,1,0:T(8,128)(2,1)S(1)} %shard_map.113), channel_id=1, source_target_pairs={{0,3},{1,2},{2,1},{3,0},{4,7},{5,6},{6,5},{7,4},{8,11},{9,10},{10,... | collective-permute-start | bytes 786440 | tf_op jit(solution)/shard_map/ppermute | solution.py:21
  166.2 8.3 %collective-permute-start.55 = (bf16[2,256,128]{2,1,0:T(8,128)(2,1)S(1)}, bf16[2,256,128]{2,1,0:T(8,128)(2,1)S(1)}, u32[]{:S(2)}, u32[]{:S(2)}) collective-permute-start(bf16[2,256,128]{2,1,0:T(8,128)(2,1)S(1)} %get-tuple-element.103), channel_id=1, source_target_pairs={{0,8},{1,9},{2,10},{3,11},{4,12},{5,13},{6,14},{7,15},{8,0},{9,1},... | collective-permute-start | bytes 393224 | tf_op jit(solution)/shard_map/ppermute | solution.py:21
  167.8 7.5 %collective-permute-start.54 = (bf16[2,256,128]{2,1,0:T(8,128)(2,1)S(1)}, bf16[2,256,128]{2,1,0:T(8,128)(2,1)S(1)}, u32[]{:S(2)}, u32[]{:S(2)}) collective-permute-start(bf16[2,256,128]{2,1,0:T(8,128)(2,1)S(1)} %get-tuple-element.113), channel_id=1, source_target_pairs={{0,12},{1,13},{2,14},{3,15},{4,8},{5,9},{6,10},{7,11},{8,4},{9,5},... | collective-permute-start | bytes 393224 | tf_op jit(solution)/shard_map/ppermute | solution.py:21
  168.6 6.7 %collective-permute-start.53 = (bf16[2,256,128]{2,1,0:T(8,128)(2,1)S(1)}, bf16[2,256,128]{2,1,0:T(8,128)(2,1)S(1)}, u32[]{:S(2)}, u32[]{:S(2)}) collective-permute-start(bf16[2,256,128]{2,1,0:T(8,128)(2,1)S(1)} %get-tuple-element.113), channel_id=1, source_target_pairs={{0,4},{1,5},{2,6},{3,7},{4,0},{5,1},{6,2},{7,3},{8,12},{9,13},{10,... | collective-permute-start | bytes 393224 | tf_op jit(solution)/shard_map/ppermute | solution.py:21
  175.5 6.3 %collective-permute-start.58 = (bf16[256,128]{1,0:T(8,128)(2,1)S(1)}, bf16[256,128]{1,0:T(8,128)(2,1)S(1)}, u32[]{:S(2)}, u32[]{:S(2)}) collective-permute-start(bf16[256,128]{1,0:T(8,128)(2,1)S(1)} %get-tuple-element.100.refs_0_.down_ref), channel_id=1, source_target_pairs={{0,64},{16,80},{32,96},{48,112},{64,0},{80,16},{96,32},{112,48},{1... | collective-permute-start | bytes 196616 | tf_op jit(solution)/shard_map/ppermute | solution.py:21
  176.9 5.5 %collective-permute-start.57 = (bf16[256,128]{1,0:T(8,128)(2,1)S(1)}, bf16[256,128]{1,0:T(8,128)(2,1)S(1)}, u32[]{:S(2)}, u32[]{:S(2)}) collective-permute-start(bf16[256,128]{1,0:T(8,128)(2,1)S(1)} %get-tuple-element.100.refs_0_.down_ref), channel_id=1, source_target_pairs={{0,96},{16,112},{32,64},{48,80},{64,32},{80,48},{96,0},{112,16},{1... | collective-permute-start | bytes 196616 | tf_op jit(solution)/shard_map/ppermute | solution.py:21
  187.3 6.4 %collective-permute-start.63 = (bf16[2,256,128]{2,1,0:T(8,128)(2,1)S(1)}, bf16[2,256,128]{2,1,0:T(8,128)(2,1)S(1)}, u32[]{:S(2)}, u32[]{:S(2)}) collective-permute-start(bf16[2,256,128]{2,1,0:T(8,128)(2,1)S(1)} %get-tuple-element.80), channel_id=1, source_target_pairs={{0,1},{1,0},{2,3},{3,2},{4,5},{5,4},{6,7},{7,6},{8,9},{9,8},{10,11... | collective-permute-start | bytes 393224 | tf_op jit(solution)/shard_map/ppermute | solution.py:21
  187.9 9.3 %collective-permute-start.64 = (bf16[2,256,128]{2,1,0:T(8,128)(2,1)S(1)}, bf16[2,256,128]{2,1,0:T(8,128)(2,1)S(1)}, u32[]{:S(2)}, u32[]{:S(2)}) collective-permute-start(bf16[2,256,128]{2,1,0:T(8,128)(2,1)S(1)} %get-tuple-element.81), channel_id=1, source_target_pairs={{0,3},{1,2},{2,1},{3,0},{4,7},{5,6},{6,5},{7,4},{8,11},{9,10},{10,... | collective-permute-start | bytes 393224 | tf_op jit(solution)/shard_map/ppermute | solution.py:21
  189.8 7.4 %collective-permute-start.65 = (bf16[2,256,128]{2,1,0:T(8,128)(2,1)S(1)}, bf16[2,256,128]{2,1,0:T(8,128)(2,1)S(1)}, u32[]{:S(2)}, u32[]{:S(2)}) collective-permute-start(bf16[2,256,128]{2,1,0:T(8,128)(2,1)S(1)} %get-tuple-element.82), channel_id=1, source_target_pairs={{0,2},{1,3},{2,0},{3,1},{4,6},{5,7},{6,4},{7,5},{8,10},{9,11},{10,... | collective-permute-start | bytes 393224 | tf_op jit(solution)/shard_map/ppermute | solution.py:21
  201.7 5.9 %collective-permute-start.69 = (bf16[256,128]{1,0:T(8,128)(2,1)S(1)}, bf16[256,128]{1,0:T(8,128)(2,1)S(1)}, u32[]{:S(2)}, u32[]{:S(2)}) collective-permute-start(bf16[256,128]{1,0:T(8,128)(2,1)S(1)} %fusion.5.refs_0_), channel_id=1, source_target_pairs={{0,64},{16,80},{32,96},{48,112},{64,0},{80,16},{96,32},{112,48},{1... | collective-permute-start | bytes 196616 | tf_op jit(solution)/shard_map/ppermute | solution.py:21
  202.3 5.9 %collective-permute-start.68 = (bf16[256,128]{1,0:T(8,128)(2,1)S(1)}, bf16[256,128]{1,0:T(8,128)(2,1)S(1)}, u32[]{:S(2)}, u32[]{:S(2)}) collective-permute-start(bf16[256,128]{1,0:T(8,128)(2,1)S(1)} %fusion.5.refs_0_), channel_id=1, source_target_pairs={{0,96},{16,112},{32,64},{48,80},{64,32},{80,48},{96,0},{112,16},{1... | collective-permute-start | bytes 196616 | tf_op jit(solution)/shard_map/ppermute | solution.py:21
  212.6 6.4 %collective-permute-start.74 = (bf16[2,256,128]{2,1,0:T(8,128)(2,1)S(1)}, bf16[2,256,128]{2,1,0:T(8,128)(2,1)S(1)}, u32[]{:S(2)}, u32[]{:S(2)}) collective-permute-start(bf16[2,256,128]{2,1,0:T(8,128)(2,1)S(1)} %get-tuple-element.84), channel_id=1, source_target_pairs={{0,1},{1,0},{2,3},{3,2},{4,5},{5,4},{6,7},{7,6},{8,9},{9,8},{10,11... | collective-permute-start | bytes 393224 | tf_op jit(solution)/shard_map/ppermute | solution.py:21
  213.0 7.7 %collective-permute-start.75 = (bf16[2,256,128]{2,1,0:T(8,128)(2,1)S(1)}, bf16[2,256,128]{2,1,0:T(8,128)(2,1)S(1)}, u32[]{:S(2)}, u32[]{:S(2)}) collective-permute-start(bf16[2,256,128]{2,1,0:T(8,128)(2,1)S(1)} %get-tuple-element.85), channel_id=1, source_target_pairs={{0,3},{1,2},{2,1},{3,0},{4,7},{5,6},{6,5},{7,4},{8,11},{9,10},{10,... | collective-permute-start | bytes 393224 | tf_op jit(solution)/shard_map/ppermute | solution.py:21
  214.8 7.7 %collective-permute-start.76 = (bf16[2,256,128]{2,1,0:T(8,128)(2,1)S(1)}, bf16[2,256,128]{2,1,0:T(8,128)(2,1)S(1)}, u32[]{:S(2)}, u32[]{:S(2)}) collective-permute-start(bf16[2,256,128]{2,1,0:T(8,128)(2,1)S(1)} %get-tuple-element.86), channel_id=1, source_target_pairs={{0,2},{1,3},{2,0},{3,1},{4,6},{5,7},{6,4},{7,5},{8,10},{9,11},{10,... | collective-permute-start | bytes 393224 | tf_op jit(solution)/shard_map/ppermute | solution.py:21
  223.1 6.2 %collective-permute-start.77 = (bf16[3,256,128]{2,1,0:T(8,128)(2,1)S(1)}, bf16[3,256,128]{2,1,0:T(8,128)(2,1)S(1)}, u32[]{:S(2)}, u32[]{:S(2)}) collective-permute-start(bf16[3,256,128]{2,1,0:T(8,128)(2,1)S(1)} %get-tuple-element.88), channel_id=1, source_target_pairs={{0,4},{1,5},{2,6},{3,7},{4,0},{5,1},{6,2},{7,3},{8,12},{9,13},{10,... | collective-permute-start | bytes 589832 | tf_op jit(solution)/shard_map/ppermute | solution.py:21
  229.9 6.3 %collective-permute-start.80 = (bf16[256,128]{1,0:T(8,128)(2,1)S(1)}, bf16[256,128]{1,0:T(8,128)(2,1)S(1)}, u32[]{:S(2)}, u32[]{:S(2)}) collective-permute-start(bf16[256,128]{1,0:T(8,128)(2,1)S(1)} %get-tuple-element.89.refs_0_.refs_8_), channel_id=1, source_target_pairs={{0,64},{16,80},{32,96},{48,112},{64,0},{80,16},{96,32},{112,48},{1... | collective-permute-start | bytes 196616 | tf_op jit(solution)/shard_map/ppermute | solution.py:21
  231.7 5.5 %collective-permute-start.79 = (bf16[256,128]{1,0:T(8,128)(2,1)S(1)}, bf16[256,128]{1,0:T(8,128)(2,1)S(1)}, u32[]{:S(2)}, u32[]{:S(2)}) collective-permute-start(bf16[256,128]{1,0:T(8,128)(2,1)S(1)} %get-tuple-element.89.refs_0_.refs_8_), channel_id=1, source_target_pairs={{0,96},{16,112},{32,64},{48,80},{64,32},{80,48},{96,0},{112,16},{1... | collective-permute-start | bytes 196616 | tf_op jit(solution)/shard_map/ppermute | solution.py:21
  241.0 5.6 %collective-permute-start.86 = (bf16[1,256,128]{2,1,0:T(8,128)(2,1)S(1)}, bf16[1,256,128]{2,1,0:T(8,128)(2,1)S(1)}, u32[]{:S(2)}, u32[]{:S(2)}) collective-permute-start(bf16[1,256,128]{2,1,0:T(8,128)(2,1)S(1)} %get-tuple-element.92), channel_id=1, source_target_pairs={{0,3},{1,2},{2,1},{3,0},{4,7},{5,6},{6,5},{7,4},{8,11},{9,10},{10,... | collective-permute-start | bytes 196616 | tf_op jit(solution)/shard_map/ppermute | solution.py:21
  242.8 5.8 %collective-permute-start.87 = (bf16[1,256,128]{2,1,0:T(8,128)(2,1)S(1)}, bf16[1,256,128]{2,1,0:T(8,128)(2,1)S(1)}, u32[]{:S(2)}, u32[]{:S(2)}) collective-permute-start(bf16[1,256,128]{2,1,0:T(8,128)(2,1)S(1)} %get-tuple-element.93), channel_id=1, source_target_pairs={{0,2},{1,3},{2,0},{3,1},{4,6},{5,7},{6,4},{7,5},{8,10},{9,11},{10,... | collective-permute-start | bytes 196616 | tf_op jit(solution)/shard_map/ppermute | solution.py:21
  248.7 5.9 %collective-permute-start.90 = (bf16[256,128]{1,0:T(8,128)(2,1)S(1)}, bf16[256,128]{1,0:T(8,128)(2,1)S(1)}, u32[]{:S(2)}, u32[]{:S(2)}) collective-permute-start(bf16[256,128]{1,0:T(8,128)(2,1)S(1)} %fusion.3.refs_0_), channel_id=1, source_target_pairs={{0,64},{16,80},{32,96},{48,112},{64,0},{80,16},{96,32},{112,48},{1... | collective-permute-start | bytes 196616 | tf_op jit(solution)/shard_map/ppermute | solution.py:21
  249.9 5.5 %collective-permute-start.89 = (bf16[256,128]{1,0:T(8,128)(2,1)S(1)}, bf16[256,128]{1,0:T(8,128)(2,1)S(1)}, u32[]{:S(2)}, u32[]{:S(2)}) collective-permute-start(bf16[256,128]{1,0:T(8,128)(2,1)S(1)} %fusion.3.refs_0_), channel_id=1, source_target_pairs={{0,96},{16,112},{32,64},{48,80},{64,32},{80,48},{96,0},{112,16},{1... | collective-permute-start | bytes 196616 | tf_op jit(solution)/shard_map/ppermute | solution.py:21
  259.1 11.4 %collective-permute-start.97 = (bf16[3,256,128]{2,1,0:T(8,128)(2,1)S(1)}, bf16[3,256,128]{2,1,0:T(8,128)(2,1)S(1)}, u32[]{:S(2)}, u32[]{:S(2)}) collective-permute-start(bf16[3,256,128]{2,1,0:T(8,128)(2,1)S(1)} %get-tuple-element.97), channel_id=1, source_target_pairs={{0,2},{1,3},{2,0},{3,1},{4,6},{5,7},{6,4},{7,5},{8,10},{9,11},{10,... | collective-permute-start | bytes 589832 | tf_op jit(solution)/shard_map/ppermute | solution.py:21
  261.4 8.1 %collective-permute-start.95 = (bf16[2,256,128]{2,1,0:T(8,128)(2,1)S(1)}, bf16[2,256,128]{2,1,0:T(8,128)(2,1)S(1)}, u32[]{:S(2)}, u32[]{:S(2)}) collective-permute-start(bf16[2,256,128]{2,1,0:T(8,128)(2,1)S(1)} %get-tuple-element.95), channel_id=1, source_target_pairs={{0,1},{1,0},{2,3},{3,2},{4,5},{5,4},{6,7},{7,6},{8,9},{9,8},{10,11... | collective-permute-start | bytes 393224 | tf_op jit(solution)/shard_map/ppermute | solution.py:21
  261.5 8.9 %collective-permute-start.96 = (bf16[2,256,128]{2,1,0:T(8,128)(2,1)S(1)}, bf16[2,256,128]{2,1,0:T(8,128)(2,1)S(1)}, u32[]{:S(2)}, u32[]{:S(2)}) collective-permute-start(bf16[2,256,128]{2,1,0:T(8,128)(2,1)S(1)} %get-tuple-element.96), channel_id=1, source_target_pairs={{0,3},{1,2},{2,1},{3,0},{4,7},{5,6},{6,5},{7,4},{8,11},{9,10},{10,... | collective-permute-start | bytes 393224 | tf_op jit(solution)/shard_map/ppermute | solution.py:21
  (49 other events, 333.0 us)

commit v4 on v3

--- a/solution.py
+++ b/solution.py
@@ -152,7 +152,7 @@
             return
         acc = scratch[1]
 
-        @pl.loop(0, 4 * tiles, unroll=tiles)
+        @pl.loop(0, 4 * tiles, unroll=4)
         def _(step):
             k, j = step & 3, step >> 2
             acc[k, j] = block(((s[Y] & mask) ^ j) * 4 + (s[X] ^ k))

time: 273 us -> 285 us (1.044); the launches traced: 272 us -> 279 us
  starting transfers between devices: 102 us -> 112 us
    ppermute x98, starting transfers between devices: 102 us -> 112 us  [swap(): return lax.ppermute(value, axis, [(i, i ^ mask) for i in range(count)])]
  transfers between devices with their start and end apart: 98 -> 98, of which waited for: 68 -> 66; matrix products, arithmetic and copies ran while one was open for 0% -> 0% of each run, Pallas kernels for 9% -> 9%
where the time goes in v4:
time: 285 us; the launch traced here: 279 us
  starting transfers between devices  112 us (39%)
  waiting for transfers between devices  104 us (36%)
  Pallas kernels  51.8 us (18%)
  local copies, waits for them, and re-layouts  9.22 us (3%)
    ppermute x98, starting transfers between devices, swap(): return lax.ppermute(value, axis, [(i, i ^ mask) for i in range(count)])  112 us
    ppermute x98, waiting for transfers between devices, swap(): return lax.ppermute(value, axis, [(i, i ^ mask) for i in range(count)])  104 us
    pallas_call x13, Pallas kernels, call(): pl.pallas_call(body, out_shape=[jax.ShapeDtypeStruct(*o) for o in outs],...  27.5 us
    pallas_call x7, Pallas kernels, relay(): pl.pallas_call(functools.partial(relay_body, groups), grid=(tiles,), out_...  17.5 us
    unnamed x31, local copies, waits for them, and re-layouts  8.49 us
    pallas_call x8, Pallas kernels, small(): pl.pallas_call(body, out_shape=[jax.ShapeDtypeStruct(*o) for o in outs],...  5.85 us
  transfers between devices with their start and end apart: 98, of which 66 were waited for; matrix products, arithmetic and copies ran while one was open for 0% of the time, Pallas kernels for 9%

profile of v4, /device:TPU:0, one launch (start us, length us, event | category | flops | bytes accessed | tf_op | source)
XLA Modules:
  0.0 279.5 jit_solution(9690817379785994197)
XLA Ops:
  4.2 2.9 %collective-permute-start.2 = (bf16[272,256]{1,0:T(8,128)(2,1)S(1)}, bf16[272,256]{1,0:T(8,128)(2,1)S(1)}, u32[]{:S(2)}, u32[]{:S(2)}) collective-permute-start(bf16[272,256]{1,0:T(8,128)(2,1)S(1)} %shard_map.96.refs_0_), channel_id=1, source_target_pairs={{0,3},{1,2},{2,1},{3,0},{4,7},{5,6},{6,5},{7,4},{8,11},{9,10},{10,... | collective-permute-start | bytes 417800 | tf_op jit(solution)/shard_map/ppermute | solution.py:21
  10.7 1.9 shard_map.95.w_ref
  13.1 2.2 collective-permute-done.1.refs_2_
  15.3 2.0 shard_map.97
  18.9 2.0 collective-permute-start.4
  20.9 3.6 %collective-permute-start.6 = (bf16[128,256]{1,0:T(8,128)(2,1)S(1)}, bf16[128,256]{1,0:T(8,128)(2,1)S(1)}, u32[]{:S(2)}, u32[]{:S(2)}) collective-permute-start(bf16[128,256]{1,0:T(8,128)(2,1)S(1)} %get-tuple-element.127), channel_id=1, source_target_pairs={{0,64},{16,80},{32,96},{48,112},{64,0},{80,16},{96,32},{112,48},{1... | collective-permute-start | bytes 196616 | tf_op jit(solution)/shard_map/ppermute | solution.py:21
  24.5 3.5 %collective-permute-done.6 = bf16[128,256]{1,0:T(8,128)(2,1)S(1)} collective-permute-done((bf16[128,256]{1,0:T(8,128)(2,1)S(1)}, bf16[128,256]{1,0:T(8,128)(2,1)S(1)}, u32[]{:S(2)}, u32[]{:S(2)}) %collective-permute-start.6) | collective-permute-done | bytes 65568 | tf_op jit(solution)/shard_map/ppermute | solution.py:21
  28.0 2.0 collective-permute-done.5
  30.0 2.2 collective-permute-start.9
  34.2 1.9 shard_map.99.w_ref
  36.1 1.8 collective-permute-done.8.refs_2_
  38.0 1.8 shard_map.100
  43.3 2.9 %collective-permute-start.12 = (bf16[128,256]{1,0:T(8,128)(2,1)S(1)}, bf16[128,256]{1,0:T(8,128)(2,1)S(1)}, u32[]{:S(2)}, u32[]{:S(2)}) collective-permute-start(bf16[128,256]{1,0:T(8,128)(2,1)S(1)} %get-tuple-element.125), channel_id=1, source_target_pairs={{0,96},{16,112},{32,64},{48,80},{64,32},{80,48},{96,0},{112,16},{1... | collective-permute-start | bytes 196616 | tf_op jit(solution)/shard_map/ppermute | solution.py:21
  58.0 2.5 shard_map.98.w_ref
  62.8 2.4 shard_map.102
  67.0 3.8 %collective-permute-start.22 = (bf16[128,256]{1,0:T(8,128)(2,1)S(1)}, bf16[128,256]{1,0:T(8,128)(2,1)S(1)}, u32[]{:S(2)}, u32[]{:S(2)}) collective-permute-start(bf16[128,256]{1,0:T(8,128)(2,1)S(1)} %get-tuple-element.121), channel_id=1, source_target_pairs={{0,64},{16,80},{32,96},{48,112},{64,0},{80,16},{96,32},{112,48},{1... | collective-permute-start | bytes 196616 | tf_op jit(solution)/shard_map/ppermute | solution.py:21
  71.6 2.7 collective-permute-done.22
  74.4 2.0 collective-permute-done.21
  78.0 2.7 collective-permute-done.23.b_ref
  85.4 2.5 shard_map.105.w_ref
  89.8 2.4 shard_map.107
  94.0 2.3 collective-permute-start.30
  96.2 2.4 collective-permute-start.29
  98.6 3.2 %collective-permute-start.35 = (bf16[144,256]{1,0:T(8,128)(2,1)S(1)}, bf16[144,256]{1,0:T(8,128)(2,1)S(1)}, u32[]{:S(2)}, u32[]{:S(2)}) collective-permute-start(bf16[144,256]{1,0:T(8,128)(2,1)S(1)} %get-tuple-element.64), channel_id=1, source_target_pairs={{0,8},{1,9},{2,10},{3,11},{4,12},{5,13},{6,14},{7,15},{8,0},{9,1},... | collective-permute-start | bytes 221192 | tf_op jit(solution)/shard_map/ppermute | solution.py:21
  103.2 1.8 collective-permute-start.33
  115.4 3.6 %shard_map.104.w_ref = bf16[1024,4096]{1,0:T(8,128)(2,1)S(1)} custom-call(bf16[32768,128]{1,0:T(8,128)(2,1)S(1)} %bitcast.113, bf16[32768,128]{1,0:T(8,128)(2,1)S(1)} %bitcast.114), custom_call_target="tpu_custom_call" | custom-call | flops 2147483648 | bytes 16777216 | tf_op jit(solution)/shard_map/pallas_call | solution.py:57
  119.0 5.1 %collective-permute-done.38.refs_3_ = bf16[4,128,256]{2,1,0:T(8,128)(2,1)S(1)} collective-permute-done((bf16[4,128,256]{2,1,0:T(8,128)(2,1)S(1)}, bf16[4,128,256]{2,1,0:T(8,128)(2,1)S(1)}, u32[]{:S(2)}, u32[]{:S(2)}) %collective-permute-start.38) | collective-permute-done | bytes 262176 | tf_op jit(solution)/shard_map/ppermute | solution.py:21
  124.7 3.7 %shard_map.109 = (f32[4,128,256]{2,1,0:T(8,128)S(1)}, bf16[4,128,256]{2,1,0:T(8,128)(2,1)S(1)}) custom-call(s32[8]{0:T(128)S(1)} %concatenate.3.s, bf16[1024,4096]{1,0:T(8,128)(2,1)S(1)} %shard_map.104.w_ref, bf16[4,128,256]{2,1,0:T(8,128)(2,1)S(1)} %shard_map.108.refs_0_, bf16[4,128,256]{2,1,0:T(8,128)(2,1)S(1)} %collective-permute-done.36.refs_1_, ...), custom_call_target="tpu_custom_call" | custom-call | flops 2147483648 | bytes 1048576 | tf_op jit(solution)/shard_map/pallas_call | solution.py:75
  130.3 3.5 %collective-permute-start.42 = (bf16[128,256]{1,0:T(8,128)(2,1)S(1)}, bf16[128,256]{1,0:T(8,128)(2,1)S(1)}, u32[]{:S(2)}, u32[]{:S(2)}) collective-permute-start(bf16[128,256]{1,0:T(8,128)(2,1)S(1)} %get-tuple-element.115), channel_id=1, source_target_pairs={{0,64},{16,80},{32,96},{48,112},{64,0},{80,16},{96,32},{112,48},{1... | collective-permute-start | bytes 196616 | tf_op jit(solution)/shard_map/ppermute | solution.py:21
  134.8 2.6 collective-permute-done.42
  137.4 2.0 collective-permute-done.41
  143.6 2.3 collective-permute-done.45.refs_3_
  148.0 2.0 shard_map.111
  150.0 2.1 collective-permute-start.50
  152.1 2.0 shard_map.112
  154.4 2.0 shard_map.113
  156.4 1.9 collective-permute-start.52
  158.3 2.5 shard_map.115.w_ref
  160.8 2.0 copy-done.5
  162.9 2.0 shard_map.114
  169.8 2.2 copy-done.2
  172.0 2.5 shard_map.116.w_ref
  177.2 1.9 collective-permute-start.57
  179.1 2.3 collective-permute-done.58.refs_3_
  183.4 9.1 %collective-permute-start.60 = (bf16[256,128]{1,0:T(8,128)(2,1)S(1)}, bf16[256,128]{1,0:T(8,128)(2,1)S(1)}, u32[]{:S(2)}, u32[]{:S(2)}) collective-permute-start(bf16[256,128]{1,0:T(8,128)(2,1)S(1)} %collective-permute-done.56.refs_1_), channel_id=1, source_target_pairs={{0,16},{16,0},{32,48},{48,32},{64,80},{80,64},{96,112},{112,96},{1... | collective-permute-start | bytes 196616 | tf_op jit(solution)/shard_map/ppermute | solution.py:21
  193.7 2.3 shard_map.117
  196.6 1.9 collective-permute-start.64
  200.2 2.2 collective-permute-done.63
  202.4 3.5 %collective-permute-done.64 = bf16[2,256,128]{2,1,0:T(8,128)(2,1)S(1)} collective-permute-done((bf16[2,256,128]{2,1,0:T(8,128)(2,1)S(1)}, bf16[2,256,128]{2,1,0:T(8,128)(2,1)S(1)}, u32[]{:S(2)}, u32[]{:S(2)}) %collective-permute-start.64) | collective-permute-done | bytes 131104 | tf_op jit(solution)/shard_map/ppermute | solution.py:21
  206.8 3.5 %collective-permute-done.66 = bf16[256,128]{1,0:T(8,128)(2,1)S(1)} collective-permute-done((bf16[256,128]{1,0:T(8,128)(2,1)S(1)}, bf16[256,128]{1,0:T(8,128)(2,1)S(1)}, u32[]{:S(2)}, u32[]{:S(2)}) %collective-permute-start.66) | collective-permute-done | bytes 65568 | tf_op jit(solution)/shard_map/ppermute | solution.py:21
  213.9 2.3 collective-permute-done.69.refs_3_
  218.6 2.3 shard_map.118
  221.3 1.8 collective-permute-start.75
  223.1 2.0 collective-permute-start.76
  225.1 2.2 collective-permute-done.74.a
  229.0 1.8 collective-permute-done.76.c
  231.7 5.9 %collective-permute-done.77.got_ref = bf16[3,256,128]{2,1,0:T(8,128)(2,1)S(1)} collective-permute-done((bf16[3,256,128]{2,1,0:T(8,128)(2,1)S(1)}, bf16[3,256,128]{2,1,0:T(8,128)(2,1)S(1)}, u32[]{:S(2)}, u32[]{:S(2)}) %collective-permute-start.77) | collective-permute-done | bytes 196640 | tf_op jit(solution)/shard_map/ppermute | solution.py:21
  241.8 2.7 collective-permute-done.80.refs_3_
  248.7 1.8 collective-permute-start.86
  250.5 2.3 collective-permute-start.87
  254.3 2.0 collective-permute-done.87
  259.9 2.6 collective-permute-done.90.refs_3_
  266.2 2.3 collective-permute-start.97
  270.4 6.3 %collective-permute-done.95.a = bf16[2,256,128]{2,1,0:T(8,128)(2,1)S(1)} collective-permute-done((bf16[2,256,128]{2,1,0:T(8,128)(2,1)S(1)}, bf16[2,256,128]{2,1,0:T(8,128)(2,1)S(1)}, u32[]{:S(2)}, u32[]{:S(2)}) %collective-permute-start.95) | collective-permute-done | bytes 131104 | tf_op jit(solution)/shard_map/ppermute | solution.py:21
  (212 shorter events, 107.8 us)
Async XLA Ops:
  4.2 8.9 %collective-permute-start.2 = (bf16[272,256]{1,0:T(8,128)(2,1)S(1)}, bf16[272,256]{1,0:T(8,128)(2,1)S(1)}, u32[]{:S(2)}, u32[]{:S(2)}) collective-permute-start(bf16[272,256]{1,0:T(8,128)(2,1)S(1)} %shard_map.96.refs_0_), channel_id=1, source_target_pairs={{0,3},{1,2},{2,1},{3,0},{4,7},{5,6},{6,5},{7,4},{8,11},{9,10},{10,... | collective-permute-start | bytes 417800 | tf_op jit(solution)/shard_map/ppermute | solution.py:21
  7.1 8.1 %collective-permute-start.1 = (bf16[272,256]{1,0:T(8,128)(2,1)S(1)}, bf16[272,256]{1,0:T(8,128)(2,1)S(1)}, u32[]{:S(2)}, u32[]{:S(2)}) collective-permute-start(bf16[272,256]{1,0:T(8,128)(2,1)S(1)} %shard_map.96.refs_0_), channel_id=1, source_target_pairs={{0,2},{1,3},{2,0},{3,1},{4,6},{5,7},{6,4},{7,5},{8,10},{9,11},{10,... | collective-permute-start | bytes 417800 | tf_op jit(solution)/shard_map/ppermute | solution.py:21
  7.9 7.3 %collective-permute-start = (bf16[272,256]{1,0:T(8,128)(2,1)S(1)}, bf16[272,256]{1,0:T(8,128)(2,1)S(1)}, u32[]{:S(2)}, u32[]{:S(2)}) collective-permute-start(bf16[272,256]{1,0:T(8,128)(2,1)S(1)} %shard_map.96.refs_0_), channel_id=1, source_target_pairs={{0,1},{1,0},{2,3},{3,2},{4,5},{5,4},{6,7},{7,6},{8,9},{9,8},{10,11... | collective-permute-start | bytes 417800 | tf_op jit(solution)/shard_map/ppermute | solution.py:21
  18.9 5.6 %collective-permute-start.4 = (bf16[128,256]{1,0:T(8,128)(2,1)S(1)}, bf16[128,256]{1,0:T(8,128)(2,1)S(1)}, u32[]{:S(2)}, u32[]{:S(2)}) collective-permute-start(bf16[128,256]{1,0:T(8,128)(2,1)S(1)} %get-tuple-element.126), channel_id=1, source_target_pairs={{0,32},{16,48},{32,0},{48,16},{64,96},{80,112},{96,64},{112,80},{1... | collective-permute-start | bytes 196616 | tf_op jit(solution)/shard_map/ppermute | solution.py:21
  20.9 7.1 %collective-permute-start.6 = (bf16[128,256]{1,0:T(8,128)(2,1)S(1)}, bf16[128,256]{1,0:T(8,128)(2,1)S(1)}, u32[]{:S(2)}, u32[]{:S(2)}) collective-permute-start(bf16[128,256]{1,0:T(8,128)(2,1)S(1)} %get-tuple-element.127), channel_id=1, source_target_pairs={{0,64},{16,80},{32,96},{48,112},{64,0},{80,16},{96,32},{112,48},{1... | collective-permute-start | bytes 196616 | tf_op jit(solution)/shard_map/ppermute | solution.py:21
  24.5 5.5 %collective-permute-start.5 = (bf16[128,256]{1,0:T(8,128)(2,1)S(1)}, bf16[128,256]{1,0:T(8,128)(2,1)S(1)}, u32[]{:S(2)}, u32[]{:S(2)}) collective-permute-start(bf16[128,256]{1,0:T(8,128)(2,1)S(1)} %get-tuple-element.128), channel_id=1, source_target_pairs={{0,96},{16,112},{32,64},{48,80},{64,32},{80,48},{96,0},{112,16},{1... | collective-permute-start | bytes 196616 | tf_op jit(solution)/shard_map/ppermute | solution.py:21
  30.0 6.1 %collective-permute-start.9 = (bf16[128,256]{1,0:T(8,128)(2,1)S(1)}, bf16[128,256]{1,0:T(8,128)(2,1)S(1)}, u32[]{:S(2)}, u32[]{:S(2)}) collective-permute-start(bf16[128,256]{1,0:T(8,128)(2,1)S(1)} %get-tuple-element.111.refs_0_), channel_id=1, source_target_pairs={{0,3},{1,2},{2,1},{3,0},{4,7},{5,6},{6,5},{7,4},{8,11},{9,10},{10,... | collective-permute-start | bytes 196616 | tf_op jit(solution)/shard_map/ppermute | solution.py:21
  32.2 5.8 %collective-permute-start.8 = (bf16[128,256]{1,0:T(8,128)(2,1)S(1)}, bf16[128,256]{1,0:T(8,128)(2,1)S(1)}, u32[]{:S(2)}, u32[]{:S(2)}) collective-permute-start(bf16[128,256]{1,0:T(8,128)(2,1)S(1)} %get-tuple-element.111.refs_0_), channel_id=1, source_target_pairs={{0,2},{1,3},{2,0},{3,1},{4,6},{5,7},{6,4},{7,5},{8,10},{9,11},{10,... | collective-permute-start | bytes 196616 | tf_op jit(solution)/shard_map/ppermute | solution.py:21
  41.4 6.4 %collective-permute-start.11 = (bf16[128,256]{1,0:T(8,128)(2,1)S(1)}, bf16[128,256]{1,0:T(8,128)(2,1)S(1)}, u32[]{:S(2)}, u32[]{:S(2)}) collective-permute-start(bf16[128,256]{1,0:T(8,128)(2,1)S(1)} %get-tuple-element.123), channel_id=1, source_target_pairs={{0,32},{16,48},{32,0},{48,16},{64,96},{80,112},{96,64},{112,80},{1... | collective-permute-start | bytes 196616 | tf_op jit(solution)/shard_map/ppermute | solution.py:21
  41.5 6.3 %collective-permute-start.13 = (bf16[128,256]{1,0:T(8,128)(2,1)S(1)}, bf16[128,256]{1,0:T(8,128)(2,1)S(1)}, u32[]{:S(2)}, u32[]{:S(2)}) collective-permute-start(bf16[128,256]{1,0:T(8,128)(2,1)S(1)} %get-tuple-element.124), channel_id=1, source_target_pairs={{0,64},{16,80},{32,96},{48,112},{64,0},{80,16},{96,32},{112,48},{1... | collective-permute-start | bytes 196616 | tf_op jit(solution)/shard_map/ppermute | solution.py:21
  43.3 5.5 %collective-permute-start.12 = (bf16[128,256]{1,0:T(8,128)(2,1)S(1)}, bf16[128,256]{1,0:T(8,128)(2,1)S(1)}, u32[]{:S(2)}, u32[]{:S(2)}) collective-permute-start(bf16[128,256]{1,0:T(8,128)(2,1)S(1)} %get-tuple-element.125), channel_id=1, source_target_pairs={{0,96},{16,112},{32,64},{48,80},{64,32},{80,48},{96,0},{112,16},{1... | collective-permute-start | bytes 196616 | tf_op jit(solution)/shard_map/ppermute | solution.py:21
  46.2 5.8 %collective-permute-start.15 = (bf16[288,256]{1,0:T(8,128)(2,1)S(1)}, bf16[288,256]{1,0:T(8,128)(2,1)S(1)}, u32[]{:S(2)}, u32[]{:S(2)}) collective-permute-start(bf16[288,256]{1,0:T(8,128)(2,1)S(1)} %get-tuple-element.56), channel_id=1, source_target_pairs={{0,4},{1,5},{2,6},{3,7},{4,0},{5,1},{6,2},{7,3},{8,12},{9,13},{10,... | collective-permute-start | bytes 442376 | tf_op jit(solution)/shard_map/ppermute | solution.py:21
  53.8 7.5 %collective-permute-start.18 = (bf16[2,128,256]{2,1,0:T(8,128)(2,1)S(1)}, bf16[2,128,256]{2,1,0:T(8,128)(2,1)S(1)}, u32[]{:S(2)}, u32[]{:S(2)}) collective-permute-start(bf16[2,128,256]{2,1,0:T(8,128)(2,1)S(1)} %get-tuple-element.57.refs_0_), channel_id=1, source_target_pairs={{0,3},{1,2},{2,1},{3,0},{4,7},{5,6},{6,5},{7,4},{8,11},{9,10},{10,... | collective-permute-start | bytes 393224 | tf_op jit(solution)/shard_map/ppermute | solution.py:21
  55.3 7.0 %collective-permute-start.17 = (bf16[2,128,256]{2,1,0:T(8,128)(2,1)S(1)}, bf16[2,128,256]{2,1,0:T(8,128)(2,1)S(1)}, u32[]{:S(2)}, u32[]{:S(2)}) collective-permute-start(bf16[2,128,256]{2,1,0:T(8,128)(2,1)S(1)} %get-tuple-element.57.refs_0_), channel_id=1, source_target_pairs={{0,2},{1,3},{2,0},{3,1},{4,6},{5,7},{6,4},{7,5},{8,10},{9,11},{10,... | collective-permute-start | bytes 393224 | tf_op jit(solution)/shard_map/ppermute | solution.py:21
  56.4 6.4 %collective-permute-start.16 = (bf16[2,128,256]{2,1,0:T(8,128)(2,1)S(1)}, bf16[2,128,256]{2,1,0:T(8,128)(2,1)S(1)}, u32[]{:S(2)}, u32[]{:S(2)}) collective-permute-start(bf16[2,128,256]{2,1,0:T(8,128)(2,1)S(1)} %get-tuple-element.57.refs_0_), channel_id=1, source_target_pairs={{0,1},{1,0},{2,3},{3,2},{4,5},{5,4},{6,7},{7,6},{8,9},{9,8},{10,11... | collective-permute-start | bytes 393224 | tf_op jit(solution)/shard_map/ppermute | solution.py:21
  67.0 7.4 %collective-permute-start.22 = (bf16[128,256]{1,0:T(8,128)(2,1)S(1)}, bf16[128,256]{1,0:T(8,128)(2,1)S(1)}, u32[]{:S(2)}, u32[]{:S(2)}) collective-permute-start(bf16[128,256]{1,0:T(8,128)(2,1)S(1)} %get-tuple-element.121), channel_id=1, source_target_pairs={{0,64},{16,80},{32,96},{48,112},{64,0},{80,16},{96,32},{112,48},{1... | collective-permute-start | bytes 196616 | tf_op jit(solution)/shard_map/ppermute | solution.py:21
  70.8 5.5 %collective-permute-start.21 = (bf16[128,256]{1,0:T(8,128)(2,1)S(1)}, bf16[128,256]{1,0:T(8,128)(2,1)S(1)}, u32[]{:S(2)}, u32[]{:S(2)}) collective-permute-start(bf16[128,256]{1,0:T(8,128)(2,1)S(1)} %get-tuple-element.122), channel_id=1, source_target_pairs={{0,96},{16,112},{32,64},{48,80},{64,32},{80,48},{96,0},{112,16},{1... | collective-permute-start | bytes 196616 | tf_op jit(solution)/shard_map/ppermute | solution.py:21
  81.3 6.7 %collective-permute-start.26 = (bf16[2,128,256]{2,1,0:T(8,128)(2,1)S(1)}, bf16[2,128,256]{2,1,0:T(8,128)(2,1)S(1)}, u32[]{:S(2)}, u32[]{:S(2)}) collective-permute-start(bf16[2,128,256]{2,1,0:T(8,128)(2,1)S(1)} %shard_map.106.refs_0_), channel_id=1, source_target_pairs={{0,3},{1,2},{2,1},{3,0},{4,7},{5,6},{6,5},{7,4},{8,11},{9,10},{10,... | collective-permute-start | bytes 393224 | tf_op jit(solution)/shard_map/ppermute | solution.py:21
  82.7 6.5 %collective-permute-start.25 = (bf16[2,128,256]{2,1,0:T(8,128)(2,1)S(1)}, bf16[2,128,256]{2,1,0:T(8,128)(2,1)S(1)}, u32[]{:S(2)}, u32[]{:S(2)}) collective-permute-start(bf16[2,128,256]{2,1,0:T(8,128)(2,1)S(1)} %shard_map.106.refs_0_), channel_id=1, source_target_pairs={{0,2},{1,3},{2,0},{3,1},{4,6},{5,7},{6,4},{7,5},{8,10},{9,11},{10,... | collective-permute-start | bytes 393224 | tf_op jit(solution)/shard_map/ppermute | solution.py:21
  84.0 5.7 %collective-permute-start.24 = (bf16[2,128,256]{2,1,0:T(8,128)(2,1)S(1)}, bf16[2,128,256]{2,1,0:T(8,128)(2,1)S(1)}, u32[]{:S(2)}, u32[]{:S(2)}) collective-permute-start(bf16[2,128,256]{2,1,0:T(8,128)(2,1)S(1)} %shard_map.106.refs_0_), channel_id=1, source_target_pairs={{0,1},{1,0},{2,3},{3,2},{4,5},{5,4},{6,7},{7,6},{8,9},{9,8},{10,11... | collective-permute-start | bytes 393224 | tf_op jit(solution)/shard_map/ppermute | solution.py:21
  93.9 9.3 %collective-permute-start.28 = (bf16[128,256]{1,0:T(8,128)(2,1)S(1)}, bf16[128,256]{1,0:T(8,128)(2,1)S(1)}, u32[]{:S(2)}, u32[]{:S(2)}) collective-permute-start(bf16[128,256]{1,0:T(8,128)(2,1)S(1)} %get-tuple-element.117), channel_id=1, source_target_pairs={{0,32},{16,48},{32,0},{48,16},{64,96},{80,112},{96,64},{112,80},{1... | collective-permute-start | bytes 196616 | tf_op jit(solution)/shard_map/ppermute | solution.py:21
  94.0 9.2 %collective-permute-start.30 = (bf16[128,256]{1,0:T(8,128)(2,1)S(1)}, bf16[128,256]{1,0:T(8,128)(2,1)S(1)}, u32[]{:S(2)}, u32[]{:S(2)}) collective-permute-start(bf16[128,256]{1,0:T(8,128)(2,1)S(1)} %get-tuple-element.118), channel_id=1, source_target_pairs={{0,64},{16,80},{32,96},{48,112},{64,0},{80,16},{96,32},{112,48},{1... | collective-permute-start | bytes 196616 | tf_op jit(solution)/shard_map/ppermute | solution.py:21
  96.2 6.9 %collective-permute-start.29 = (bf16[128,256]{1,0:T(8,128)(2,1)S(1)}, bf16[128,256]{1,0:T(8,128)(2,1)S(1)}, u32[]{:S(2)}, u32[]{:S(2)}) collective-permute-start(bf16[128,256]{1,0:T(8,128)(2,1)S(1)} %get-tuple-element.119), channel_id=1, source_target_pairs={{0,96},{16,112},{32,64},{48,80},{64,32},{80,48},{96,0},{112,16},{1... | collective-permute-start | bytes 196616 | tf_op jit(solution)/shard_map/ppermute | solution.py:21
  98.6 8.1 %collective-permute-start.35 = (bf16[144,256]{1,0:T(8,128)(2,1)S(1)}, bf16[144,256]{1,0:T(8,128)(2,1)S(1)}, u32[]{:S(2)}, u32[]{:S(2)}) collective-permute-start(bf16[144,256]{1,0:T(8,128)(2,1)S(1)} %get-tuple-element.64), channel_id=1, source_target_pairs={{0,8},{1,9},{2,10},{3,11},{4,12},{5,13},{6,14},{7,15},{8,0},{9,1},... | collective-permute-start | bytes 221192 | tf_op jit(solution)/shard_map/ppermute | solution.py:21
  101.8 6.3 %collective-permute-start.34 = (bf16[144,256]{1,0:T(8,128)(2,1)S(1)}, bf16[144,256]{1,0:T(8,128)(2,1)S(1)}, u32[]{:S(2)}, u32[]{:S(2)}) collective-permute-start(bf16[144,256]{1,0:T(8,128)(2,1)S(1)} %get-tuple-element.64), channel_id=1, source_target_pairs={{0,12},{1,13},{2,14},{3,15},{4,8},{5,9},{6,10},{7,11},{8,4},{9,5},... | collective-permute-start | bytes 221192 | tf_op jit(solution)/shard_map/ppermute | solution.py:21
  103.2 6.5 %collective-permute-start.33 = (bf16[128,256]{1,0:T(8,128)(2,1)S(1)}, bf16[128,256]{1,0:T(8,128)(2,1)S(1)}, u32[]{:S(2)}, u32[]{:S(2)}) collective-permute-start(bf16[128,256]{1,0:T(8,128)(2,1)S(1)} %get-tuple-element.105), channel_id=1, source_target_pairs={{0,8},{1,9},{2,10},{3,11},{4,12},{5,13},{6,14},{7,15},{8,0},{9,1},... | collective-permute-start | bytes 196616 | tf_op jit(solution)/shard_map/ppermute | solution.py:21
  105.0 5.5 %collective-permute-start.32 = (bf16[128,256]{1,0:T(8,128)(2,1)S(1)}, bf16[128,256]{1,0:T(8,128)(2,1)S(1)}, u32[]{:S(2)}, u32[]{:S(2)}) collective-permute-start(bf16[128,256]{1,0:T(8,128)(2,1)S(1)} %get-tuple-element.105), channel_id=1, source_target_pairs={{0,12},{1,13},{2,14},{3,15},{4,8},{5,9},{6,10},{7,11},{8,4},{9,5},... | collective-permute-start | bytes 196616 | tf_op jit(solution)/shard_map/ppermute | solution.py:21
  111.2 12.9 %collective-permute-start.38 = (bf16[4,128,256]{2,1,0:T(8,128)(2,1)S(1)}, bf16[4,128,256]{2,1,0:T(8,128)(2,1)S(1)}, u32[]{:S(2)}, u32[]{:S(2)}) collective-permute-start(bf16[4,128,256]{2,1,0:T(8,128)(2,1)S(1)} %shard_map.108.refs_0_), channel_id=1, source_target_pairs={{0,3},{1,2},{2,1},{3,0},{4,7},{5,6},{6,5},{7,4},{8,11},{9,10},{10,... | collective-permute-start | bytes 786440 | tf_op jit(solution)/shard_map/ppermute | solution.py:21
  112.6 11.4 %collective-permute-start.37 = (bf16[4,128,256]{2,1,0:T(8,128)(2,1)S(1)}, bf16[4,128,256]{2,1,0:T(8,128)(2,1)S(1)}, u32[]{:S(2)}, u32[]{:S(2)}) collective-permute-start(bf16[4,128,256]{2,1,0:T(8,128)(2,1)S(1)} %shard_map.108.refs_0_), channel_id=1, source_target_pairs={{0,2},{1,3},{2,0},{3,1},{4,6},{5,7},{6,4},{7,5},{8,10},{9,11},{10,... | collective-permute-start | bytes 786440 | tf_op jit(solution)/shard_map/ppermute | solution.py:21
  113.9 10.7 %collective-permute-start.36 = (bf16[4,128,256]{2,1,0:T(8,128)(2,1)S(1)}, bf16[4,128,256]{2,1,0:T(8,128)(2,1)S(1)}, u32[]{:S(2)}, u32[]{:S(2)}) collective-permute-start(bf16[4,128,256]{2,1,0:T(8,128)(2,1)S(1)} %shard_map.108.refs_0_), channel_id=1, source_target_pairs={{0,1},{1,0},{2,3},{3,2},{4,5},{5,4},{6,7},{7,6},{8,9},{9,8},{10,11... | collective-permute-start | bytes 786440 | tf_op jit(solution)/shard_map/ppermute | solution.py:21
  130.3 7.1 %collective-permute-start.42 = (bf16[128,256]{1,0:T(8,128)(2,1)S(1)}, bf16[128,256]{1,0:T(8,128)(2,1)S(1)}, u32[]{:S(2)}, u32[]{:S(2)}) collective-permute-start(bf16[128,256]{1,0:T(8,128)(2,1)S(1)} %get-tuple-element.115), channel_id=1, source_target_pairs={{0,64},{16,80},{32,96},{48,112},{64,0},{80,16},{96,32},{112,48},{1... | collective-permute-start | bytes 196616 | tf_op jit(solution)/shard_map/ppermute | solution.py:21
  133.9 5.5 %collective-permute-start.41 = (bf16[128,256]{1,0:T(8,128)(2,1)S(1)}, bf16[128,256]{1,0:T(8,128)(2,1)S(1)}, u32[]{:S(2)}, u32[]{:S(2)}) collective-permute-start(bf16[128,256]{1,0:T(8,128)(2,1)S(1)} %get-tuple-element.116), channel_id=1, source_target_pairs={{0,96},{16,112},{32,64},{48,80},{64,32},{80,48},{96,0},{112,16},{1... | collective-permute-start | bytes 196616 | tf_op jit(solution)/shard_map/ppermute | solution.py:21
  140.1 5.9 %collective-permute-start.45 = (bf16[256,128]{1,0:T(8,128)(2,1)S(1)}, bf16[256,128]{1,0:T(8,128)(2,1)S(1)}, u32[]{:S(2)}, u32[]{:S(2)}) collective-permute-start(bf16[256,128]{1,0:T(8,128)(2,1)S(1)} %shard_map.110.refs_0_), channel_id=1, source_target_pairs={{0,64},{16,80},{32,96},{48,112},{64,0},{80,16},{96,32},{112,48},{1... | collective-permute-start | bytes 196616 | tf_op jit(solution)/shard_map/ppermute | solution.py:21
  140.4 6.2 %collective-permute-start.44 = (bf16[256,128]{1,0:T(8,128)(2,1)S(1)}, bf16[256,128]{1,0:T(8,128)(2,1)S(1)}, u32[]{:S(2)}, u32[]{:S(2)}) collective-permute-start(bf16[256,128]{1,0:T(8,128)(2,1)S(1)} %shard_map.110.refs_0_), channel_id=1, source_target_pairs={{0,96},{16,112},{32,64},{48,80},{64,32},{80,48},{96,0},{112,16},{1... | collective-permute-start | bytes 196616 | tf_op jit(solution)/shard_map/ppermute | solution.py:21
  150.0 14.8 %collective-permute-start.50 = (bf16[4,256,128]{2,1,0:T(8,128)(2,1)S(1)}, bf16[4,256,128]{2,1,0:T(8,128)(2,1)S(1)}, u32[]{:S(2)}, u32[]{:S(2)}) collective-permute-start(bf16[4,256,128]{2,1,0:T(8,128)(2,1)S(1)} %shard_map.111), channel_id=1, source_target_pairs={{0,2},{1,3},{2,0},{3,1},{4,6},{5,7},{6,4},{7,5},{8,10},{9,11},{10,... | collective-permute-start | bytes 786440 | tf_op jit(solution)/shard_map/ppermute | solution.py:21
  154.1 10.7 %collective-permute-start.51 = (bf16[4,256,128]{2,1,0:T(8,128)(2,1)S(1)}, bf16[4,256,128]{2,1,0:T(8,128)(2,1)S(1)}, u32[]{:S(2)}, u32[]{:S(2)}) collective-permute-start(bf16[4,256,128]{2,1,0:T(8,128)(2,1)S(1)} %shard_map.112), channel_id=1, source_target_pairs={{0,1},{1,0},{2,3},{3,2},{4,5},{5,4},{6,7},{7,6},{8,9},{9,8},{10,11... | collective-permute-start | bytes 786440 | tf_op jit(solution)/shard_map/ppermute | solution.py:21
  156.4 9.7 %collective-permute-start.52 = (bf16[4,256,128]{2,1,0:T(8,128)(2,1)S(1)}, bf16[4,256,128]{2,1,0:T(8,128)(2,1)S(1)}, u32[]{:S(2)}, u32[]{:S(2)}) collective-permute-start(bf16[4,256,128]{2,1,0:T(8,128)(2,1)S(1)} %shard_map.113), channel_id=1, source_target_pairs={{0,3},{1,2},{2,1},{3,0},{4,7},{5,6},{6,5},{7,4},{8,11},{9,10},{10,... | collective-permute-start | bytes 786440 | tf_op jit(solution)/shard_map/ppermute | solution.py:21
  166.2 8.3 %collective-permute-start.55 = (bf16[2,256,128]{2,1,0:T(8,128)(2,1)S(1)}, bf16[2,256,128]{2,1,0:T(8,128)(2,1)S(1)}, u32[]{:S(2)}, u32[]{:S(2)}) collective-permute-start(bf16[2,256,128]{2,1,0:T(8,128)(2,1)S(1)} %get-tuple-element.103), channel_id=1, source_target_pairs={{0,8},{1,9},{2,10},{3,11},{4,12},{5,13},{6,14},{7,15},{8,0},{9,1},... | collective-permute-start | bytes 393224 | tf_op jit(solution)/shard_map/ppermute | solution.py:21
  167.8 7.5 %collective-permute-start.54 = (bf16[2,256,128]{2,1,0:T(8,128)(2,1)S(1)}, bf16[2,256,128]{2,1,0:T(8,128)(2,1)S(1)}, u32[]{:S(2)}, u32[]{:S(2)}) collective-permute-start(bf16[2,256,128]{2,1,0:T(8,128)(2,1)S(1)} %get-tuple-element.113), channel_id=1, source_target_pairs={{0,12},{1,13},{2,14},{3,15},{4,8},{5,9},{6,10},{7,11},{8,4},{9,5},... | collective-permute-start | bytes 393224 | tf_op jit(solution)/shard_map/ppermute | solution.py:21
  168.6 6.7 %collective-permute-start.53 = (bf16[2,256,128]{2,1,0:T(8,128)(2,1)S(1)}, bf16[2,256,128]{2,1,0:T(8,128)(2,1)S(1)}, u32[]{:S(2)}, u32[]{:S(2)}) collective-permute-start(bf16[2,256,128]{2,1,0:T(8,128)(2,1)S(1)} %get-tuple-element.113), channel_id=1, source_target_pairs={{0,4},{1,5},{2,6},{3,7},{4,0},{5,1},{6,2},{7,3},{8,12},{9,13},{10,... | collective-permute-start | bytes 393224 | tf_op jit(solution)/shard_map/ppermute | solution.py:21
  175.5 6.0 %collective-permute-start.58 = (bf16[256,128]{1,0:T(8,128)(2,1)S(1)}, bf16[256,128]{1,0:T(8,128)(2,1)S(1)}, u32[]{:S(2)}, u32[]{:S(2)}) collective-permute-start(bf16[256,128]{1,0:T(8,128)(2,1)S(1)} %get-tuple-element.100.refs_0_.down_ref), channel_id=1, source_target_pairs={{0,64},{16,80},{32,96},{48,112},{64,0},{80,16},{96,32},{112,48},{1... | collective-permute-start | bytes 196616 | tf_op jit(solution)/shard_map/ppermute | solution.py:21
  177.2 5.5 %collective-permute-start.57 = (bf16[256,128]{1,0:T(8,128)(2,1)S(1)}, bf16[256,128]{1,0:T(8,128)(2,1)S(1)}, u32[]{:S(2)}, u32[]{:S(2)}) collective-permute-start(bf16[256,128]{1,0:T(8,128)(2,1)S(1)} %get-tuple-element.100.refs_0_.down_ref), channel_id=1, source_target_pairs={{0,96},{16,112},{32,64},{48,80},{64,32},{80,48},{96,0},{112,16},{1... | collective-permute-start | bytes 196616 | tf_op jit(solution)/shard_map/ppermute | solution.py:21
  179.1 13.3 %collective-permute-start.59 = (bf16[256,128]{1,0:T(8,128)(2,1)S(1)}, bf16[256,128]{1,0:T(8,128)(2,1)S(1)}, u32[]{:S(2)}, u32[]{:S(2)}) collective-permute-start(bf16[256,128]{1,0:T(8,128)(2,1)S(1)} %get-tuple-element.100.refs_0_.down_ref), channel_id=1, source_target_pairs={{0,16},{16,0},{32,48},{48,32},{64,80},{80,64},{96,112},{112,96},{1... | collective-permute-start | bytes 196616 | tf_op jit(solution)/shard_map/ppermute | solution.py:21
  181.4 11.1 %collective-permute-start.62 = (bf16[256,128]{1,0:T(8,128)(2,1)S(1)}, bf16[256,128]{1,0:T(8,128)(2,1)S(1)}, u32[]{:S(2)}, u32[]{:S(2)}) collective-permute-start(bf16[256,128]{1,0:T(8,128)(2,1)S(1)} %collective-permute-done.58.refs_3_), channel_id=1, source_target_pairs={{0,16},{16,0},{32,48},{48,32},{64,80},{80,64},{96,112},{112,96},{1... | collective-permute-start | bytes 196616 | tf_op jit(solution)/shard_map/ppermute | solution.py:21
  182.7 9.8 %collective-permute-start.61 = (bf16[256,128]{1,0:T(8,128)(2,1)S(1)}, bf16[256,128]{1,0:T(8,128)(2,1)S(1)}, u32[]{:S(2)}, u32[]{:S(2)}) collective-permute-start(bf16[256,128]{1,0:T(8,128)(2,1)S(1)} %collective-permute-done.57.refs_2_), channel_id=1, source_target_pairs={{0,16},{16,0},{32,48},{48,32},{64,80},{80,64},{96,112},{112,96},{1... | collective-permute-start | bytes 196616 | tf_op jit(solution)/shard_map/ppermute | solution.py:21
  183.4 10.3 %collective-permute-start.60 = (bf16[256,128]{1,0:T(8,128)(2,1)S(1)}, bf16[256,128]{1,0:T(8,128)(2,1)S(1)}, u32[]{:S(2)}, u32[]{:S(2)}) collective-permute-start(bf16[256,128]{1,0:T(8,128)(2,1)S(1)} %collective-permute-done.56.refs_1_), channel_id=1, source_target_pairs={{0,16},{16,0},{32,48},{48,32},{64,80},{80,64},{96,112},{112,96},{1... | collective-permute-start | bytes 196616 | tf_op jit(solution)/shard_map/ppermute | solution.py:21
  196.0 6.4 %collective-permute-start.63 = (bf16[2,256,128]{2,1,0:T(8,128)(2,1)S(1)}, bf16[2,256,128]{2,1,0:T(8,128)(2,1)S(1)}, u32[]{:S(2)}, u32[]{:S(2)}) collective-permute-start(bf16[2,256,128]{2,1,0:T(8,128)(2,1)S(1)} %get-tuple-element.80), channel_id=1, source_target_pairs={{0,1},{1,0},{2,3},{3,2},{4,5},{5,4},{6,7},{7,6},{8,9},{9,8},{10,11... | collective-permute-start | bytes 393224 | tf_op jit(solution)/shard_map/ppermute | solution.py:21
  196.6 9.3 %collective-permute-start.64 = (bf16[2,256,128]{2,1,0:T(8,128)(2,1)S(1)}, bf16[2,256,128]{2,1,0:T(8,128)(2,1)S(1)}, u32[]{:S(2)}, u32[]{:S(2)}) collective-permute-start(bf16[2,256,128]{2,1,0:T(8,128)(2,1)S(1)} %get-tuple-element.81), channel_id=1, source_target_pairs={{0,3},{1,2},{2,1},{3,0},{4,7},{5,6},{6,5},{7,4},{8,11},{9,10},{10,... | collective-permute-start | bytes 393224 | tf_op jit(solution)/shard_map/ppermute | solution.py:21
  198.5 7.4 %collective-permute-start.65 = (bf16[2,256,128]{2,1,0:T(8,128)(2,1)S(1)}, bf16[2,256,128]{2,1,0:T(8,128)(2,1)S(1)}, u32[]{:S(2)}, u32[]{:S(2)}) collective-permute-start(bf16[2,256,128]{2,1,0:T(8,128)(2,1)S(1)} %get-tuple-element.82), channel_id=1, source_target_pairs={{0,2},{1,3},{2,0},{3,1},{4,6},{5,7},{6,4},{7,5},{8,10},{9,11},{10,... | collective-permute-start | bytes 393224 | tf_op jit(solution)/shard_map/ppermute | solution.py:21
  210.3 5.9 %collective-permute-start.69 = (bf16[256,128]{1,0:T(8,128)(2,1)S(1)}, bf16[256,128]{1,0:T(8,128)(2,1)S(1)}, u32[]{:S(2)}, u32[]{:S(2)}) collective-permute-start(bf16[256,128]{1,0:T(8,128)(2,1)S(1)} %fusion.5.refs_0_), channel_id=1, source_target_pairs={{0,64},{16,80},{32,96},{48,112},{64,0},{80,16},{96,32},{112,48},{1... | collective-permute-start | bytes 196616 | tf_op jit(solution)/shard_map/ppermute | solution.py:21
  211.3 5.6 %collective-permute-start.68 = (bf16[256,128]{1,0:T(8,128)(2,1)S(1)}, bf16[256,128]{1,0:T(8,128)(2,1)S(1)}, u32[]{:S(2)}, u32[]{:S(2)}) collective-permute-start(bf16[256,128]{1,0:T(8,128)(2,1)S(1)} %fusion.5.refs_0_), channel_id=1, source_target_pairs={{0,96},{16,112},{32,64},{48,80},{64,32},{80,48},{96,0},{112,16},{1... | collective-permute-start | bytes 196616 | tf_op jit(solution)/shard_map/ppermute | solution.py:21
  220.9 6.4 %collective-permute-start.74 = (bf16[2,256,128]{2,1,0:T(8,128)(2,1)S(1)}, bf16[2,256,128]{2,1,0:T(8,128)(2,1)S(1)}, u32[]{:S(2)}, u32[]{:S(2)}) collective-permute-start(bf16[2,256,128]{2,1,0:T(8,128)(2,1)S(1)} %get-tuple-element.84), channel_id=1, source_target_pairs={{0,1},{1,0},{2,3},{3,2},{4,5},{5,4},{6,7},{7,6},{8,9},{9,8},{10,11... | collective-permute-start | bytes 393224 | tf_op jit(solution)/shard_map/ppermute | solution.py:21
  221.3 7.8 %collective-permute-start.75 = (bf16[2,256,128]{2,1,0:T(8,128)(2,1)S(1)}, bf16[2,256,128]{2,1,0:T(8,128)(2,1)S(1)}, u32[]{:S(2)}, u32[]{:S(2)}) collective-permute-start(bf16[2,256,128]{2,1,0:T(8,128)(2,1)S(1)} %get-tuple-element.85), channel_id=1, source_target_pairs={{0,3},{1,2},{2,1},{3,0},{4,7},{5,6},{6,5},{7,4},{8,11},{9,10},{10,... | collective-permute-start | bytes 393224 | tf_op jit(solution)/shard_map/ppermute | solution.py:21
  223.1 7.7 %collective-permute-start.76 = (bf16[2,256,128]{2,1,0:T(8,128)(2,1)S(1)}, bf16[2,256,128]{2,1,0:T(8,128)(2,1)S(1)}, u32[]{:S(2)}, u32[]{:S(2)}) collective-permute-start(bf16[2,256,128]{2,1,0:T(8,128)(2,1)S(1)} %get-tuple-element.86), channel_id=1, source_target_pairs={{0,2},{1,3},{2,0},{3,1},{4,6},{5,7},{6,4},{7,5},{8,10},{9,11},{10,... | collective-permute-start | bytes 393224 | tf_op jit(solution)/shard_map/ppermute | solution.py:21
  231.4 6.2 %collective-permute-start.77 = (bf16[3,256,128]{2,1,0:T(8,128)(2,1)S(1)}, bf16[3,256,128]{2,1,0:T(8,128)(2,1)S(1)}, u32[]{:S(2)}, u32[]{:S(2)}) collective-permute-start(bf16[3,256,128]{2,1,0:T(8,128)(2,1)S(1)} %get-tuple-element.88), channel_id=1, source_target_pairs={{0,4},{1,5},{2,6},{3,7},{4,0},{5,1},{6,2},{7,3},{8,12},{9,13},{10,... | collective-permute-start | bytes 589832 | tf_op jit(solution)/shard_map/ppermute | solution.py:21
  238.2 6.3 %collective-permute-start.80 = (bf16[256,128]{1,0:T(8,128)(2,1)S(1)}, bf16[256,128]{1,0:T(8,128)(2,1)S(1)}, u32[]{:S(2)}, u32[]{:S(2)}) collective-permute-start(bf16[256,128]{1,0:T(8,128)(2,1)S(1)} %get-tuple-element.89.refs_0_.refs_8_), channel_id=1, source_target_pairs={{0,64},{16,80},{32,96},{48,112},{64,0},{80,16},{96,32},{112,48},{1... | collective-permute-start | bytes 196616 | tf_op jit(solution)/shard_map/ppermute | solution.py:21
  240.0 5.5 %collective-permute-start.79 = (bf16[256,128]{1,0:T(8,128)(2,1)S(1)}, bf16[256,128]{1,0:T(8,128)(2,1)S(1)}, u32[]{:S(2)}, u32[]{:S(2)}) collective-permute-start(bf16[256,128]{1,0:T(8,128)(2,1)S(1)} %get-tuple-element.89.refs_0_.refs_8_), channel_id=1, source_target_pairs={{0,96},{16,112},{32,64},{48,80},{64,32},{80,48},{96,0},{112,16},{1... | collective-permute-start | bytes 196616 | tf_op jit(solution)/shard_map/ppermute | solution.py:21
  248.7 5.6 %collective-permute-start.86 = (bf16[1,256,128]{2,1,0:T(8,128)(2,1)S(1)}, bf16[1,256,128]{2,1,0:T(8,128)(2,1)S(1)}, u32[]{:S(2)}, u32[]{:S(2)}) collective-permute-start(bf16[1,256,128]{2,1,0:T(8,128)(2,1)S(1)} %get-tuple-element.92), channel_id=1, source_target_pairs={{0,3},{1,2},{2,1},{3,0},{4,7},{5,6},{6,5},{7,4},{8,11},{9,10},{10,... | collective-permute-start | bytes 196616 | tf_op jit(solution)/shard_map/ppermute | solution.py:21
  250.5 5.8 %collective-permute-start.87 = (bf16[1,256,128]{2,1,0:T(8,128)(2,1)S(1)}, bf16[1,256,128]{2,1,0:T(8,128)(2,1)S(1)}, u32[]{:S(2)}, u32[]{:S(2)}) collective-permute-start(bf16[1,256,128]{2,1,0:T(8,128)(2,1)S(1)} %get-tuple-element.93), channel_id=1, source_target_pairs={{0,2},{1,3},{2,0},{3,1},{4,6},{5,7},{6,4},{7,5},{8,10},{9,11},{10,... | collective-permute-start | bytes 196616 | tf_op jit(solution)/shard_map/ppermute | solution.py:21
  256.4 6.2 %collective-permute-start.90 = (bf16[256,128]{1,0:T(8,128)(2,1)S(1)}, bf16[256,128]{1,0:T(8,128)(2,1)S(1)}, u32[]{:S(2)}, u32[]{:S(2)}) collective-permute-start(bf16[256,128]{1,0:T(8,128)(2,1)S(1)} %fusion.3.refs_0_), channel_id=1, source_target_pairs={{0,64},{16,80},{32,96},{48,112},{64,0},{80,16},{96,32},{112,48},{1... | collective-permute-start | bytes 196616 | tf_op jit(solution)/shard_map/ppermute | solution.py:21
  257.9 5.5 %collective-permute-start.89 = (bf16[256,128]{1,0:T(8,128)(2,1)S(1)}, bf16[256,128]{1,0:T(8,128)(2,1)S(1)}, u32[]{:S(2)}, u32[]{:S(2)}) collective-permute-start(bf16[256,128]{1,0:T(8,128)(2,1)S(1)} %fusion.3.refs_0_), channel_id=1, source_target_pairs={{0,96},{16,112},{32,64},{48,80},{64,32},{80,48},{96,0},{112,16},{1... | collective-permute-start | bytes 196616 | tf_op jit(solution)/shard_map/ppermute | solution.py:21
  266.2 11.6 %collective-permute-start.97 = (bf16[3,256,128]{2,1,0:T(8,128)(2,1)S(1)}, bf16[3,256,128]{2,1,0:T(8,128)(2,1)S(1)}, u32[]{:S(2)}, u32[]{:S(2)}) collective-permute-start(bf16[3,256,128]{2,1,0:T(8,128)(2,1)S(1)} %get-tuple-element.97), channel_id=1, source_target_pairs={{0,2},{1,3},{2,0},{3,1},{4,6},{5,7},{6,4},{7,5},{8,10},{9,11},{10,... | collective-permute-start | bytes 589832 | tf_op jit(solution)/shard_map/ppermute | solution.py:21
  268.5 8.2 %collective-permute-start.95 = (bf16[2,256,128]{2,1,0:T(8,128)(2,1)S(1)}, bf16[2,256,128]{2,1,0:T(8,128)(2,1)S(1)}, u32[]{:S(2)}, u32[]{:S(2)}) collective-permute-start(bf16[2,256,128]{2,1,0:T(8,128)(2,1)S(1)} %get-tuple-element.95), channel_id=1, source_target_pairs={{0,1},{1,0},{2,3},{3,2},{4,5},{5,4},{6,7},{7,6},{8,9},{9,8},{10,11... | collective-permute-start | bytes 393224 | tf_op jit(solution)/shard_map/ppermute | solution.py:21
  268.7 9.1 %collective-permute-start.96 = (bf16[2,256,128]{2,1,0:T(8,128)(2,1)S(1)}, bf16[2,256,128]{2,1,0:T(8,128)(2,1)S(1)}, u32[]{:S(2)}, u32[]{:S(2)}) collective-permute-start(bf16[2,256,128]{2,1,0:T(8,128)(2,1)S(1)} %get-tuple-element.96), channel_id=1, source_target_pairs={{0,3},{1,2},{2,1},{3,0},{4,7},{5,6},{6,5},{7,4},{8,11},{9,10},{10,... | collective-permute-start | bytes 393224 | tf_op jit(solution)/shard_map/ppermute | solution.py:21
  (49 other events, 352.8 us)
